TPU v7x, 32 devices: a whole 2x2x4 slice. The times are simulated.
32 devices in a mesh: pipe: 2 (over x), dp: 4 (over y, core), tensor: 4 (over z).
Axes of the slice: x: 2, y: 2, z: 4, core: 2. Of those that a mesh axis runs over, the one named last changes fastest.
Arguments:
- inputs: bfloat16 [2, 4, 1024, 768], P('pipe', 'dp', 'tensor'), may hold values from -6 to 6
- cotangent: bfloat16 [2, 4, 1024, 768], P('pipe', 'dp', 'tensor'), may hold values from -6 to 6
- gain_one: float32 [2, 768], P('pipe'), may hold values from 0.5 to 1.5
- shift_one: float32 [2, 768], P('pipe'), may hold values from -1.5 to 1.5
- attend_in: bfloat16 [2, 768, 3, 768], P('pipe', None, None, 'tensor'), may hold values from -0.21875 to 0.21875
- attend_bias: float32 [2, 2, 768], P('pipe', None, 'tensor'), may hold values from -2.5 to 2.5
- attend_out: bfloat16 [2, 768, 768], P('pipe', 'tensor'), may hold values from -3.5 to 3.5
- out_bias: float32 [2, 768], P('pipe'), may hold values from -2.5 to 2.5
- gain_two: float32 [2, 768], P('pipe'), may hold values from 0.5 to 1.5
- shift_two: float32 [2, 768], P('pipe'), may hold values from -1.5 to 1.5
- expand_in: bfloat16 [2, 768, 3072], P('pipe', None, 'tensor'), may hold values from -0.21875 to 0.21875
- expand_bias: float32 [2, 3072], P('pipe', 'tensor'), may hold values from -2.5 to 2.5
- reduce_out: bfloat16 [2, 3072, 768], P('pipe', 'tensor'), may hold values from -0.4375 to 0.4375
- reduce_bias: float32 [2, 768], P('pipe'), may hold values from -2.5 to 2.5
Outputs:
- outputs: bfloat16 [2, 4, 1024, 768], P('pipe', 'dp', 'tensor')
- input_grad: bfloat16 [2, 4, 1024, 768], P('pipe', 'dp', 'tensor')
- grad_gain_one: float32 [2, 768], P('pipe')
- grad_shift_one: float32 [2, 768], P('pipe')
- grad_attend_in: float32 [2, 768, 3, 768], P('pipe', None, None, 'tensor')
- grad_attend_bias: float32 [2, 2, 768], P('pipe', None, 'tensor')
- grad_attend_out: float32 [2, 768, 768], P('pipe', 'tensor')
- grad_out_bias: float32 [2, 768], P('pipe')
- grad_gain_two: float32 [2, 768], P('pipe')
- grad_shift_two: float32 [2, 768], P('pipe')
- grad_expand_in: float32 [2, 768, 3072], P('pipe', None, 'tensor')
- grad_expand_bias: float32 [2, 3072], P('pipe', 'tensor')
- grad_reduce_out: float32 [2, 3072, 768], P('pipe', 'tensor')
- grad_reduce_bias: float32 [2, 768], P('pipe')
All inputs are finite; a program needn't handle non-finite values.
Results may differ from a plain program's by a relative error of at most 0.022.
Values may be sent and summed in bfloat16 or wider, within the bound.
No kernel may reach another device: no remote copies, remote signals or barrier semaphores. Data moves between devices by JAX's collectives and lax.ppermute only.
A program may use at most 192 MiB of HBM per device.

v0:
```python
import jax
import jax.numpy as jnp
from jax import lax
from jax.sharding import PartitionSpec as P

HEAD = 64
DEPTH = 12


EPSILON = 1e-05
NEGATIVE = -1e30


def from_partner(shard, axis, distance):
    return lax.ppermute(shard, axis, [(i, i ^ 1 << distance) for i in range(lax.axis_size(axis))])


def passed_along(shard, axis, by):
    count = lax.axis_size(axis)
    pairs = [(i, i + by) for i in range(count) if 0 <= i + by < count]
    return lax.ppermute(shard, axis, pairs)


def for_sending(shard):
    return jax.tree.map(lambda a: a.astype(jnp.bfloat16) if a.dtype == jnp.float32 else a, shard)


def normalize_rows(tok_rows):
    centred = tok_rows - jnp.mean(tok_rows, axis=-1, keepdims=True)
    inverse = lax.rsqrt(jnp.mean(centred * centred, axis=-1, keepdims=True) + EPSILON)
    return (centred * inverse, inverse)


def norm_backward(grad_normed, normed, inverse, gain_vec):
    scaled = grad_normed * gain_vec
    centred = scaled - jnp.mean(scaled, axis=-1, keepdims=True)
    return inverse * (centred - normed * jnp.mean(scaled * normed, axis=-1, keepdims=True))


def smooth_gate(values):
    return jax.nn.gelu(values, approximate=True)


def spread_rows(piece):
    return lax.all_gather(piece, "tensor", axis=1, tiled=True)


def collect_rows(piece):
    return lax.psum_scatter(piece, "tensor", scatter_dimension=1, tiled=True)


def spread_grads(piece):
    return lax.all_gather(piece, "tensor", axis=1, tiled=True)


def collect_grads(piece):
    return lax.psum_scatter(
        piece.astype(jnp.bfloat16), "tensor", scatter_dimension=1, tiled=True
    ).astype(jnp.float32)


def causal_scores(query_block, key_rows, offset, block_rows, length, factor):
    scores = (
        jnp.einsum("bqhe,bkhe->bhqk", query_block, key_rows, preferred_element_type=jnp.float32)
        * factor
    )
    places = jnp.arange(length)
    allowed = places[offset : offset + block_rows, None] >= places[None, :]
    return jnp.where(allowed[None, None], scores, NEGATIVE)


def attend_forward(queries, key_rows, values):
    batch_size, length, local = queries.shape
    heads_here = local // HEAD
    block_rows = min(512, length)
    factor = HEAD ** (-0.5)
    queries = queries.reshape(batch_size, length, heads_here, HEAD)
    key_rows = key_rows.reshape(batch_size, length, heads_here, HEAD)
    values = values.reshape(batch_size, length, heads_here, HEAD)
    pieces = []
    totals = []
    for offset in range(0, length, block_rows):
        query_block = queries[:, offset : offset + block_rows]
        scores = causal_scores(query_block, key_rows, offset, block_rows, length, factor)
        peak_score = jnp.max(scores, axis=-1, keepdims=True)
        log_total = peak_score + jnp.log(
            jnp.sum(jnp.exp(scores - peak_score), axis=-1, keepdims=True)
        )
        weights = jnp.exp(scores - log_total).astype(jnp.bfloat16)
        pieces.append(
            jnp.einsum("bhqk,bkhe->bqhe", weights, values, preferred_element_type=jnp.float32)
        )
        totals.append(log_total)
    mixed = jnp.concatenate(pieces, axis=1).reshape(batch_size, length, local).astype(jnp.bfloat16)
    return (mixed, jnp.concatenate(totals, axis=2))


def attend_backward(queries, key_rows, values, log_totals, grad_mixed):
    batch_size, length, local = queries.shape
    heads_here = local // HEAD
    block_rows = min(512, length)
    factor = HEAD ** (-0.5)
    queries = queries.reshape(batch_size, length, heads_here, HEAD)
    key_rows = key_rows.reshape(batch_size, length, heads_here, HEAD)
    values = values.reshape(batch_size, length, heads_here, HEAD)
    grad_mixed = grad_mixed.reshape(batch_size, length, heads_here, HEAD)
    grad_query_parts = []
    grad_keys = jnp.zeros((batch_size, length, heads_here, HEAD), jnp.float32)
    grad_values = jnp.zeros((batch_size, length, heads_here, HEAD), jnp.float32)
    for offset in range(0, length, block_rows):
        query_block = queries[:, offset : offset + block_rows]
        grad_block = grad_mixed[:, offset : offset + block_rows]
        scores = causal_scores(query_block, key_rows, offset, block_rows, length, factor)
        weights = jnp.exp(scores - log_totals[:, :, offset : offset + block_rows])
        rounded = weights.astype(jnp.bfloat16)
        grad_weights = jnp.einsum(
            "bqhe,bkhe->bhqk", grad_block, values, preferred_element_type=jnp.float32
        )
        inner = jnp.sum(grad_weights * weights, axis=-1, keepdims=True)
        grad_scores = (weights * (grad_weights - inner)).astype(jnp.bfloat16)
        grad_query_parts.append(
            jnp.einsum("bhqk,bkhe->bqhe", grad_scores, key_rows, preferred_element_type=jnp.float32)
            * factor
        )
        grad_keys = (
            grad_keys
            + jnp.einsum(
                "bhqk,bqhe->bkhe", grad_scores, query_block, preferred_element_type=jnp.float32
            )
            * factor
        )
        grad_values = grad_values + jnp.einsum(
            "bhqk,bqhe->bkhe", rounded, grad_block, preferred_element_type=jnp.float32
        )
    grad_queries = jnp.concatenate(grad_query_parts, axis=1).reshape(batch_size, length, local)
    return (
        grad_queries,
        grad_keys.reshape(batch_size, length, local),
        grad_values.reshape(batch_size, length, local),
    )


def layer_forward(layer_in, weights):
    (
        gain_a,
        shift_a,
        proj_in,
        proj_bias,
        proj_out,
        bias_out,
        gain_b,
        shift_b,
        expand_w,
        expand_b,
        reduce_w,
        reduce_b,
    ) = weights
    width = proj_in.shape[0]
    local = proj_in.shape[2]
    branch = DEPTH ** (-0.5)
    normed_one, inverse_one = normalize_rows(layer_in)
    gathered_one = spread_rows((normed_one * gain_a + shift_a).astype(jnp.bfloat16))
    batch_size, length, _ = gathered_one.shape
    projected = jnp.einsum(
        "bsd,dc->bsc",
        gathered_one,
        proj_in.reshape(width, 3 * local),
        preferred_element_type=jnp.float32,
    )
    projected = projected.reshape(batch_size, length, 3, local)
    queries = (projected[:, :, 0] + proj_bias[0]).astype(jnp.bfloat16)
    key_rows = projected[:, :, 1].astype(jnp.bfloat16)
    values = (projected[:, :, 2] + proj_bias[1]).astype(jnp.bfloat16)
    mixed, log_totals = attend_forward(queries, key_rows, values)
    attended = (
        collect_rows(jnp.einsum("bsc,cd->bsd", mixed, proj_out, preferred_element_type=jnp.float32))
        + bias_out
    )
    middle = layer_in + branch * attended
    normed_two, inverse_two = normalize_rows(middle)
    gathered_two = spread_rows((normed_two * gain_b + shift_b).astype(jnp.bfloat16))
    hidden_pre = (
        jnp.einsum("bsd,df->bsf", gathered_two, expand_w, preferred_element_type=jnp.float32)
        + expand_b
    )
    hidden = smooth_gate(hidden_pre).astype(jnp.bfloat16)
    outcome = (
        collect_rows(
            jnp.einsum("bsf,fd->bsd", hidden, reduce_w, preferred_element_type=jnp.float32)
        )
        + reduce_b
    )
    result = middle + branch * outcome
    kept = (
        normed_one,
        inverse_one,
        gathered_one,
        queries,
        key_rows,
        values,
        mixed,
        log_totals,
        normed_two,
        inverse_two,
        gathered_two,
        hidden_pre,
        hidden,
    )
    return (result, kept)


def layer_backward(kept, grad_result, weights):
    (
        gain_a,
        shift_a,
        proj_in,
        proj_bias,
        proj_out,
        bias_out,
        gain_b,
        shift_b,
        expand_w,
        expand_b,
        reduce_w,
        reduce_b,
    ) = weights
    (
        normed_one,
        inverse_one,
        gathered_one,
        queries,
        key_rows,
        values,
        mixed,
        log_totals,
        normed_two,
        inverse_two,
        gathered_two,
        hidden_pre,
        hidden,
    ) = kept
    width = proj_in.shape[0]
    local = proj_in.shape[2]
    branch = DEPTH ** (-0.5)
    grad_outcome = branch * grad_result
    grad_reduce_b = jnp.sum(grad_outcome, axis=(0, 1))
    full_outcome = spread_grads(grad_outcome.astype(jnp.bfloat16))
    grad_reduce_w = jnp.einsum(
        "bsf,bsd->fd", hidden, full_outcome, preferred_element_type=jnp.float32
    )
    grad_hidden = jnp.einsum(
        "bsd,fd->bsf", full_outcome, reduce_w, preferred_element_type=jnp.float32
    )
    grad_pre = jax.vjp(smooth_gate, hidden_pre)[1](grad_hidden)[0]
    grad_expand_b = jnp.sum(grad_pre, axis=(0, 1))
    rounded_pre = grad_pre.astype(jnp.bfloat16)
    grad_expand_w = jnp.einsum(
        "bsd,bsf->df", gathered_two, rounded_pre, preferred_element_type=jnp.float32
    )
    grad_normed_two = collect_grads(
        jnp.einsum("bsf,df->bsd", rounded_pre, expand_w, preferred_element_type=jnp.float32)
    )
    grad_gain_b = jnp.sum(grad_normed_two * normed_two, axis=(0, 1))
    grad_shift_b = jnp.sum(grad_normed_two, axis=(0, 1))
    grad_middle = grad_result + norm_backward(grad_normed_two, normed_two, inverse_two, gain_b)
    grad_attended = branch * grad_middle
    grad_bias_out = jnp.sum(grad_attended, axis=(0, 1))
    full_attended = spread_grads(grad_attended.astype(jnp.bfloat16))
    grad_proj_out = jnp.einsum(
        "bsc,bsd->cd", mixed, full_attended, preferred_element_type=jnp.float32
    )
    grad_mixed = jnp.einsum(
        "bsd,cd->bsc", full_attended, proj_out, preferred_element_type=jnp.float32
    ).astype(jnp.bfloat16)
    grad_queries, grad_keys, grad_values = attend_backward(
        queries, key_rows, values, log_totals, grad_mixed
    )
    grad_proj_bias = jnp.stack(
        [jnp.sum(grad_queries, axis=(0, 1)), jnp.sum(grad_values, axis=(0, 1))]
    )
    batch_size, length, _ = grad_queries.shape
    rounded_proj = (
        jnp.stack([grad_queries, grad_keys, grad_values], axis=2)
        .astype(jnp.bfloat16)
        .reshape(batch_size, length, 3 * local)
    )
    grad_proj_in = jnp.einsum(
        "bsd,bsc->dc", gathered_one, rounded_proj, preferred_element_type=jnp.float32
    ).reshape(width, 3, local)
    grad_normed_one = collect_grads(
        jnp.einsum(
            "bsc,dc->bsd",
            rounded_proj,
            proj_in.reshape(width, 3 * local),
            preferred_element_type=jnp.float32,
        )
    )
    grad_gain_a = jnp.sum(grad_normed_one * normed_one, axis=(0, 1))
    grad_shift_a = jnp.sum(grad_normed_one, axis=(0, 1))
    grad_in = grad_middle + norm_backward(grad_normed_one, normed_one, inverse_one, gain_a)
    shared = (grad_gain_a, grad_shift_a, grad_bias_out, grad_gain_b, grad_shift_b, grad_reduce_b)
    sharded = (
        grad_proj_in,
        grad_proj_bias,
        grad_proj_out,
        grad_expand_w,
        grad_expand_b,
        grad_reduce_w,
    )
    return (grad_in, shared, sharded)


def shards(
    inputs,
    cotangent,
    gain_one,
    shift_one,
    attend_in,
    attend_bias,
    attend_out,
    out_bias,
    gain_two,
    shift_two,
    expand_in,
    expand_bias,
    reduce_out,
    reduce_bias,
):
    weights = tuple(
        (
            stacked[0]
            for stacked in (
                gain_one,
                shift_one,
                attend_in,
                attend_bias,
                attend_out,
                out_bias,
                gain_two,
                shift_two,
                expand_in,
                expand_bias,
                reduce_out,
                reduce_bias,
            )
        )
    )
    is_first = lax.axis_index("pipe") == 0
    mine_in = inputs[0]
    mine_cot = cotangent[0]
    entry = from_partner(jnp.where(is_first, mine_cot, mine_in), "pipe", 0)
    received = jnp.zeros_like(mine_in)
    section_inputs = []
    results = []
    kept_all = []
    for period in range(3):
        first_in = mine_in if period == 0 else entry
        layer_in = jnp.where(is_first, first_in, received).astype(jnp.float32)
        result, kept = layer_forward(layer_in, weights)
        section_inputs.append(layer_in)
        results.append(result)
        kept_all.append(kept)
        if period < 2:
            received = passed_along(result.astype(jnp.bfloat16), "pipe", 1)
    last_cot = (entry, mine_cot)
    returned = jnp.zeros_like(mine_in)
    shared_acc = None
    sharded_acc = None
    grads_in = []
    for period in range(3):
        early_index = max(period - 1, 0)
        late_index = min(period + 1, 2)
        layer_in = jnp.where(is_first, section_inputs[early_index], section_inputs[late_index])
        grad_result = jnp.where(is_first, returned, last_cot[min(period, 1)]).astype(jnp.float32)
        valid = jnp.where(is_first, period >= 1, period < 2).astype(jnp.float32)
        kept = layer_forward(layer_in, weights)[1]
        grad_in, shared, sharded = layer_backward(kept, grad_result, weights)
        shared = tuple((member * valid for member in shared))
        sharded = tuple((member * valid for member in sharded))
        if shared_acc is None:
            shared_acc = shared
            sharded_acc = sharded
        else:
            shared_acc = tuple((total + member for total, member in zip(shared_acc, shared)))
            sharded_acc = tuple((total + member for total, member in zip(sharded_acc, sharded)))
        rounded_in = grad_in.astype(jnp.bfloat16)
        if period >= 1:
            grads_in.append(rounded_in)
        if period < 2:
            returned = passed_along(rounded_in, "pipe", -1)
    late = jax.tree.map(
        lambda part: part.astype(jnp.float32), lax.psum(for_sending(sharded_acc), "dp")
    )
    shared_total = lax.psum(shared_acc, ("dp", "tensor"))
    exit_send = jnp.where(is_first, grads_in[1], results[1].astype(jnp.bfloat16))
    exit_recv = from_partner(exit_send, "pipe", 0)
    outputs = jnp.where(is_first, exit_recv, results[2].astype(jnp.bfloat16))[None]
    input_grad = jnp.where(is_first, grads_in[0], exit_recv)[None]
    return (
        outputs,
        input_grad,
        shared_total[0][None],
        shared_total[1][None],
        late[0][None],
        late[1][None],
        late[2][None],
        shared_total[2][None],
        shared_total[3][None],
        shared_total[4][None],
        late[3][None],
        late[4][None],
        late[5][None],
        shared_total[5][None],
    )


def solution(mesh):
    placed = (
        P("pipe", "dp", "tensor", None),
        P("pipe", "dp", "tensor", None),
        P("pipe", None),
        P("pipe", None),
        P("pipe", None, None, "tensor"),
        P("pipe", None, "tensor"),
        P("pipe", "tensor", None),
        P("pipe", None),
        P("pipe", None),
        P("pipe", None),
        P("pipe", None, "tensor"),
        P("pipe", "tensor"),
        P("pipe", "tensor", None),
        P("pipe", None),
    )
    return jax.shard_map(
        shards,
        mesh=mesh,
        in_specs=placed,
        out_specs=(
            P("pipe", "dp", "tensor", None),
            P("pipe", "dp", "tensor", None),
            P("pipe", None),
            P("pipe", None),
            P("pipe", None, None, "tensor"),
            P("pipe", None, "tensor"),
            P("pipe", "tensor", None),
            P("pipe", None),
            P("pipe", None),
            P("pipe", None),
            P("pipe", None, "tensor"),
            P("pipe", "tensor"),
            P("pipe", "tensor", None),
            P("pipe", None),
        ),
        check_vma=False,
    )
```

profile of v0, /device:TPU:17, one launch (start us, length us, event | category | flops | bytes accessed | tf_op | source)
XLA Modules:
  0.0 1781.6 jit_solution(9194627020075652379)
XLA Ops:
  14.9 35.4 %all-gather.19.cloned.1.call-done = bf16[1,1024,768]{2,1,0:T(8,128)(2,1)} async-done(((bf16[1,256,768]{2,1,0:T(8,128)(2,1)}), bf16[1,1024,768]{2,1,0:T(8,128)(2,1)}) %all-gather.19.cloned.1.call-update) | async-done | bytes 1572880 | tf_op jit(solution)/shard_map/all_gather | solution.py:45
  65.9 60.3 %reduce-scatter.16.cloned.1.call-done = f32[1,256,768]{2,1,0:T(8,128)} async-done(((f32[1,1024,768]{2,1,0:T(8,128)}), f32[1,256,768]{2,1,0:T(8,128)}) %reduce-scatter.16.cloned.1.call-update) | async-done | bytes 786448 | tf_op jit(solution)/shard_map/reduce_scatter | solution.py:49
  131.5 35.8 %all-gather.21.cloned.1.call-done = bf16[1,1024,768]{2,1,0:T(8,128)(2,1)} async-done(((bf16[1,256,768]{2,1,0:T(8,128)(2,1)}), bf16[1,1024,768]{2,1,0:T(8,128)(2,1)}) %all-gather.21.cloned.1.call-update) | async-done | bytes 1572880 | tf_op jit(solution)/shard_map/all_gather | solution.py:45
  167.2 6.4 convolution_bitcast_fusion.7
  176.6 57.5 %reduce-scatter.18.cloned.1.call-done = f32[1,256,768]{2,1,0:T(8,128)} async-done(((f32[1,1024,768]{2,1,0:T(8,128)}), f32[1,256,768]{2,1,0:T(8,128)}) %reduce-scatter.18.cloned.1.call-update) | async-done | bytes 786448 | tf_op jit(solution)/shard_map/reduce_scatter | solution.py:49
  239.6 7.0 collective-permute-done.1
  249.2 36.9 %all-gather.31.cloned.1.call-done = bf16[1,1024,768]{2,1,0:T(8,128)(2,1)} async-done(((bf16[1,256,768]{2,1,0:T(8,128)(2,1)}), bf16[1,1024,768]{2,1,0:T(8,128)(2,1)}) %all-gather.31.cloned.1.call-update) | async-done | bytes 1572880 | tf_op jit(solution)/shard_map/all_gather | solution.py:45
  301.6 60.4 %reduce-scatter.26.cloned.1.call-done = f32[1,256,768]{2,1,0:T(8,128)} async-done(((f32[1,1024,768]{2,1,0:T(8,128)}), f32[1,256,768]{2,1,0:T(8,128)}) %reduce-scatter.26.cloned.1.call-update) | async-done | bytes 786448 | tf_op jit(solution)/shard_map/reduce_scatter | solution.py:49
  367.4 35.6 %all-gather.33.cloned.1.call-done = bf16[1,1024,768]{2,1,0:T(8,128)(2,1)} async-done(((bf16[1,256,768]{2,1,0:T(8,128)(2,1)}), bf16[1,1024,768]{2,1,0:T(8,128)(2,1)}) %all-gather.33.cloned.1.call-update) | async-done | bytes 1572880 | tf_op jit(solution)/shard_map/all_gather | solution.py:45
  403.0 6.1 convolution_bitcast_fusion.4
  409.1 60.4 %reduce-scatter.28.cloned.1.call-done = f32[1,256,768]{2,1,0:T(8,128)} async-done(((f32[1,1024,768]{2,1,0:T(8,128)}), f32[1,256,768]{2,1,0:T(8,128)}) %reduce-scatter.28.cloned.1.call-update) | async-done | bytes 786448 | tf_op jit(solution)/shard_map/reduce_scatter | solution.py:49
  474.0 7.8 collective-permute-done.3
  488.4 36.0 %all-gather.51.cloned.1.call-done = bf16[1,1024,768]{2,1,0:T(8,128)(2,1)} async-done(((bf16[1,256,768]{2,1,0:T(8,128)(2,1)}), bf16[1,1024,768]{2,1,0:T(8,128)(2,1)}) %all-gather.51.cloned.1.call-update) | async-done | bytes 1572880 | tf_op jit(solution)/shard_map/all_gather | solution.py:45
  529.2 33.2 %all-gather.43.cloned.1.call-done = bf16[1,1024,768]{2,1,0:T(8,128)(2,1)} async-done(((bf16[1,256,768]{2,1,0:T(8,128)(2,1)}), bf16[1,1024,768]{2,1,0:T(8,128)(2,1)}) %all-gather.43.cloned.1.call-update) | async-done | bytes 1572880 | tf_op jit(solution)/shard_map/all_gather | solution.py:45
  567.1 33.4 %all-gather.23.cloned.1.call-done = bf16[1,1024,768]{2,1,0:T(8,128)(2,1)} async-done(((bf16[1,256,768]{2,1,0:T(8,128)(2,1)}), bf16[1,1024,768]{2,1,0:T(8,128)(2,1)}) %all-gather.23.cloned.1.call-update) | async-done | bytes 1572880 | tf_op jit(solution)/shard_map/all_gather | solution.py:45
  607.4 30.6 %all-gather.35.cloned.1.call-done = bf16[1,1024,768]{2,1,0:T(8,128)(2,1)} async-done(((bf16[1,256,768]{2,1,0:T(8,128)(2,1)}), bf16[1,1024,768]{2,1,0:T(8,128)(2,1)}) %all-gather.35.cloned.1.call-update) | async-done | bytes 1572880 | tf_op jit(solution)/shard_map/all_gather | solution.py:45
  657.2 8.9 exponential_reduce_fusion.1
  666.2 9.1 exponential_reduce_fusion
  684.9 10.1 exponential_reduce_fusion.3
  724.6 20.1 %reduce-scatter.42.cloned.1.call-done = f32[1,256,768]{2,1,0:T(8,128)} async-done(((f32[1,1024,768]{2,1,0:T(8,128)}), f32[1,256,768]{2,1,0:T(8,128)}) %reduce-scatter.42.cloned.1.call-update) | async-done | bytes 786448 | tf_op jit(solution)/shard_map/reduce_scatter | solution.py:49
  744.7 62.5 %reduce-scatter.30.cloned.1.call-done = f32[1,256,768]{2,1,0:T(8,128)} async-done(((f32[1,1024,768]{2,1,0:T(8,128)}), f32[1,256,768]{2,1,0:T(8,128)}) %reduce-scatter.30.cloned.1.call-update) | async-done | bytes 786448 | tf_op jit(solution)/shard_map/reduce_scatter | solution.py:49
  807.2 62.5 %reduce-scatter.20.cloned.1.call-done = f32[1,256,768]{2,1,0:T(8,128)} async-done(((f32[1,1024,768]{2,1,0:T(8,128)}), f32[1,256,768]{2,1,0:T(8,128)}) %reduce-scatter.20.cloned.1.call-update) | async-done | bytes 786448 | tf_op jit(solution)/shard_map/reduce_scatter | solution.py:49
  875.0 35.0 %all-gather.27.cloned.1.call-done = bf16[1,1024,768]{2,1,0:T(8,128)(2,1)} async-done(((bf16[1,256,768]{2,1,0:T(8,128)(2,1)}), bf16[1,1024,768]{2,1,0:T(8,128)(2,1)}) %all-gather.27.cloned.1.call-update) | async-done | bytes 1572880 | tf_op jit(solution)/shard_map/all_gather | solution.py:45
  914.5 33.6 %all-gather.25.cloned.1.call-done = bf16[1,1024,768]{2,1,0:T(8,128)(2,1)} async-done(((bf16[1,256,768]{2,1,0:T(8,128)(2,1)}), bf16[1,1024,768]{2,1,0:T(8,128)(2,1)}) %all-gather.25.cloned.1.call-update) | async-done | bytes 1572880 | tf_op jit(solution)/shard_map/all_gather | solution.py:53
  948.0 6.3 fusion.483
  958.2 34.4 %reduce-scatter.22.cloned.1.call-done = bf16[1,256,768]{2,1,0:T(8,128)(2,1)} async-done(((bf16[1,1024,768]{2,1,0:T(8,128)(2,1)}), bf16[1,256,768]{2,1,0:T(8,128)(2,1)}) %reduce-scatter.22.cloned.1.call-update) | async-done | bytes 393232 | tf_op jit(solution)/shard_map/reduce_scatter | solution.py:57
  998.9 36.1 %all-gather.29.cloned.1.call-done = bf16[1,1024,768]{2,1,0:T(8,128)(2,1)} async-done(((bf16[1,256,768]{2,1,0:T(8,128)(2,1)}), bf16[1,1024,768]{2,1,0:T(8,128)(2,1)}) %all-gather.29.cloned.1.call-update) | async-done | bytes 1572880 | tf_op jit(solution)/shard_map/all_gather | solution.py:53
  1062.9 33.7 %reduce-scatter.24.cloned.1.call-done = bf16[1,256,768]{2,1,0:T(8,128)(2,1)} async-done(((bf16[1,1024,768]{2,1,0:T(8,128)(2,1)}), bf16[1,256,768]{2,1,0:T(8,128)(2,1)}) %reduce-scatter.24.cloned.1.call-update) | async-done | bytes 393232 | tf_op jit(solution)/shard_map/reduce_scatter | solution.py:57
  1101.1 10.7 collective-permute-done.2
  1113.8 20.3 %all-gather.39.cloned.1.call-done = bf16[1,1024,768]{2,1,0:T(8,128)(2,1)} async-done(((bf16[1,256,768]{2,1,0:T(8,128)(2,1)}), bf16[1,1024,768]{2,1,0:T(8,128)(2,1)}) %all-gather.39.cloned.1.call-update) | async-done | bytes 1572880 | tf_op jit(solution)/shard_map/all_gather | solution.py:45
  1138.7 33.6 %all-gather.37.cloned.1.call-done = bf16[1,1024,768]{2,1,0:T(8,128)(2,1)} async-done(((bf16[1,256,768]{2,1,0:T(8,128)(2,1)}), bf16[1,1024,768]{2,1,0:T(8,128)(2,1)}) %all-gather.37.cloned.1.call-update) | async-done | bytes 1572880 | tf_op jit(solution)/shard_map/all_gather | solution.py:53
  1172.2 6.3 fusion.482
  1182.4 34.4 %reduce-scatter.32.cloned.1.call-done = bf16[1,256,768]{2,1,0:T(8,128)(2,1)} async-done(((bf16[1,1024,768]{2,1,0:T(8,128)(2,1)}), bf16[1,256,768]{2,1,0:T(8,128)(2,1)}) %reduce-scatter.32.cloned.1.call-update) | async-done | bytes 393232 | tf_op jit(solution)/shard_map/reduce_scatter | solution.py:57
  1222.0 36.0 %all-gather.41.cloned.1.call-done = bf16[1,1024,768]{2,1,0:T(8,128)(2,1)} async-done(((bf16[1,256,768]{2,1,0:T(8,128)(2,1)}), bf16[1,1024,768]{2,1,0:T(8,128)(2,1)}) %all-gather.41.cloned.1.call-update) | async-done | bytes 1572880 | tf_op jit(solution)/shard_map/all_gather | solution.py:53
  1300.0 21.4 %reduce-scatter.34.cloned.1.call-done = bf16[1,256,768]{2,1,0:T(8,128)(2,1)} async-done(((bf16[1,1024,768]{2,1,0:T(8,128)(2,1)}), bf16[1,256,768]{2,1,0:T(8,128)(2,1)}) %reduce-scatter.34.cloned.1.call-update) | async-done | bytes 393232 | tf_op jit(solution)/shard_map/reduce_scatter | solution.py:57
  1323.4 60.4 %reduce-scatter.36.cloned.1.call-done = f32[1,256,768]{2,1,0:T(8,128)} async-done(((f32[1,1024,768]{2,1,0:T(8,128)}), f32[1,256,768]{2,1,0:T(8,128)}) %reduce-scatter.36.cloned.1.call-update) | async-done | bytes 786448 | tf_op jit(solution)/shard_map/reduce_scatter | solution.py:49
  1390.4 11.0 collective-permute-done.4
  1403.4 21.7 %all-gather.47.cloned.1.call-done = bf16[1,1024,768]{2,1,0:T(8,128)(2,1)} async-done(((bf16[1,256,768]{2,1,0:T(8,128)(2,1)}), bf16[1,1024,768]{2,1,0:T(8,128)(2,1)}) %all-gather.47.cloned.1.call-update) | async-done | bytes 1572880 | tf_op jit(solution)/shard_map/all_gather | solution.py:45
  1429.7 33.6 %all-gather.45.cloned.1.call-done = bf16[1,1024,768]{2,1,0:T(8,128)(2,1)} async-done(((bf16[1,256,768]{2,1,0:T(8,128)(2,1)}), bf16[1,1024,768]{2,1,0:T(8,128)(2,1)}) %all-gather.45.cloned.1.call-update) | async-done | bytes 1572880 | tf_op jit(solution)/shard_map/all_gather | solution.py:53
  1463.3 5.7 fusion.481
  1473.0 34.2 %reduce-scatter.38.cloned.1.call-done = bf16[1,256,768]{2,1,0:T(8,128)(2,1)} async-done(((bf16[1,1024,768]{2,1,0:T(8,128)(2,1)}), bf16[1,256,768]{2,1,0:T(8,128)(2,1)}) %reduce-scatter.38.cloned.1.call-update) | async-done | bytes 393232 | tf_op jit(solution)/shard_map/reduce_scatter | solution.py:57
  1531.1 7.0 fusion.148
  1540.8 7.6 all-gather.49.cloned.1.call-done
  1586.5 6.4 convolution_bitcast_fusion
  1594.3 5.9 all-reduce.1
  1601.3 64.3 %all-reduce.5.cloned.1.call-done = (bf16[1,768,3,192]{1,3,2,0:T(8,128)(2,1)}, bf16[1,192,768]{2,1,0:T(8,128)(2,1)}, bf16[1,768,768]{2,1,0:T(8,128)(2,1)}, bf16[1,768,768]{2,1,0:T(8,128)(2,1)}) async-done(((bf16[1,768,3,192]{1,3,2,0:T(8,128)(2,1)}, bf16[1,192,768]{2,1,0:T(8,128)(2,1)}, bf16[1,768,768]{2,1,0:T(8,128)(2,1)}, bf16[1,768,768]{2,1,0:T(8,128)(2,1)}), (bf16[1,768,3,192]{1,3,2,0:T(8,128)(2,1)}, ...) | async-done | bytes 3538960 | tf_op jit(solution)/shard_map/psum | solution.py:392
  1673.4 29.0 %reduce-scatter.40.cloned.1.call-done = bf16[1,256,768]{2,1,0:T(8,128)(2,1)} async-done(((bf16[1,1024,768]{2,1,0:T(8,128)(2,1)}), bf16[1,256,768]{2,1,0:T(8,128)(2,1)}) %reduce-scatter.40.cloned.1.call-update) | async-done | bytes 393232 | tf_op jit(solution)/shard_map/reduce_scatter | solution.py:57
  1707.5 64.6 %all-reduce = (f32[1,768]{1,0:T(1,128)}, f32[1,768]{1,0:T(1,128)}, f32[1,768]{1,0:T(1,128)}, f32[1,768]{1,0:T(1,128)}, f32[1,768]{1,0:T(1,128)}, /*index=5*/f32[1,768]{1,0:T(1,128)}) all-reduce(f32[1,768]{1,0:T(1,128)S(1)} %broadcast_in_dim.287, ...), channel_id=1, replica_groups=mesh['pipe'=2,'dp'=4,'tensor'=4] {'dp','tensor'}, use_global_device_ids=true, to_apply=%region_84.85 | all-reduce | flops 4608 | bytes 36864 | tf_op jit(solution)/shard_map/psum | solution.py:394
  (692 shorter events, 354.9 us)
Async XLA Ops:
  7.2 160.1 %copy-start = (bf16[1,768,768]{2,1,0:T(8,128)(2,1)S(1)}, bf16[1,768,768]{2,1,0:T(8,128)(2,1)}, u32[]{:S(2)}) copy-start(bf16[1,768,768]{2,1,0:T(8,128)(2,1)} %param.24) | copy-start | bytes 3538948
  7.2 43.1 %all-gather.19.cloned.1.call-start = ((), (), s32[]{:S(2)}) async-start(), calls=%async_computation.15 | async-start | bytes 1966080 | tf_op jit(solution)/shard_map/all_gather | solution.py:45
  11.1 237.0 %copy-start.91 = (f32[768]{0:T(1024)}, f32[768]{0:T(1024)S(1)}, u32[]{:S(2)}) copy-start(f32[768]{0:T(1024)S(1)} %reduce.121) | copy-start | bytes 9220
  13.1 113.1 %reduce-scatter.16.cloned.1.call-start = ((), (), s32[]{:S(2)}) async-start(), calls=%async_computation.16 | async-start | bytes 3932160 | tf_op jit(solution)/shard_map/reduce_scatter | solution.py:49
  14.0 283.3 %copy-start.118 = (f32[3,64]{1,0:T(4,128)}, f32[3,64]{1,0:T(4,128)S(1)}, u32[]{:S(2)}) copy-start(f32[3,64]{1,0:T(4,128)S(1)} %add.847) | copy-start | bytes 2308
  14.1 275.0 %copy-start.94 = (f32[3,64]{1,0:T(4,128)}, f32[3,64]{1,0:T(4,128)S(1)}, u32[]{:S(2)}) copy-start(f32[3,64]{1,0:T(4,128)S(1)} %add.850) | copy-start | bytes 2308
  14.5 282.8 %copy-start.9 = (pred[512,1024]{1,0:T(8,128)(4,1)}, pred[512,1024]{1,0:T(8,128)(4,1)S(1)}, u32[]{:S(2)}) copy-start(pred[512,1024]{1,0:T(8,128)(4,1)S(1)} %iota_compare_fusion.1) | copy-start | bytes 1572868
  14.9 280.6 %copy-start.6 = (pred[512,1024]{1,0:T(8,128)(4,1)}, pred[512,1024]{1,0:T(8,128)(4,1)S(1)}, u32[]{:S(2)}) copy-start(pred[512,1024]{1,0:T(8,128)(4,1)S(1)} %iota_compare_fusion) | copy-start | bytes 1572868
  65.7 101.5 %all-gather.21.cloned.1.call-start = ((), (), s32[]{:S(2)}) async-start(), calls=%async_computation.17 | async-start | bytes 1966080 | tf_op jit(solution)/shard_map/all_gather | solution.py:45
  131.2 103.0 %reduce-scatter.18.cloned.1.call-start = ((), (), s32[]{:S(2)}) async-start(), calls=%async_computation.18 | async-start | bytes 3932160 | tf_op jit(solution)/shard_map/reduce_scatter | solution.py:49
  173.7 112.4 %all-gather.31.cloned.1.call-start = ((), (), s32[]{:S(2)}) async-start(), calls=%async_computation.26 | async-start | bytes 1966080 | tf_op jit(solution)/shard_map/all_gather | solution.py:45
  175.4 63.5 %collective-permute-start = (bf16[1,256,768]{2,1,0:T(8,128)(2,1)}, bf16[1,256,768]{2,1,0:T(8,128)(2,1)S(1)}, u32[]{:S(2)}, u32[]{:S(2)}) collective-permute-start(bf16[1,256,768]{2,1,0:T(8,128)(2,1)} %bitcast_select_fusion.1), channel_id=1, source_target_pairs={{0,16},{16,0},{1,17},{17,1},{2,18},{18,2},{3,19},{19,3},{4,20},{20... | collective-permute-start | bytes 1179656 | tf_op jit(solution)/shard_map/ppermute | solution.py:15
  176.6 292.9 %copy-start.92 = (f32[768]{0:T(1024)}, f32[768]{0:T(1024)S(1)}, u32[]{:S(2)}) copy-start(f32[768]{0:T(1024)S(1)} %reduce.128) | copy-start | bytes 9220
  235.8 10.9 collective-permute-start.1
  249.2 112.8 %reduce-scatter.26.cloned.1.call-start = ((), (), s32[]{:S(2)}) async-start(), calls=%async_computation.27 | async-start | bytes 3932160 | tf_op jit(solution)/shard_map/reduce_scatter | solution.py:49
  301.5 101.4 %all-gather.33.cloned.1.call-start = ((), (), s32[]{:S(2)}) async-start(), calls=%async_computation.28 | async-start | bytes 1966080 | tf_op jit(solution)/shard_map/all_gather | solution.py:45
  366.9 102.7 %reduce-scatter.28.cloned.1.call-start = ((), (), s32[]{:S(2)}) async-start(), calls=%async_computation.29 | async-start | bytes 3932160 | tf_op jit(solution)/shard_map/reduce_scatter | solution.py:49
  409.1 115.4 %all-gather.51.cloned.1.call-start = ((), (), s32[]{:S(2)}) async-start(), calls=%async_computation.44 | async-start | bytes 1966080 | tf_op jit(solution)/shard_map/all_gather | solution.py:45
  470.9 10.9 collective-permute-start.3
  486.5 75.9 %all-gather.43.cloned.1.call-start = ((), (), s32[]{:S(2)}) async-start(), calls=%async_computation.37 | async-start | bytes 1966080 | tf_op jit(solution)/shard_map/all_gather | solution.py:45
  487.1 113.5 %all-gather.23.cloned.1.call-start = ((), (), s32[]{:S(2)}) async-start(), calls=%async_computation.19 | async-start | bytes 1966080 | tf_op jit(solution)/shard_map/all_gather | solution.py:45
  487.8 150.1 %all-gather.35.cloned.1.call-start = ((), (), s32[]{:S(2)}) async-start(), calls=%async_computation.30 | async-start | bytes 1966080 | tf_op jit(solution)/shard_map/all_gather | solution.py:45
  488.4 256.3 %reduce-scatter.42.cloned.1.call-start = ((), (), s32[]{:S(2)}) async-start(), calls=%async_computation.45 | async-start | bytes 3932160 | tf_op jit(solution)/shard_map/reduce_scatter | solution.py:49
  684.2 123.0 %reduce-scatter.30.cloned.1.call-start = ((), (), s32[]{:S(2)}) async-start(), calls=%async_computation.31 | async-start | bytes 3932160 | tf_op jit(solution)/shard_map/reduce_scatter | solution.py:49
  711.3 158.3 %reduce-scatter.20.cloned.1.call-start = ((), (), s32[]{:S(2)}) async-start(), calls=%async_computation.20 | async-start | bytes 3932160 | tf_op jit(solution)/shard_map/reduce_scatter | solution.py:49
  722.2 147.5 %copy-start.14 = (bf16[1,256,768]{2,1,0:T(8,128)(2,1)S(1)}, bf16[1,256,768]{2,1,0:T(8,128)(2,1)}, u32[]{:S(2)}) copy-start(bf16[1,256,768]{2,1,0:T(8,128)(2,1)} %copy-done.13) | copy-start | bytes 1179652
  724.5 185.5 %all-gather.27.cloned.1.call-start = ((), (), s32[]{:S(2)}) async-start(), calls=%async_computation.22 | async-start | bytes 1966080 | tf_op jit(solution)/shard_map/all_gather | solution.py:45
  874.0 74.0 %all-gather.25.cloned.1.call-start = ((), (), s32[]{:S(2)}) async-start(), calls=%async_computation.21 | async-start | bytes 1966080 | tf_op jit(solution)/shard_map/all_gather | solution.py:53
  874.6 118.0 %reduce-scatter.22.cloned.1.call-start = ((), (), s32[]{:S(2)}) async-start(), calls=%async_computation.23 | async-start | bytes 1966080 | tf_op jit(solution)/shard_map/reduce_scatter | solution.py:57
  958.1 76.9 %all-gather.29.cloned.1.call-start = ((), (), s32[]{:S(2)}) async-start(), calls=%async_computation.24 | async-start | bytes 1966080 | tf_op jit(solution)/shard_map/all_gather | solution.py:53
  998.9 97.8 %reduce-scatter.24.cloned.1.call-start = ((), (), s32[]{:S(2)}) async-start(), calls=%async_computation.25 | async-start | bytes 1966080 | tf_op jit(solution)/shard_map/reduce_scatter | solution.py:57
  1062.1 72.0 %all-gather.39.cloned.1.call-start = ((), (), s32[]{:S(2)}) async-start(), calls=%async_computation.33 | async-start | bytes 1966080 | tf_op jit(solution)/shard_map/all_gather | solution.py:45
  1062.9 109.4 %all-gather.37.cloned.1.call-start = ((), (), s32[]{:S(2)}) async-start(), calls=%async_computation.32 | async-start | bytes 1966080 | tf_op jit(solution)/shard_map/all_gather | solution.py:53
  1099.8 12.0 collective-permute-start.2
  1113.5 103.3 %reduce-scatter.32.cloned.1.call-start = ((), (), s32[]{:S(2)}) async-start(), calls=%async_computation.34 | async-start | bytes 1966080 | tf_op jit(solution)/shard_map/reduce_scatter | solution.py:57
  1182.3 75.7 %all-gather.41.cloned.1.call-start = ((), (), s32[]{:S(2)}) async-start(), calls=%async_computation.35 | async-start | bytes 1966080 | tf_op jit(solution)/shard_map/all_gather | solution.py:53
  1221.9 99.5 %reduce-scatter.34.cloned.1.call-start = ((), (), s32[]{:S(2)}) async-start(), calls=%async_computation.36 | async-start | bytes 1966080 | tf_op jit(solution)/shard_map/reduce_scatter | solution.py:57
  1286.9 97.0 %reduce-scatter.36.cloned.1.call-start = ((), (), s32[]{:S(2)}) async-start(), calls=%async_computation.38 | async-start | bytes 3932160 | tf_op jit(solution)/shard_map/reduce_scatter | solution.py:49
  1299.9 125.2 %all-gather.47.cloned.1.call-start = ((), (), s32[]{:S(2)}) async-start(), calls=%async_computation.40 | async-start | bytes 1966080 | tf_op jit(solution)/shard_map/all_gather | solution.py:45
  1389.1 74.2 %all-gather.45.cloned.1.call-start = ((), (), s32[]{:S(2)}) async-start(), calls=%async_computation.39 | async-start | bytes 1966080 | tf_op jit(solution)/shard_map/all_gather | solution.py:53
  1389.1 12.3 collective-permute-start.4
  1403.4 103.9 %reduce-scatter.38.cloned.1.call-start = ((), (), s32[]{:S(2)}) async-start(), calls=%async_computation.41 | async-start | bytes 1966080 | tf_op jit(solution)/shard_map/reduce_scatter | solution.py:57
  1472.8 75.6 %all-gather.49.cloned.1.call-start = ((), (), s32[]{:S(2)}) async-start(), calls=%async_computation.42 | async-start | bytes 1966080 | tf_op jit(solution)/shard_map/all_gather | solution.py:53
  1512.3 74.2 %all-gather.53.cloned.1.call-start = ((), (), s32[]{:S(2)}) async-start(), calls=%async_computation.46 | async-start | bytes 1966080 | tf_op jit(solution)/shard_map/all_gather | solution.py:45
  1530.6 135.1 %all-reduce.5.cloned.1.call-start = ((), (), s32[]{:S(2)}) async-start(), calls=%async_computation.48 | async-start | bytes 7077888 | tf_op jit(solution)/shard_map/psum | solution.py:392
  1578.8 123.6 %reduce-scatter.40.cloned.1.call-start = ((), (), s32[]{:S(2)}) async-start(), calls=%async_computation.43 | async-start | bytes 1966080 | tf_op jit(solution)/shard_map/reduce_scatter | solution.py:57
  1583.6 188.5 %reduce-scatter.44.cloned.1.call-start = ((), (), s32[]{:S(2)}) async-start(), calls=%async_computation.47 | async-start | bytes 3932160 | tf_op jit(solution)/shard_map/reduce_scatter | solution.py:49
  1706.3 65.8 %collective-permute-start.5 = (bf16[1,256,768]{2,1,0:T(8,128)(2,1)}, bf16[1,256,768]{2,1,0:T(8,128)(2,1)S(1)}, u32[]{:S(2)}, u32[]{:S(2)}) collective-permute-start(bf16[1,256,768]{2,1,0:T(8,128)(2,1)} %fusion.350), channel_id=1, source_target_pairs={{0,16},{16,0},{1,17},{17,1},{2,18},{18,2},{3,19},{19,3},{4,20},{20... | collective-permute-start | bytes 1179656 | tf_op jit(solution)/shard_map/ppermute | solution.py:15
  (171 other events, 1673.9 us)
Sparse Core Ops, SparseCore 0:
  13.2 37.0 all-gather.18
  65.8 60.3 reduce-scatter.15
  131.3 35.8 all-gather.20
  173.8 60.3 reduce-scatter.17
  249.3 36.7 all-gather.30
  301.6 60.3 reduce-scatter.25
  367.0 35.8 all-gather.32
  409.2 60.3 reduce-scatter.27
  486.6 37.7 all-gather.50
  526.4 35.9 all-gather.42
  564.6 35.9 all-gather.22
  602.0 35.9 all-gather.34
  684.3 60.3 reduce-scatter.41
  746.9 60.2 reduce-scatter.29
  809.4 60.2 reduce-scatter.19
  874.1 35.8 all-gather.26
  912.0 35.9 all-gather.24
  958.3 34.3 reduce-scatter.21
  999.0 35.9 all-gather.28
  1062.3 34.3 reduce-scatter.23
  1098.2 35.8 all-gather.38
  1136.3 35.9 all-gather.36
  1182.4 34.3 reduce-scatter.31
  1222.1 35.8 all-gather.40
  1287.0 34.3 reduce-scatter.33
  1323.6 60.2 reduce-scatter.35
  1389.2 35.8 all-gather.46
  1427.3 35.9 all-gather.44
  1472.9 34.2 reduce-scatter.37
  1512.4 35.8 all-gather.48
  1550.5 35.9 all-gather.52
  1590.2 75.3 all-reduce.4
  1667.8 34.5 reduce-scatter.39
  1704.7 62.2 reduce-scatter.43
where the time goes:
time: 1800 us; the launch traced here: 1780 us
  waiting for transfers between devices  1270 us (71%)
  matrix products  264 us (15%)
  other arithmetic  110 us (6%)
  blocking collectives  70.5 us (4%)
  local copies, waits for them, and re-layouts  33.2 us (2%)
    reduce_scatter x9, waiting for transfers between devices, collect_rows(): return lax.psum_scatter(piece, 'tensor', scatter_dimension=1, tiled=True)  444 us
    all_gather x12, waiting for transfers between devices, spread_rows(): return lax.all_gather(piece, 'tensor', axis=1, tiled=True)  357 us
    reduce_scatter x6, waiting for transfers between devices, collect_grads(): lax.psum_scatter(piece.astype(jnp.bfloat16), 'tensor', scatter_dimension=...  187 us
    all_gather x6, waiting for transfers between devices, spread_grads(): return lax.all_gather(piece, 'tensor', axis=1, tiled=True)  180 us
    psum x1, blocking collectives, shards(): shared_total = lax.psum(shared_acc, ('dp', 'tensor'))  64.6 us
    psum x1, waiting for transfers between devices, shards(): lax.psum(for_sending(sharded_acc), 'dp')  64.3 us
    dot_general x12, matrix products, attend_forward(): jnp.einsum('bhqk,bkhe->bqhe', weights, values, preferred_element_type=jnp...  36.6 us
    ppermute x4, waiting for transfers between devices, passed_along(): return lax.ppermute(shard, axis, pairs)  36.4 us
  transfers between devices with their start and end apart: 40, of which 37 were waited for; matrix products, arithmetic and copies ran while one was open for 9% of the time, Pallas kernels for 0%

commit v1 on v0

v1 whole, which is shorter than its diff:
```python
import functools

import jax
import jax.numpy as jnp
import numpy as np
from jax import lax
from jax.experimental import pallas as pl
from jax.experimental.pallas import tpu as pltpu
from jax.sharding import Mesh
from jax.sharding import PartitionSpec as P

HEAD = 64
DEPTH = 12
BRANCH = DEPTH ** (-0.5)
EPSILON = 1e-05
NEGATIVE = -1e30
LANES = 128
AXES = ("pipe", "y", "core", "tensor")
F32 = jnp.float32
BF16 = jnp.bfloat16


def ring_order(count):
    return list(range(0, count, 2)) + list(range(1, count, 2))[::-1]


def ring(value):
    order = ring_order(lax.axis_size("tensor"))
    return lax.ppermute(value, "tensor", list(zip(order, order[1:] + order[:1])))


def swap(value, axis):
    return lax.ppermute(value, axis, [(0, 1), (1, 0)])


def along_pipe(value, by):
    return lax.ppermute(value, "pipe", [(0, 1)] if by > 0 else [(1, 0)])


def routes(section, large):
    count = lax.axis_size("tensor")

    def index(x, y, c, z):
        return ((x * 2 + y) * 2 + c) * count + z

    pairs = []
    for micro in range(2):
        for y in range(2):
            for c in range(2):
                for core in range(2):
                    block = 3 - core if large else core
                    pairs.append((index(micro, y, c, block), index(section, y, core, 2 * micro + c)))
    return pairs


def fetch(block, section):
    return [lax.ppermute(block, AXES, routes(section, large)) for large in (False, True)]


def give_back(small, large, section):
    pieces = []
    for rows, is_large in ((small, False), (large, True)):
        pairs = [(b, a) for a, b in routes(section, is_large)]
        pieces.append(lax.ppermute(rows, AXES, pairs))
    return jnp.where(lax.axis_index("tensor") < 2, pieces[0], pieces[1])


def nt(left, right):
    return lax.dot_general(left, right, (((1,), (1,)), ((), ())), preferred_element_type=F32)


def tn(left, right):
    return lax.dot_general(left, right, (((0,), (0,)), ((), ())), preferred_element_type=F32)


def tk(left, right):
    turned = right.astype(F32).T.astype(BF16)
    return nn(turned, left).T


def nn(left, right):
    return lax.dot_general(left, right, (((1,), (0,)), ((), ())), preferred_element_type=F32)


def head_mask(rows, head):
    lanes = lax.broadcasted_iota(jnp.int32, (rows, LANES), 1)
    return (lanes >= head * HEAD) & (lanes < (head + 1) * HEAD)


def only(mask, value, factor=1.0):
    return jnp.where(mask, value.astype(F32) * factor, 0.0).astype(BF16)


def attend_kernel(keep_weights, core_ref, q_ref, k_ref, v_ref, ko_ref, vo_ref, o_ref, *p_refs):
    rows = q_ref.shape[0] // 2
    second = core_ref[0] == 1
    keys = lax.broadcasted_iota(jnp.int32, (rows, rows), 0)
    places = lax.broadcasted_iota(jnp.int32, (rows, rows), 1)
    allowed = keys <= places
    factor = HEAD ** (-0.5)
    small = pl.ds(0, rows)
    large = pl.ds(rows, rows)
    k5 = jnp.where(second, ko_ref[small, :].astype(F32), ko_ref[large, :].astype(F32)).astype(BF16)
    v5 = jnp.where(second, vo_ref[small, :].astype(F32), vo_ref[large, :].astype(F32))
    out_small = None
    out_large = None
    for head in range(LANES // HEAD):
        mask = head_mask(rows, head)

        def query(value):
            return only(mask, value, factor)

        qs, ql = query(q_ref[small, :]), query(q_ref[large, :])
        qf = query(jnp.where(second, q_ref[small, :].astype(F32), q_ref[large, :].astype(F32)))
        s1 = jnp.where(allowed, nt(k_ref[small, :], qs), NEGATIVE)
        s2 = nt(k_ref[small, :], ql)
        s3 = jnp.where(allowed, nt(k_ref[large, :], ql), NEGATIVE)
        s4 = nt(ko_ref[small, :], ql)
        s5 = nt(k5, qf)

        def peak(value):
            return jnp.max(value, axis=0, keepdims=True)

        def total(value):
            return jnp.sum(value, axis=0, keepdims=True)

        m5 = peak(s5)
        ms = peak(s1)
        ml = jnp.maximum(jnp.maximum(peak(s2), peak(s3)), peak(s4))
        ms = jnp.where(second, jnp.maximum(ms, m5), ms)
        ml = jnp.where(second, ml, jnp.maximum(ml, m5))
        mf = jnp.where(second, ms, ml)
        e1 = jnp.exp(s1 - ms)
        e2 = jnp.exp(s2 - ml)
        e3 = jnp.exp(s3 - ml)
        e4 = jnp.exp(s4 - ml)
        e5 = jnp.exp(s5 - mf)
        t5 = total(e5)
        rs = total(e1)
        rl = total(e2) + total(e3) + total(e4)
        rs = 1.0 / jnp.where(second, rs + t5, rs)
        rl = 1.0 / jnp.where(second, rl, rl + t5)
        rf = jnp.where(second, rs, rl)
        p1 = (e1 * rs).astype(BF16)
        p2 = (e2 * rl).astype(BF16)
        p3 = (e3 * rl).astype(BF16)
        p4 = (e4 * rl).astype(BF16)
        p5 = (e5 * rf).astype(BF16)
        if keep_weights:
            for place, value in enumerate((p1, p2, p3, p4, p5)):
                p_refs[0][head, place] = value
        vs = only(mask, v_ref[small, :])
        o5 = tk(p5, only(mask, v5))
        os = tk(p1, vs) + jnp.where(second, o5, 0.0)
        ol = (
            tk(p2, vs)
            + tk(p3, only(mask, v_ref[large, :]))
            + tk(p4, only(mask, vo_ref[small, :]))
            + jnp.where(second, 0.0, o5)
        )
        out_small = os if out_small is None else out_small + os
        out_large = ol if out_large is None else out_large + ol
    o_ref[small, :] = out_small.astype(BF16)
    o_ref[large, :] = out_large.astype(BF16)


def attend_back_kernel(
    core_ref, q_ref, k_ref, v_ref, ko_ref, vo_ref, go_ref, o_ref, p_ref, gq_ref, own_ref, other_ref, sums_ref
):
    rows = q_ref.shape[0] // 2
    second = core_ref[0] == 1
    factor = HEAD ** (-0.5)
    small = pl.ds(0, rows)
    large = pl.ds(rows, rows)

    def fifth(ref, first, last):
        return jnp.where(second, ref[first, :].astype(F32), ref[last, :].astype(F32))

    k5 = fifth(ko_ref, small, large)
    v5 = fifth(vo_ref, small, large).astype(BF16)
    q5 = fifth(q_ref, small, large)
    g5 = fifth(go_ref, small, large)
    product = go_ref[...].astype(F32) * o_ref[...].astype(F32)
    high = product.astype(BF16)
    low = (product - high.astype(F32)).astype(BF16)
    totals = {}

    def add(name, value):
        totals[name] = value if name not in totals else totals[name] + value

    for head in range(LANES // HEAD):
        mask = head_mask(rows, head)
        ones = jnp.where(head_mask(16, head), 1.0, 0.0).astype(BF16)
        inner = (nt(ones, high) + nt(ones, low))[0:1]
        ds_, dl_ = inner[:, :rows], inner[:, rows:]
        df_ = jnp.where(second, ds_, dl_)

        def weight(place):
            return p_ref[head, place]

        qs, ql, qf = (only(mask, value, factor) for value in (q_ref[small, :], q_ref[large, :], q5))
        gs, gl, gf = (only(mask, value) for value in (go_ref[small, :], go_ref[large, :], g5))

        def score_grad(place, values, rows_grad, shift):
            return (weight(place).astype(F32) * (nt(values, rows_grad) - shift)).astype(BF16)

        z1 = score_grad(0, v_ref[small, :], gs, ds_)
        z2 = score_grad(1, v_ref[small, :], gl, dl_)
        z3 = score_grad(2, v_ref[large, :], gl, dl_)
        z4 = score_grad(3, vo_ref[small, :], gl, dl_)
        z5 = score_grad(4, v5, gf, df_)
        k_small = only(mask, k_ref[small, :])
        gq5 = tk(z5, only(mask, k5))
        add("qs", tk(z1, k_small) + jnp.where(second, gq5, 0.0))
        add(
            "ql",
            tk(z2, k_small)
            + tk(z3, only(mask, k_ref[large, :]))
            + tk(z4, only(mask, ko_ref[small, :]))
            + jnp.where(second, 0.0, gq5),
        )
        add("ks", nn(z1, qs) + nn(z2, ql))
        add("kl", nn(z3, ql))
        add("k4", nn(z4, ql))
        add("k5", nn(z5, qf))
        add("vs", nn(weight(0), gs) + nn(weight(1), gl))
        add("vl", nn(weight(2), gl))
        add("v4", nn(weight(3), gl))
        add("v5", nn(weight(4), gf))
    gqs, gql = totals["qs"] * factor, totals["ql"] * factor
    gq_ref[small, :] = gqs.astype(BF16)
    gq_ref[large, :] = gql.astype(BF16)
    for place, name in enumerate("kv"):
        own_ref[place, small, :] = totals[name + "s"]
        own_ref[place, large, :] = totals[name + "l"]
        four, five = totals[name + "4"], totals[name + "5"]
        other_ref[place, small, :] = (four + jnp.where(second, five, 0.0)).astype(BF16)
        other_ref[place, large, :] = jnp.where(second, 0.0, five).astype(BF16)
    sum_q = jnp.sum(gqs, axis=0, keepdims=True) + jnp.sum(gql, axis=0, keepdims=True)
    sum_v = jnp.sum(totals["vs"] + totals["vl"] + totals["v4"] + totals["v5"], axis=0, keepdims=True)
    row = lax.broadcasted_iota(jnp.int32, (8, LANES), 0)
    sums_ref[...] = jnp.where(row == 0, sum_q, jnp.where(row == 1, sum_v, 0.0))


def attend(core, qkv, kv_other, keep_weights):
    length, triple = qkv.shape
    width = triple // 3
    pairs = width // LANES
    rows = length // 2

    def at(shift):
        return pl.BlockSpec((length, LANES), lambda i: (0, i + shift))

    shapes = [jax.ShapeDtypeStruct((length, width), BF16)]
    outs = [at(0)]
    if keep_weights:
        shapes.append(jax.ShapeDtypeStruct((width // HEAD, 5, rows, rows), BF16))
        outs.append(pl.BlockSpec((2, 5, rows, rows), lambda i: (i, 0, 0, 0)))
    return pl.pallas_call(
        functools.partial(attend_kernel, keep_weights),
        grid=(pairs,),
        out_shape=shapes,
        in_specs=[
            pl.BlockSpec(memory_space=pltpu.SMEM),
            at(0),
            at(pairs),
            at(2 * pairs),
            at(0),
            at(pairs),
        ],
        out_specs=outs,
        compiler_params=pltpu.CompilerParams(vmem_limit_bytes=48 * 1024 * 1024),
        cost_estimate=pl.CostEstimate(
            flops=20 * rows * rows * width * 2, bytes_accessed=16 * length * width, transcendentals=5 * rows * rows * 12
        ),
        name="attend",
    )(core, qkv, qkv, qkv, kv_other, kv_other)


def attend_back(core, qkv, kv_other, grad_mixed, mixed, weights):
    length, triple = qkv.shape
    width = triple // 3
    pairs = width // LANES
    rows = length // 2

    def at(shift):
        return pl.BlockSpec((length, LANES), lambda i: (0, i + shift))

    double = pl.BlockSpec((2, length, LANES), lambda i: (0, 0, i))
    return pl.pallas_call(
        attend_back_kernel,
        grid=(pairs,),
        out_shape=[
            jax.ShapeDtypeStruct((length, width), BF16),
            jax.ShapeDtypeStruct((2, length, width), F32),
            jax.ShapeDtypeStruct((2, length, width), BF16),
            jax.ShapeDtypeStruct((8, width), F32),
        ],
        in_specs=[
            pl.BlockSpec(memory_space=pltpu.SMEM),
            at(0),
            at(pairs),
            at(2 * pairs),
            at(0),
            at(pairs),
            at(0),
            at(0),
            pl.BlockSpec((2, 5, rows, rows), lambda i: (i, 0, 0, 0)),
        ],
        out_specs=[at(0), double, double, pl.BlockSpec((8, LANES), lambda i: (0, i))],
        compiler_params=pltpu.CompilerParams(vmem_limit_bytes=48 * 1024 * 1024),
        cost_estimate=pl.CostEstimate(
            flops=40 * rows * rows * width * 2, bytes_accessed=40 * length * width, transcendentals=0
        ),
        name="attend_back",
    )(core, qkv, qkv, qkv, kv_other, kv_other, grad_mixed, mixed, weights)


def gelu_and_slope(values):
    root = float(np.sqrt(2 / np.pi))
    cubic = 0.044715 * root
    square = values * values
    bend = jnp.tanh(values * (root + cubic * square))
    half = 0.5 + 0.5 * bend
    gate = values * half
    slope = half + gate * ((1.0 - bend) * (root + (3 * cubic) * square))
    return (gate, slope)


def tiles_of(units):
    return units // 512 if units % 512 == 0 else 1


def expand_kernel(rows_ref, expand_ref, bias_ref, reduce_ref, start_ref, total_ref, hidden_ref, slope_ref):
    units = expand_ref.shape[0]
    piece = 256 if units % 256 == 0 else units
    rows = rows_ref[...]
    total = None
    for offset in range(0, units, piece):
        part = pl.ds(offset, piece)
        gate, slope = gelu_and_slope(nt(rows, expand_ref[part, :]) + bias_ref[:, part])
        hidden = gate.astype(BF16)
        hidden_ref[:, part] = hidden
        slope_ref[:, part] = slope.astype(BF16)
        term = nn(hidden, reduce_ref[part, :])
        total = term if total is None else total + term

    @pl.when(pl.program_id(0) == 0)
    def _():
        total_ref[...] = start_ref[...] + total

    @pl.when(pl.program_id(0) > 0)
    def _():
        total_ref[...] += total


def contract_kernel(grad_ref, expand_ref, slope_ref, reduce_ref, start_ref, total_ref, pre_ref, sums_ref):
    units = expand_ref.shape[0]
    piece = 256 if units % 256 == 0 else units
    grad = grad_ref[...]
    total = None
    for offset in range(0, units, piece):
        part = pl.ds(offset, piece)
        pre = nt(grad, reduce_ref[part, :]) * slope_ref[:, part].astype(F32)
        sums_ref[:, part] = jnp.broadcast_to(jnp.sum(pre, axis=0, keepdims=True), (8, piece))
        rounded = pre.astype(BF16)
        pre_ref[:, part] = rounded
        term = nn(rounded, expand_ref[part, :])
        total = term if total is None else total + term

    @pl.when(pl.program_id(0) == 0)
    def _():
        total_ref[...] = start_ref[...] + total

    @pl.when(pl.program_id(0) > 0)
    def _():
        total_ref[...] += total


def feed_half(rows, expand_w, bias, reduce_w, start):
    length, width = rows.shape
    units = expand_w.shape[0]
    steps = tiles_of(units)
    tile = units // steps
    whole = pl.BlockSpec((length, width), lambda i: (0, 0))
    weight = pl.BlockSpec((tile, width), lambda i: (i, 0))
    across = pl.BlockSpec((length, tile), lambda i: (0, i))
    return pl.pallas_call(
        expand_kernel,
        grid=(steps,),
        out_shape=[
            jax.ShapeDtypeStruct((length, width), F32),
            jax.ShapeDtypeStruct((length, units), BF16),
            jax.ShapeDtypeStruct((length, units), BF16),
        ],
        in_specs=[whole, weight, pl.BlockSpec((1, tile), lambda i: (0, i)), weight, whole],
        out_specs=[whole, across, across],
        compiler_params=pltpu.CompilerParams(vmem_limit_bytes=40 * 1024 * 1024),
        cost_estimate=pl.CostEstimate(
            flops=4 * length * width * units, bytes_accessed=4 * width * units, transcendentals=length * units
        ),
        name="feed_half",
    )(rows, expand_w, bias.reshape(1, units), reduce_w, start)


def feed_half_back(grad, expand_w, slope, reduce_w, start):
    length, width = grad.shape
    units = expand_w.shape[0]
    steps = tiles_of(units)
    tile = units // steps
    whole = pl.BlockSpec((length, width), lambda i: (0, 0))
    weight = pl.BlockSpec((tile, width), lambda i: (i, 0))
    across = pl.BlockSpec((length, tile), lambda i: (0, i))
    return pl.pallas_call(
        contract_kernel,
        grid=(steps,),
        out_shape=[
            jax.ShapeDtypeStruct((length, width), F32),
            jax.ShapeDtypeStruct((length, units), BF16),
            jax.ShapeDtypeStruct((8, units), F32),
        ],
        in_specs=[whole, weight, across, weight, whole],
        out_specs=[whole, across, pl.BlockSpec((8, tile), lambda i: (0, i))],
        compiler_params=pltpu.CompilerParams(vmem_limit_bytes=40 * 1024 * 1024),
        cost_estimate=pl.CostEstimate(
            flops=4 * length * width * units, bytes_accessed=4 * width * units, transcendentals=0
        ),
        name="feed_half_back",
    )(grad, expand_w, slope, reduce_w, start)


def tie(value, *others):
    return lax.optimization_barrier((value, *others))[0]


def normalize_rows(rows):
    centred = rows - jnp.mean(rows, axis=-1, keepdims=True)
    inverse = lax.rsqrt(jnp.mean(centred * centred, axis=-1, keepdims=True) + EPSILON)
    return (centred * inverse, inverse)


def norm_backward(grad_normed, normed, inverse, gain):
    scaled = grad_normed * gain
    centred = scaled - jnp.mean(scaled, axis=-1, keepdims=True)
    return inverse * (centred - normed * jnp.mean(scaled * normed, axis=-1, keepdims=True))


def attention_forward(core, rows_in, weights, keep, after_projection=None):
    gain_a, shift_a, proj_in, proj_bias, proj_out, bias_out = weights
    normed_one, inverse_one = normalize_rows(rows_in)
    ready_one = (normed_one * gain_a + shift_a).astype(BF16)
    qkv = (nt(ready_one, proj_in) + proj_bias).astype(BF16)
    width = rows_in.shape[1]
    kv_other = swap(qkv[:, width:], "core")
    mixed, *kept_weights = attend(core, qkv, kv_other, keep)
    middle = rows_in + BRANCH * (nn(mixed, proj_out) + bias_out)
    kept = (normed_one, inverse_one, ready_one, qkv, kv_other, mixed, *kept_weights)
    return middle, kept


def feed_forward(middle, weights):
    gain_b, shift_b, halves, reduce_b = weights
    normed_two, inverse_two = normalize_rows(middle)
    ready_two = (normed_two * gain_b + shift_b).astype(BF16)
    total = jnp.broadcast_to(reduce_b, middle.shape)
    hidden, slope = [], []
    for expand_w, expand_b, reduce_w in halves:
        total, hidden_part, slope_part = feed_half(ready_two, expand_w, expand_b, reduce_w, total)
        hidden.append(hidden_part)
        slope.append(slope_part)
    return middle + BRANCH * total, (normed_two, inverse_two, ready_two, hidden, slope)


def feed_backward(kept, grad_result, weights):
    gain_b, _, halves, _ = weights
    normed_two, inverse_two, ready_two, hidden, slope = kept
    grad_outcome = BRANCH * grad_result
    rounded_outcome = grad_outcome.astype(BF16)
    total = jnp.zeros_like(grad_result)
    rounded_pre, sums = [], []
    for (expand_w, _, reduce_w), slope_part in zip(halves, slope):
        total, pre, sum_part = feed_half_back(rounded_outcome, expand_w, slope_part, reduce_w, total)
        rounded_pre.append(pre)
        sums.append(sum_part[0])
    grad_middle = grad_result + norm_backward(total, normed_two, inverse_two, gain_b)
    shared = [total * normed_two, total, grad_outcome]
    return grad_middle, rounded_outcome, rounded_pre, sums, shared


def attention_backward(core, kept, grad_middle, weights, last=()):
    gain_a, _, proj_in, _, proj_out, _ = weights
    normed_one, inverse_one, ready_one, qkv, kv_other, mixed, attention = kept
    width = normed_one.shape[1]
    grad_attended = BRANCH * grad_middle
    rounded_attended = grad_attended.astype(BF16)
    grad_mixed = nt(rounded_attended, proj_out).astype(BF16)
    grad_q, own, other, sums = attend_back(core, qkv, kv_other, grad_mixed, mixed, attention)
    other = tie(other, *last)
    grad_kv = (own + swap(other, "core").astype(F32)).astype(BF16)
    grad_normed_one = (
        nn(grad_q, proj_in[:width]) + nn(grad_kv[0], proj_in[width : 2 * width]) + nn(grad_kv[1], proj_in[2 * width :])
    )
    grad_in = grad_middle + norm_backward(grad_normed_one, normed_one, inverse_one, gain_a)
    shared = [grad_normed_one * normed_one, grad_normed_one, grad_attended]
    return grad_in, rounded_attended, (grad_q, grad_kv[0], grad_kv[1]), sums[:2], shared


def narrow(value):
    return value.astype(BF16)


def wide_add(left, right):
    return narrow(left.astype(F32) + right.astype(F32))


def over_groups(value):
    return lax.psum(value, "outer") if lax.axis_size("outer") > 1 else value


def ring_add(parts):
    count = len(parts)
    total = parts[1 % count]
    for step in range(1, count):
        total = wide_add(ring(total), parts[(step + 1) % count])
    return total


def thirds(values):
    pieces = []
    for _ in range(3):
        piece = lax.reduce_precision(values, 8, 7)
        pieces.append(narrow(piece))
        values = values - piece
    return jnp.stack(pieces)


def shards(
    inputs, cotangent, gain_one, shift_one, attend_in, attend_bias, attend_out, out_bias,
    gain_two, shift_two, expand_in, expand_bias, reduce_out, reduce_bias,
):
    count = lax.axis_size("tensor")
    x, y, c, z = (lax.axis_index(axis) for axis in AXES)
    is_first = x == 0
    core = c.reshape(1).astype(jnp.int32)
    width = attend_in.shape[1]
    local = attend_in.shape[3]
    units = expand_in.shape[2]
    half = local // 2
    part = units // 4
    spare = 16

    def either(index, pair):
        first, second = pair
        return jnp.where(index == 0, first, second), jnp.where(index == 0, second, first)

    def quarters(value, axis):
        blocks = jnp.split(value, 4, axis)
        rows = [either(y, blocks[:2]), either(y, blocks[2:])]
        return list(zip(*(either(c, pair) for pair in zip(*rows))))

    rows_in = jnp.concatenate(fetch(inputs[0, 0], 0))
    own = jnp.concatenate([attend_in[0].transpose(1, 2, 0), attend_out])
    mine = jnp.where(c == 0, own[:2], own[2:])
    biases = thirds(jnp.concatenate([attend_bias[0].reshape(2 * local), expand_bias[0]])).reshape(-1)
    biases = jnp.pad(biases, (0, spare * width - biases.size)).reshape(spare, width)
    piece = jnp.where(y == 0, mine[:, :half], mine[:, half:]).reshape(local, width)
    piece = jnp.concatenate([piece, biases])
    bias_rows = [biases]
    pieces = []
    for _ in range(count - 1):
        piece = ring(piece)
        pieces.append(piece)
    expand_own = quarters(expand_in[0].T, 0)
    reduce_own = quarters(reduce_out[0], 0)
    feed = [jnp.stack([expand_own[0][0], reduce_own[0][0]])]
    feed_y = [jnp.stack([expand_own[0][1], reduce_own[0][1]])]
    moving = ring(tie(feed[0], pieces[0]))
    moving = tie(moving, pieces[-1])
    feed.append(moving)
    feed_y.append(swap(moving, "y"))
    moving = ring(moving)
    halves = []
    for piece in pieces:
        bias_rows.append(piece[local:])
        piece = piece[:local]
        pair = [value.reshape(2, half, width) for value in either(y, (piece, swap(piece, "y")))]
        halves.append(jnp.concatenate(pair, axis=1))
    halves = jnp.concatenate(halves, axis=1)
    first, second = either(c, (halves, swap(halves, "core")))
    both = [jnp.concatenate([own[kind], (first, second)[kind // 2][kind % 2]]) for kind in range(4)]
    proj_in = jnp.concatenate(both[:3])
    proj_out = both[3]
    biases = jnp.stack(bias_rows).reshape(count, -1)[:, : 3 * (2 * local + units)].reshape(count, 3, 2 * local + units)
    biases = biases.astype(F32)
    biases = biases[:, 0] + (biases[:, 1] + biases[:, 2])
    bias_q, bias_v = biases[:, :local].reshape(width), biases[:, local : 2 * local].reshape(width)
    proj_bias = jnp.concatenate([bias_q, jnp.zeros_like(bias_q), bias_v])
    expand_b = quarters(biases[:, 2 * local :], 1)
    expand_b = [jnp.concatenate([value.reshape(count * part) for value in pair]) for pair in expand_b]
    attention_weights = (gain_one[0], shift_one[0], proj_in, proj_bias, proj_out, out_bias[0])

    block = rows_in.shape[0] // 2
    middle, parts = attention_forward(core, rows_in.astype(F32), attention_weights, False)
    last = fetch(cotangent[0, 0], 1)
    moving = tie(moving, parts[3])
    feed.append(moving)
    feed_y.append(swap(moving, "y"))
    moving = ring(moving)
    moving = tie(moving, parts[5], *last)
    feed.append(moving)
    feed_y.append(swap(moving, "y"))
    last = jnp.concatenate(last)
    own_half = [jnp.concatenate([value[kind] for value in feed + feed_y]) for kind in range(2)]
    other_half = [swap(value, "core") for value in own_half]
    feed_weights = (
        gain_two[0],
        shift_two[0],
        [(own_half[0], expand_b[0], own_half[1]), (other_half[0], expand_b[1], other_half[1])],
        reduce_bias[0],
    )
    result = narrow(feed_forward(middle, feed_weights)[0])
    passed = jnp.concatenate([along_pipe(result[:block], 1), along_pipe(result[block:], 1)])
    rows_in = jnp.where(is_first, rows_in, passed)
    middle, kept_attention = attention_forward(core, rows_in.astype(F32), attention_weights, True)
    result, kept_feed = feed_forward(middle, feed_weights)
    result = narrow(result)
    outputs = give_back(result[:block], result[block:], 1)
    grad_middle = feed_backward(kept_feed, last.astype(F32), feed_weights)[0]
    grad_in = attention_backward(core, kept_attention, grad_middle, attention_weights, (outputs,))[0]
    grad_in = narrow(grad_in)
    returned = jnp.concatenate([along_pipe(grad_in[:block], -1), along_pipe(grad_in[block:], -1)])
    grad_result = jnp.where(is_first, returned, last)

    def unit_grads(units_of, rows_of, core_half, y_half):
        piece = units_of[core_half]
        span = piece.shape[1] // 2
        return tn(piece[:, y_half * span : (y_half + 1) * span], rows_of)

    rounded_outcome = narrow(BRANCH * grad_result.astype(F32))
    hidden = kept_feed[3]
    send = [unit_grads(hidden, rounded_outcome, 1, i) for i in range(2)]
    keep = [unit_grads(hidden, rounded_outcome, 0, i) for i in range(2)]
    send = [narrow(value) for value in send]
    reduce_arrived = [swap(value, "core") for value in send]
    grad_result, *keep = lax.optimization_barrier((grad_result, *keep, *send))[:3]
    grad_middle, _, rounded_pre, sums_pre, shared_feed = feed_backward(kept_feed, grad_result.astype(F32), feed_weights)
    reduce_sums = [wide_add(a, tie(b, grad_middle)) for a, b in zip(keep, reduce_arrived)]
    reduce_sums = jnp.stack(reduce_sums).reshape(2, count, part, width)
    reduce_total = ring_add([reduce_sums[:, slot] for slot in range(count)])
    ready_two = kept_feed[2]
    send = [unit_grads(rounded_pre, ready_two, 1, i) for i in (1, 0)]
    keep = [unit_grads(rounded_pre, ready_two, 0, i) for i in (1, 0)]
    send = [narrow(value) for value in send]
    grad_middle, *keep = lax.optimization_barrier((grad_middle, *keep, *send))[:3]
    expand_sums = [wide_add(a, swap(b, "core")).reshape(count, part, width) for a, b in zip(keep, send)]
    expand_parts = [None] * count
    for slot in list(range(1, count)) + [0]:
        expand_parts[slot] = wide_add(expand_sums[1][slot], swap(expand_sums[0][slot], "y"))
    expand_total = ring_add(expand_parts)
    grad_in, rounded_attended, grad_qkv, sums_qv, shared_attention = attention_backward(
        core, kept_attention, grad_middle, attention_weights
    )
    grad_in = narrow(grad_in)
    mixed, ready_one = kept_attention[5], kept_attention[2]
    typed_grads = [narrow(tn(value, ready_one)) for value in grad_qkv] + [narrow(tn(mixed, rounded_attended))]
    typed_grads = jnp.stack(typed_grads).reshape(2, 2, count, 2, half, width)
    typed_grads = typed_grads.transpose(0, 3, 2, 1, 4, 5).reshape(2, 2, count, local, width)
    shared = shared_attention[:2] + [shared_attention[2]] + shared_feed
    shared = jnp.stack([jnp.sum(value, axis=0) for value in shared])
    sums_qv = jnp.pad(sums_qv.reshape(2, count, local), ((0, 0), (0, 0), (0, 0)))
    sums_qv = jnp.concatenate([sums_qv[0], sums_qv[1], jnp.zeros((count, width - 2 * local), F32)], axis=1)[:, None]
    sums_pre = [[value.reshape(count, part) for value in jnp.split(half_sums, 2)] for half_sums in sums_pre]
    sums_pre = quarters(jnp.concatenate(sums_pre[0] + sums_pre[1], axis=1), 1)
    sums_pre = jnp.concatenate(sums_pre[0] + sums_pre[1], axis=1)[:, None]
    vectors = jnp.concatenate([jnp.broadcast_to(shared, (count,) + shared.shape), sums_qv, sums_pre], axis=1)
    vectors = narrow(vectors).reshape(count, 2, 2, 2, width).transpose(1, 2, 0, 3, 4)
    vectors = jnp.pad(vectors, ((0, 0), (0, 0), (0, 0), (0, spare - 2), (0, 0)))
    typed_grads = jnp.concatenate([typed_grads, vectors], axis=3)
    keep, send = either(c, (typed_grads[0], typed_grads[1]))
    typed_sums = wide_add(keep, swap(send, "core"))
    keep, send = either(y, (typed_sums[0], typed_sums[1]))
    typed_parts = [None] * count
    for slot in list(range(1, count)) + [0]:
        typed_parts[slot] = wide_add(keep[slot], swap(send[slot], "y"))
    typed_total = ring_add(typed_parts)
    input_grad = give_back(grad_in[:block], grad_in[block:], 0)
    def gathered(pair):
        pair = jnp.concatenate(pair)
        blocks = quarters(jnp.concatenate([pair, swap(pair, "core")]), 0)
        return jnp.concatenate(blocks[0] + blocks[1])

    reduce_other = swap(reduce_total, "y")
    grad_reduce = [over_groups(wide_add(reduce_total[i], reduce_other[1 - i])) for i in range(2)]
    grad_reduce = gathered(grad_reduce).astype(F32)
    expand_total = over_groups(expand_total)
    grad_expand = gathered([expand_total, swap(expand_total, "y")]).T.astype(F32)
    typed_total = over_groups(typed_total)
    pair = jnp.stack(either(y, (typed_total, swap(typed_total, "y"))))
    whole = either(c, (pair, swap(pair, "core")))
    vectors = jnp.stack([value[:, local : local + 2] for value in whole]).reshape(8, width).astype(F32)
    whole = [value[:, :local].reshape(2, 2, half, width).transpose(1, 0, 2, 3).reshape(2, local, width) for value in whole]
    grad_attend_in = jnp.concatenate([whole[0], whole[1][:1]]).transpose(2, 0, 1).astype(F32)
    grad_attend_out = whole[1][1].astype(F32)
    return (
        outputs[None, None],
        input_grad[None, None],
        vectors[0][None],
        vectors[1][None],
        grad_attend_in[None],
        vectors[6, : 2 * local].reshape(1, 2, local),
        grad_attend_out[None],
        vectors[2][None],
        vectors[3][None],
        vectors[4][None],
        grad_expand[None],
        vectors[7, :units][None],
        grad_reduce[None],
        vectors[5][None],
    )


def solution(mesh):
    pipe, groups, count = mesh.devices.shape
    split = Mesh(mesh.devices.reshape(pipe, groups // 4, 2, 2, count), ("pipe", "outer", "y", "core", "tensor"))
    dp = ("outer", "y", "core")
    rows = P("pipe", dp, "tensor", None)
    vector = P("pipe", None)
    placed = (
        rows,
        rows,
        vector,
        vector,
        P("pipe", None, None, "tensor"),
        P("pipe", None, "tensor"),
        P("pipe", "tensor", None),
        vector,
        vector,
        vector,
        P("pipe", None, "tensor"),
        P("pipe", "tensor"),
        P("pipe", "tensor", None),
        vector,
    )
    return jax.shard_map(shards, mesh=split, in_specs=placed, out_specs=(rows, rows) + placed[2:], check_vma=False)
```

time: 1800 us -> 520 us (0.29)
  waiting for transfers between devices: 1270 us -> 208 us
  matrix products: 264 us -> 39 us
  Pallas kernels: 0 us -> 109 us
  blocking collectives: 70.5 us -> 0 us
  other arithmetic: 110 us -> 49.5 us
  starting transfers between devices: 14.6 us -> 54.6 us
    reduce_scatter x15 -> x0, waiting for transfers between devices: 631 us -> none  [the longest x9 444 us: collect_rows(): return lax.psum_scatter(piece, 'tensor', scatter_dimension=1, tiled=True)]
    all_gather x18 -> x0, waiting for transfers between devices: 537 us -> none  [the longest x12 357 us: spread_rows(): return lax.all_gather(piece, 'tensor', axis=1, tiled=True)]
    dot_general x90 -> x24, matrix products: 264 us -> 39 us  [the longest x12 21.6 us: tn(): lax.dot_general(left, right, (((0,), (0,)), ((), ())), preferred_element_...]
    ppermute x6 -> x59, waiting for transfers between devices: 36.4 us -> 208 us  [the longest x15 84.8 us: ring(): lax.ppermute(value, 'tensor', list(zip(order, order[1:] + order[:1])))]
    pallas_call x0 -> x12, Pallas kernels: none -> 109 us  [the longest x2 30.1 us: attend_back(): pl.pallas_call(attend_back_kernel, grid=(pairs,), out_shape=[jax.ShapeDty...]
    psum x2 -> x0, blocking collectives: 70.5 us -> none  [the longest x1 64.6 us: shards(): shared_total = lax.psum(shared_acc, ('dp', 'tensor'))]
    psum x1 -> x0, waiting for transfers between devices: 64.3 us -> none  [shards(): lax.psum(for_sending(sharded_acc), 'dp')]
    reduce_sum x27 -> x6, other arithmetic: 51.5 us -> 5.74 us  [the longest x3 4.61 us: shards(): shared = jnp.stack([jnp.sum(value, axis=0) for value in shared])]
  transfers between devices with their start and end apart: 40 -> 59, of which waited for: 37 -> 28; matrix products, arithmetic and copies ran while one was open for 9% -> 16% of each run, Pallas kernels for 0% -> 7%
where the time goes in v1:
time: 520 us; the launch traced here: 513 us
  waiting for transfers between devices  208 us (40%)
  Pallas kernels  109 us (21%)
  starting transfers between devices  54.6 us (10%)
  local copies, waits for them, and re-layouts  50.6 us (10%)
  other arithmetic  49.5 us (10%)
  matrix products  39 us (8%)
    ppermute x15, waiting for transfers between devices, ring(): lax.ppermute(value, 'tensor', list(zip(order, order[1:] + order[:1])))  84.8 us
    ppermute x32, waiting for transfers between devices, swap(): return lax.ppermute(value, axis, [(0, 1), (1, 0)])  40.8 us
    ppermute x4, waiting for transfers between devices, fetch(): lax.ppermute(block, AXES, routes(section, large))  36.2 us
    unnamed x200, local copies, waits for them, and re-layouts  34.1 us
    ppermute x4, waiting for transfers between devices, along_pipe(): return lax.ppermute(value, 'pipe', [(0, 1)] if by > 0 else [(1, 0)])  33.3 us
    pallas_call x2, Pallas kernels, attend_back(): pl.pallas_call(attend_back_kernel, grid=(pairs,), out_shape=[jax.ShapeDty...  30.1 us
    pallas_call x4, Pallas kernels, feed_half(): pl.pallas_call(expand_kernel, grid=(steps,), out_shape=[jax.ShapeDtypeStr...  28.3 us
    pallas_call x2, Pallas kernels, attend(): pl.pallas_call(functools.partial(attend_kernel, keep_weights), grid=(pair...  25.4 us
  transfers between devices with their start and end apart: 59, of which 28 were waited for; matrix products, arithmetic and copies ran while one was open for 16% of the time, Pallas kernels for 7%

profile of v1, /device:TPU:17, one launch (start us, length us, event | category | flops | bytes accessed | tf_op | source)
XLA Modules:
  0.0 513.0 jit_solution(11065430359866999751)
XLA Ops:
  1.9 5.2 %collective-permute-start.1 = (bf16[256,768]{1,0:T(8,128)(2,1)}, bf16[256,768]{1,0:T(8,128)(2,1)}, u32[]{:S(2)}, u32[]{:S(2)}) collective-permute-start(bf16[256,768]{1,0:T(8,128)(2,1)} %bitcast.287), channel_id=1, source_target_pairs={{3,0},{2,4},{7,1},{6,5},{11,8},{10,12},{15,9},{14,13},{19,2},{18,6... | collective-permute-start | bytes 1179656 | tf_op jit(solution)/shard_map/ppermute | solution.py:57
  17.5 4.0 collective-permute-done.2
  24.1 25.5 %collective-permute-done = bf16[256,768]{1,0:T(8,128)(2,1)} collective-permute-done((bf16[256,768]{1,0:T(8,128)(2,1)}, bf16[256,768]{1,0:T(8,128)(2,1)}, u32[]{:S(2)}, u32[]{:S(2)}) %collective-permute-start) | collective-permute-done | bytes 393248 | tf_op jit(solution)/shard_map/ppermute | solution.py:57
  52.2 4.2 collective-permute-start.5
  58.0 8.9 %collective-permute-done.6 = bf16[208,768]{1,0:T(8,128)(2,1)S(1)} collective-permute-done((bf16[208,768]{1,0:T(8,128)(2,1)S(1)}, bf16[208,768]{1,0:T(8,128)(2,1)S(1)}, u32[]{:S(2)}, u32[]{:S(2)}) %collective-permute-start.6) | collective-permute-done | bytes 319520 | tf_op jit(solution)/shard_map/ppermute | solution.py:29
  68.7 5.8 %collective-permute-done.7 = bf16[192,768]{1,0:T(8,128)(2,1)S(1)} collective-permute-done((bf16[192,768]{1,0:T(8,128)(2,1)S(1)}, bf16[192,768]{1,0:T(8,128)(2,1)S(1)}, u32[]{:S(2)}, u32[]{:S(2)}) %collective-permute-start.7) | collective-permute-done | bytes 294944 | tf_op jit(solution)/shard_map/ppermute | solution.py:33
  81.6 2.2 broadcast_select_fusion
  91.5 13.1 %collective-permute-done.11 = bf16[2,192,768]{2,1,0:T(8,128)(2,1)S(1)} collective-permute-done((bf16[2,192,768]{2,1,0:T(8,128)(2,1)}, bf16[2,192,768]{2,1,0:T(8,128)(2,1)S(1)}, u32[]{:S(2)}, u32[]{:S(2)}) %collective-permute-start.11) | collective-permute-done | bytes 589856 | tf_op jit(solution)/shard_map/ppermute | solution.py:29
  107.7 11.3 %attend.2 = bf16[512,768]{1,0:T(8,128)(2,1)S(1)} custom-call(s32[1]{0:T(128)} %bitcast.1.core_ref, bf16[512,2304]{1,0:T(8,128)(2,1)S(1)} %fusion.3.q_ref.k_ref.v_ref, bf16[512,2304]{1,0:T(8,128)(2,1)S(1)} %fusion.3.q_ref.k_ref.v_ref, bf16[512,2304]{1,0:T(8,128)(2,1)S(1)} %fusion.3.q_ref.k_ref.v_ref, ...), custom_call_target="tpu_custom_call" | custom-call | flops 2013265920 | bytes 6291456 | tf_op jit(solution)/shard_map/attend/pallas_call | solution.py:259
  119.0 10.7 %collective-permute-done.14 = bf16[256,768]{1,0:T(8,128)(2,1)S(1)} collective-permute-done((bf16[256,768]{1,0:T(8,128)(2,1)S(1)}, bf16[256,768]{1,0:T(8,128)(2,1)S(1)}, u32[]{:S(2)}, u32[]{:S(2)}) %collective-permute-start.14) | collective-permute-done | bytes 393248 | tf_op jit(solution)/shard_map/ppermute | solution.py:57
  134.2 10.7 %collective-permute-done.17 = bf16[2,192,768]{2,1,0:T(8,128)(2,1)S(1)} collective-permute-done((bf16[2,192,768]{2,1,0:T(8,128)(2,1)S(1)}, bf16[2,192,768]{2,1,0:T(8,128)(2,1)S(1)}, u32[]{:S(2)}, u32[]{:S(2)}) %collective-permute-start.17) | collective-permute-done | bytes 589856 | tf_op jit(solution)/shard_map/ppermute | solution.py:33
  153.9 2.6 slice_bitcast_fusion.1
  158.6 7.7 %feed_half.4 = (f32[512,768]{1,0:T(8,128)S(1)}, bf16[512,1536]{1,0:T(8,128)(2,1)}, bf16[512,1536]{1,0:T(8,128)(2,1)}) custom-call(bf16[512,768]{1,0:T(8,128)(2,1)S(1)} %add_convert_fusion.9.rows_ref, bf16[1536,768]{1,0:T(8,128)(2,1)S(1)} %get-tuple-element.197.expand_ref, f32[1,1536]{1,0:T(1,128)S(1)} %reshape.530.bias_ref, ...), custom_call_target="tpu_custom_call" | custom-call | flops 2415919104 | bytes 4718592 | tf_op jit(solution)/shard_map/feed_half/pallas_call | solution.py:388
  166.4 7.5 %feed_half.5 = (f32[512,768]{1,0:T(8,128)S(1)}, bf16[512,1536]{1,0:T(8,128)(2,1)}, bf16[512,1536]{1,0:T(8,128)(2,1)}) custom-call(bf16[512,768]{1,0:T(8,128)(2,1)S(1)} %add_convert_fusion.9.rows_ref, bf16[1536,768]{1,0:T(8,128)(2,1)} %collective-permute-done.18.expand_ref, f32[1,1536]{1,0:T(1,128)S(1)} %reshape.527.bias_ref, ...), custom_call_target="tpu_custom_call" | custom-call | flops 2415919104 | bytes 4718592 | tf_op jit(solution)/shard_map/feed_half/pallas_call | solution.py:388
  176.9 6.6 %collective-permute-done.20 = bf16[256,768]{1,0:T(8,128)(2,1)S(1)} collective-permute-done((bf16[256,768]{1,0:T(8,128)(2,1)S(1)}, bf16[256,768]{1,0:T(8,128)(2,1)S(1)}, u32[]{:S(2)}, u32[]{:S(2)}) %collective-permute-start.20) | collective-permute-done | bytes 393248 | tf_op jit(solution)/shard_map/ppermute | solution.py:37
  183.5 8.4 %collective-permute-done.21 = bf16[256,768]{1,0:T(8,128)(2,1)S(1)} collective-permute-done((bf16[256,768]{1,0:T(8,128)(2,1)S(1)}, bf16[256,768]{1,0:T(8,128)(2,1)S(1)}, u32[]{:S(2)}, u32[]{:S(2)}) %collective-permute-start.21) | collective-permute-done | bytes 393248 | tf_op jit(solution)/shard_map/ppermute | solution.py:37
  192.7 4.2 fusion.4.q_ref.k_ref.v_ref
  203.0 14.1 %attend.3 = (bf16[512,768]{1,0:T(8,128)(2,1)S(1)}, bf16[12,5,256,256]{3,2,1,0:T(8,128)(2,1)}) custom-call(s32[1]{0:T(128)} %bitcast.1.core_ref, bf16[512,2304]{1,0:T(8,128)(2,1)S(1)} %fusion.4.q_ref.k_ref.v_ref, bf16[512,2304]{1,0:T(8,128)(2,1)S(1)} %fusion.4.q_ref.k_ref.v_ref, bf16[512,2304]{1,0:T(8,128)(2,1)S(1)} %fusion.4.q_ref.k_ref.v_ref, ...), custom_call_target="tpu_custom_call" | custom-call | flops 2013265920 | bytes 6291456 | tf_op jit(solution)/shard_map/attend/pallas_call | solution.py:259
  220.7 6.5 %feed_half.6 = (f32[512,768]{1,0:T(8,128)S(1)}, bf16[512,1536]{1,0:T(8,128)(2,1)S(1)}, bf16[512,1536]{1,0:T(8,128)(2,1)S(1)}) custom-call(bf16[512,768]{1,0:T(8,128)(2,1)S(1)} %add_convert_fusion.7.rows_ref, bf16[1536,768]{1,0:T(8,128)(2,1)S(1)} %copy-done.4, f32[1,1536]{1,0:T(1,128)S(1)} %reshape.530.bias_ref, ...), custom_call_target="tpu_custom_call" | custom-call | flops 2415919104 | bytes 4718592 | tf_op jit(solution)/shard_map/feed_half/pallas_call | solution.py:388
  227.3 6.8 %feed_half_back.4 = (f32[512,768]{1,0:T(8,128)S(1)}, bf16[512,1536]{1,0:T(8,128)(2,1)}, f32[8,1536]{1,0:T(8,128)}) custom-call(bf16[512,768]{1,0:T(8,128)(2,1)S(1)} %fusion.35.grad_ref, bf16[1536,768]{1,0:T(8,128)(2,1)S(1)} %copy-done.4, bf16[512,1536]{1,0:T(8,128)(2,1)S(1)} %get-tuple-element.62.slope_ref, bf16[1536,768]{1,0:T(8,128)(2,1)} %get-tuple-element.196.reduce_ref, ...), custom_call_target="tpu_custom_call" | custom-call | flops 2415919104 | bytes 4718592 | tf_op jit(solution)/shard_map/feed_half_back/pallas_call | solution.py:414
  235.3 6.6 %feed_half.7 = (f32[512,768]{1,0:T(8,128)S(1)}, bf16[512,1536]{1,0:T(8,128)(2,1)S(1)}, bf16[512,1536]{1,0:T(8,128)(2,1)S(1)}) custom-call(bf16[512,768]{1,0:T(8,128)(2,1)S(1)} %add_convert_fusion.7.rows_ref, bf16[1536,768]{1,0:T(8,128)(2,1)} %collective-permute-done.18.expand_ref, f32[1,1536]{1,0:T(1,128)S(1)} %reshape.527.bias_ref, ...), custom_call_target="tpu_custom_call" | custom-call | flops 2415919104 | bytes 4718592 | tf_op jit(solution)/shard_map/feed_half/pallas_call | solution.py:388
  247.0 6.8 %feed_half_back.5 = (f32[512,768]{1,0:T(8,128)S(1)}, bf16[512,1536]{1,0:T(8,128)(2,1)}, f32[8,1536]{1,0:T(8,128)}) custom-call(bf16[512,768]{1,0:T(8,128)(2,1)S(1)} %fusion.35.grad_ref, bf16[1536,768]{1,0:T(8,128)(2,1)} %collective-permute-done.18.expand_ref, bf16[512,1536]{1,0:T(8,128)(2,1)S(1)} %copy-done.8, ...), custom_call_target="tpu_custom_call" | custom-call | flops 2415919104 | bytes 4718592 | tf_op jit(solution)/shard_map/feed_half_back/pallas_call | solution.py:414
  258.0 15.1 %attend_back.2 = (bf16[512,768]{1,0:T(8,128)(2,1)S(1)}, f32[2,512,768]{2,1,0:T(8,128)}, bf16[2,512,768]{2,1,0:T(8,128)(2,1)S(1)}, f32[8,768]{1,0:T(8,128)}) custom-call(s32[1]{0:T(128)} %bitcast.1.core_ref, bf16[512,2304]{1,0:T(8,128)(2,1)} %copy-done, bf16[512,2304]{1,0:T(8,128)(2,1)} %copy-done, bf16[512,2304]{1,0:T(8,128)(2,1)} %copy-done, ...), custom_call_target="tpu_custom_call" | custom-call | flops 4026531840 | bytes 15728640 | tf_op jit(solution)/shard_map/attend_back/pallas_call | solution.py:290
  273.1 3.7 collective-permute-done.24
  288.3 9.9 %collective-permute-done.26 = bf16[256,768]{1,0:T(8,128)(2,1)S(1)} collective-permute-done((bf16[256,768]{1,0:T(8,128)(2,1)S(1)}, bf16[256,768]{1,0:T(8,128)(2,1)S(1)}, u32[]{:S(2)}, u32[]{:S(2)}) %collective-permute-start.26) | collective-permute-done | bytes 393248 | tf_op jit(solution)/shard_map/ppermute | solution.py:37
  298.2 8.4 %collective-permute-done.27 = bf16[256,768]{1,0:T(8,128)(2,1)S(1)} collective-permute-done((bf16[256,768]{1,0:T(8,128)(2,1)S(1)}, bf16[256,768]{1,0:T(8,128)(2,1)S(1)}, u32[]{:S(2)}, u32[]{:S(2)}) %collective-permute-start.27) | collective-permute-done | bytes 393248 | tf_op jit(solution)/shard_map/ppermute | solution.py:37
  310.6 2.3 fusion.54
  312.8 2.3 fusion.56
  316.5 6.0 %feed_half_back.6 = (f32[512,768]{1,0:T(8,128)S(1)}, bf16[512,1536]{1,0:T(8,128)(2,1)S(1)}, f32[8,1536]{1,0:T(8,128)S(1)}) custom-call(bf16[512,768]{1,0:T(8,128)(2,1)S(1)} %fusion.6.grad_ref, bf16[1536,768]{1,0:T(8,128)(2,1)S(1)} %copy-done.4, bf16[512,1536]{1,0:T(8,128)(2,1)S(1)} %copy-done.6, bf16[1536,768]{1,0:T(8,128)(2,1)} %get-tuple-element.196.reduce_ref, ...), custom_call_target="tpu_custom_call" | custom-call | flops 2415919104 | bytes 4718592 | tf_op jit(solution)/shard_map/feed_half_back/pallas_call | solution.py:414
  322.5 5.8 %feed_half_back.7 = (f32[512,768]{1,0:T(8,128)S(1)}, bf16[512,1536]{1,0:T(8,128)(2,1)S(1)}, f32[8,1536]{1,0:T(8,128)S(1)}) custom-call(bf16[512,768]{1,0:T(8,128)(2,1)S(1)} %fusion.6.grad_ref, bf16[1536,768]{1,0:T(8,128)(2,1)} %collective-permute-done.18.expand_ref, bf16[512,1536]{1,0:T(8,128)(2,1)S(1)} %copy-done.9, ...), custom_call_target="tpu_custom_call" | custom-call | flops 2415919104 | bytes 4718592 | tf_op jit(solution)/shard_map/feed_half_back/pallas_call | solution.py:414
  339.0 2.2 convolution_convert_fusion.8.go_ref
  341.3 15.0 %attend_back.3 = (bf16[512,768]{1,0:T(8,128)(2,1)S(1)}, f32[2,512,768]{2,1,0:T(8,128)}, bf16[2,512,768]{2,1,0:T(8,128)(2,1)}, f32[8,768]{1,0:T(8,128)S(1)}) custom-call(s32[1]{0:T(128)} %bitcast.1.core_ref, bf16[512,2304]{1,0:T(8,128)(2,1)} %copy-done, bf16[512,2304]{1,0:T(8,128)(2,1)} %copy-done, bf16[512,2304]{1,0:T(8,128)(2,1)} %copy-done, ...), custom_call_target="tpu_custom_call" | custom-call | flops 4026531840 | bytes 15728640 | tf_op jit(solution)/shard_map/attend_back/pallas_call | solution.py:290
  370.0 2.6 copy.34
  376.3 2.7 fusion.1
  390.5 5.4 %collective-permute-done.43 = bf16[192,768]{1,0:T(8,128)(2,1)S(1)} collective-permute-done((bf16[192,768]{1,0:T(8,128)(2,1)S(1)}, bf16[192,768]{1,0:T(8,128)(2,1)S(1)}, u32[]{:S(2)}, u32[]{:S(2)}) %collective-permute-start.43) | collective-permute-done | bytes 294944 | tf_op jit(solution)/shard_map/ppermute | solution.py:33
  397.4 2.5 collective-permute-done.54
  402.3 3.1 collective-permute-done.44
  408.9 15.5 %collective-permute-done.46 = bf16[192,768]{1,0:T(8,128)(2,1)S(1)} collective-permute-done((bf16[192,768]{1,0:T(8,128)(2,1)S(1)}, bf16[192,768]{1,0:T(8,128)(2,1)S(1)}, u32[]{:S(2)}, u32[]{:S(2)}) %collective-permute-start.46) | collective-permute-done | bytes 294944 | tf_op jit(solution)/shard_map/ppermute | solution.py:29
  426.5 5.2 %collective-permute-done.34 = bf16[208,768]{1,0:T(8,128)(2,1)S(1)} collective-permute-done((bf16[208,768]{1,0:T(8,128)(2,1)S(1)}, bf16[208,768]{1,0:T(8,128)(2,1)S(1)}, u32[]{:S(2)}, u32[]{:S(2)}) %collective-permute-start.34) | collective-permute-done | bytes 319520 | tf_op jit(solution)/shard_map/ppermute | solution.py:33
  431.8 3.7 collective-permute-start.29
  435.4 3.7 collective-permute-done.33
  439.2 5.7 %collective-permute-start.30 = (bf16[256,768]{1,0:T(8,128)(2,1)S(1)}, bf16[256,768]{1,0:T(8,128)(2,1)S(1)}, u32[]{:S(2)}, u32[]{:S(2)}) collective-permute-start(bf16[256,768]{1,0:T(8,128)(2,1)S(1)} %get-tuple-element.178), channel_id=1, source_target_pairs={{0,3},{4,2},{1,7},{5,6},{8,11},{12,10},{9,15},{13,14},{2,19},{6,18... | collective-permute-start | bytes 1179656 | tf_op jit(solution)/shard_map/ppermute | solution.py:64
  445.5 6.3 %collective-permute-done.56 = bf16[2,192,768]{2,1,0:T(8,128)(2,1)S(1)} collective-permute-done((bf16[2,192,768]{2,1,0:T(8,128)(2,1)S(1)}, bf16[2,192,768]{2,1,0:T(8,128)(2,1)S(1)}, u32[]{:S(2)}, u32[]{:S(2)}) %collective-permute-start.56) | collective-permute-done | bytes 589856 | tf_op jit(solution)/shard_map/ppermute | solution.py:29
  453.6 19.6 %collective-permute-done.35 = bf16[208,768]{1,0:T(8,128)(2,1)S(1)} collective-permute-done((bf16[208,768]{1,0:T(8,128)(2,1)S(1)}, bf16[208,768]{1,0:T(8,128)(2,1)S(1)}, u32[]{:S(2)}, u32[]{:S(2)}) %collective-permute-start.35) | collective-permute-done | bytes 319520 | tf_op jit(solution)/shard_map/ppermute | solution.py:29
  473.6 8.7 %collective-permute-done.29 = bf16[256,768]{1,0:T(8,128)(2,1)S(1)} collective-permute-done((bf16[256,768]{1,0:T(8,128)(2,1)S(1)}, bf16[256,768]{1,0:T(8,128)(2,1)S(1)}, u32[]{:S(2)}, u32[]{:S(2)}) %collective-permute-start.29) | collective-permute-done | bytes 393248 | tf_op jit(solution)/shard_map/ppermute | solution.py:64
  483.7 8.1 %collective-permute-done.37 = bf16[208,768]{1,0:T(8,128)(2,1)S(1)} collective-permute-done((bf16[208,768]{1,0:T(8,128)(2,1)S(1)}, bf16[208,768]{1,0:T(8,128)(2,1)S(1)}, u32[]{:S(2)}, u32[]{:S(2)}) %collective-permute-start.37) | collective-permute-done | bytes 319520 | tf_op jit(solution)/shard_map/ppermute | solution.py:29
  494.4 5.3 %collective-permute-done.39 = bf16[208,768]{1,0:T(8,128)(2,1)S(1)} collective-permute-done((bf16[208,768]{1,0:T(8,128)(2,1)S(1)}, bf16[208,768]{1,0:T(8,128)(2,1)S(1)}, u32[]{:S(2)}, u32[]{:S(2)}) %collective-permute-start.39) | collective-permute-done | bytes 319520 | tf_op jit(solution)/shard_map/ppermute | solution.py:33
  500.6 2.3 collective-permute-start.40
  (474 shorter events, 159.9 us)
Async XLA Ops:
  0.6 48.9 %collective-permute-start = (bf16[256,768]{1,0:T(8,128)(2,1)}, bf16[256,768]{1,0:T(8,128)(2,1)}, u32[]{:S(2)}, u32[]{:S(2)}) collective-permute-start(bf16[256,768]{1,0:T(8,128)(2,1)} %bitcast.286), channel_id=1, source_target_pairs={{0,0},{1,4},{4,1},{5,5},{8,8},{9,12},{12,9},{13,13},{16,2},{17,6},... | collective-permute-start | bytes 1179656 | tf_op jit(solution)/shard_map/ppermute | solution.py:57
  1.9 48.7 %collective-permute-start.1 = (bf16[256,768]{1,0:T(8,128)(2,1)}, bf16[256,768]{1,0:T(8,128)(2,1)}, u32[]{:S(2)}, u32[]{:S(2)}) collective-permute-start(bf16[256,768]{1,0:T(8,128)(2,1)} %bitcast.287), channel_id=1, source_target_pairs={{3,0},{2,4},{7,1},{6,5},{11,8},{10,12},{15,9},{14,13},{19,2},{18,6... | collective-permute-start | bytes 1179656 | tf_op jit(solution)/shard_map/ppermute | solution.py:57
  10.9 10.6 %collective-permute-start.2 = (bf16[208,768]{1,0:T(8,128)(2,1)}, bf16[208,768]{1,0:T(8,128)(2,1)S(1)}, u32[]{:S(2)}, u32[]{:S(2)}) collective-permute-start(bf16[208,768]{1,0:T(8,128)(2,1)} %pad_maximum_fusion.19), channel_id=1, source_target_pairs={{0,2},{2,3},{3,1},{1,0},{4,6},{6,7},{7,5},{5,4},{8,10},{10,11},{11... | collective-permute-start | bytes 958472 | tf_op jit(solution)/shard_map/ppermute | solution.py:29
  21.5 34.9 %collective-permute-start.3 = (bf16[192,768]{1,0:T(8,128)(2,1)S(1)}, bf16[192,768]{1,0:T(8,128)(2,1)S(1)}, u32[]{:S(2)}, u32[]{:S(2)}) collective-permute-start(bf16[192,768]{1,0:T(8,128)(2,1)S(1)} %slice.457), channel_id=1, source_target_pairs={{0,8},{8,0},{1,9},{9,1},{2,10},{10,2},{3,11},{11,3},{4,12},{12,4},... | collective-permute-start | bytes 884744 | tf_op jit(solution)/shard_map/ppermute | solution.py:33
  22.9 65.8 %collective-permute-start.10 = (bf16[2,192,768]{2,1,0:T(8,128)(2,1)}, bf16[2,192,768]{2,1,0:T(8,128)(2,1)}, u32[]{:S(2)}, u32[]{:S(2)}) collective-permute-start(bf16[2,192,768]{2,1,0:T(8,128)(2,1)} %pad_maximum_fusion.16), channel_id=1, source_target_pairs={{0,2},{2,3},{3,1},{1,0},{4,6},{6,7},{7,5},{5,4},{8,10},{10,11},{11... | collective-permute-start | bytes 1769480 | tf_op jit(solution)/shard_map/ppermute | solution.py:29
  23.0 29.2 %collective-permute-start.4 = (bf16[208,768]{1,0:T(8,128)(2,1)S(1)}, bf16[208,768]{1,0:T(8,128)(2,1)S(1)}, u32[]{:S(2)}, u32[]{:S(2)}) collective-permute-start(bf16[208,768]{1,0:T(8,128)(2,1)S(1)} %collective-permute-done.2), channel_id=1, source_target_pairs={{0,2},{2,3},{3,1},{1,0},{4,6},{6,7},{7,5},{5,4},{8,10},{10,11},{11... | collective-permute-start | bytes 958472 | tf_op jit(solution)/shard_map/ppermute | solution.py:29
  52.2 15.0 %collective-permute-start.5 = (bf16[192,768]{1,0:T(8,128)(2,1)S(1)}, bf16[192,768]{1,0:T(8,128)(2,1)S(1)}, u32[]{:S(2)}, u32[]{:S(2)}) collective-permute-start(bf16[192,768]{1,0:T(8,128)(2,1)S(1)} %slice.458), channel_id=1, source_target_pairs={{0,8},{8,0},{1,9},{9,1},{2,10},{10,2},{3,11},{11,3},{4,12},{12,4},... | collective-permute-start | bytes 884744 | tf_op jit(solution)/shard_map/ppermute | solution.py:33
  56.5 10.4 %collective-permute-start.6 = (bf16[208,768]{1,0:T(8,128)(2,1)S(1)}, bf16[208,768]{1,0:T(8,128)(2,1)S(1)}, u32[]{:S(2)}, u32[]{:S(2)}) collective-permute-start(bf16[208,768]{1,0:T(8,128)(2,1)S(1)} %collective-permute-done.4), channel_id=1, source_target_pairs={{0,2},{2,3},{3,1},{1,0},{4,6},{6,7},{7,5},{5,4},{8,10},{10,11},{11... | collective-permute-start | bytes 958472 | tf_op jit(solution)/shard_map/ppermute | solution.py:29
  88.3 19.1 %collective-permute-start.9 = (bf16[512,1536]{1,0:T(8,128)(2,1)S(1)}, bf16[512,1536]{1,0:T(8,128)(2,1)S(1)}, u32[]{:S(2)}, u32[]{:S(2)}) collective-permute-start(bf16[512,1536]{1,0:T(8,128)(2,1)S(1)} %slice.473), channel_id=1, source_target_pairs={{0,4},{4,0},{1,5},{5,1},{2,6},{6,2},{3,7},{7,3},{8,12},{12,8},{9,1... | collective-permute-start | bytes 4718600 | tf_op jit(solution)/shard_map/ppermute | solution.py:33
  88.7 15.9 %collective-permute-start.11 = (bf16[2,192,768]{2,1,0:T(8,128)(2,1)}, bf16[2,192,768]{2,1,0:T(8,128)(2,1)S(1)}, u32[]{:S(2)}, u32[]{:S(2)}) collective-permute-start(bf16[2,192,768]{2,1,0:T(8,128)(2,1)} %collective-permute-done.10), channel_id=1, source_target_pairs={{0,2},{2,3},{3,1},{1,0},{4,6},{6,7},{7,5},{5,4},{8,10},{10,11},{11... | collective-permute-start | bytes 1769480 | tf_op jit(solution)/shard_map/ppermute | solution.py:29
  89.1 29.9 %collective-permute-start.13 = (bf16[256,768]{1,0:T(8,128)(2,1)S(1)}, bf16[256,768]{1,0:T(8,128)(2,1)S(1)}, u32[]{:S(2)}, u32[]{:S(2)}) collective-permute-start(bf16[256,768]{1,0:T(8,128)(2,1)S(1)} %bitcast.288), channel_id=1, source_target_pairs={{0,16},{1,20},{4,17},{5,21},{8,24},{9,28},{12,25},{13,29},{16,18},... | collective-permute-start | bytes 1179656 | tf_op jit(solution)/shard_map/ppermute | solution.py:57
  89.8 39.9 %collective-permute-start.14 = (bf16[256,768]{1,0:T(8,128)(2,1)S(1)}, bf16[256,768]{1,0:T(8,128)(2,1)S(1)}, u32[]{:S(2)}, u32[]{:S(2)}) collective-permute-start(bf16[256,768]{1,0:T(8,128)(2,1)S(1)} %bitcast.289), channel_id=1, source_target_pairs={{3,16},{2,20},{7,17},{6,21},{11,24},{10,28},{15,25},{14,29},{19,18... | collective-permute-start | bytes 1179656 | tf_op jit(solution)/shard_map/ppermute | solution.py:57
  91.2 41.4 %collective-permute-start.15 = (bf16[2,192,768]{2,1,0:T(8,128)(2,1)}, bf16[2,192,768]{2,1,0:T(8,128)(2,1)S(1)}, u32[]{:S(2)}, u32[]{:S(2)}) collective-permute-start(bf16[2,192,768]{2,1,0:T(8,128)(2,1)} %collective-permute-done.10), channel_id=1, source_target_pairs={{0,8},{8,0},{1,9},{9,1},{2,10},{10,2},{3,11},{11,3},{4,12},{12,4},... | collective-permute-start | bytes 1769480 | tf_op jit(solution)/shard_map/ppermute | solution.py:33
  104.6 25.9 %collective-permute-start.12 = (bf16[2,192,768]{2,1,0:T(8,128)(2,1)S(1)}, bf16[2,192,768]{2,1,0:T(8,128)(2,1)S(1)}, u32[]{:S(2)}, u32[]{:S(2)}) collective-permute-start(bf16[2,192,768]{2,1,0:T(8,128)(2,1)S(1)} %collective-permute-done.11), channel_id=1, source_target_pairs={{0,2},{2,3},{3,1},{1,0},{4,6},{6,7},{7,5},{5,4},{8,10},{10,11},{11... | collective-permute-start | bytes 1769480 | tf_op jit(solution)/shard_map/ppermute | solution.py:29
  107.4 26.0 %collective-permute-start.16 = (bf16[2,192,768]{2,1,0:T(8,128)(2,1)S(1)}, bf16[2,192,768]{2,1,0:T(8,128)(2,1)S(1)}, u32[]{:S(2)}, u32[]{:S(2)}) collective-permute-start(bf16[2,192,768]{2,1,0:T(8,128)(2,1)S(1)} %collective-permute-done.11), channel_id=1, source_target_pairs={{0,8},{8,0},{1,9},{9,1},{2,10},{10,2},{3,11},{11,3},{4,12},{12,4},... | collective-permute-start | bytes 1769480 | tf_op jit(solution)/shard_map/ppermute | solution.py:33
  130.5 14.4 %collective-permute-start.17 = (bf16[2,192,768]{2,1,0:T(8,128)(2,1)S(1)}, bf16[2,192,768]{2,1,0:T(8,128)(2,1)S(1)}, u32[]{:S(2)}, u32[]{:S(2)}) collective-permute-start(bf16[2,192,768]{2,1,0:T(8,128)(2,1)S(1)} %collective-permute-done.12), channel_id=1, source_target_pairs={{0,8},{8,0},{1,9},{9,1},{2,10},{10,2},{3,11},{11,3},{4,12},{12,4},... | collective-permute-start | bytes 1769480 | tf_op jit(solution)/shard_map/ppermute | solution.py:33
  145.7 20.7 %collective-permute-start.18 = (bf16[1536,768]{1,0:T(8,128)(2,1)S(1)}, bf16[1536,768]{1,0:T(8,128)(2,1)}, u32[]{:S(2)}, u32[]{:S(2)}) collective-permute-start(bf16[1536,768]{1,0:T(8,128)(2,1)S(1)} %get-tuple-element.197.expand_ref), channel_id=1, source_target_pairs={{0,4},{4,0},{1,5},{5,1},{2,6},{6,2},{3,7},{7,3},{8,12},{12,8},{9,1... | collective-permute-start | bytes 7077896 | tf_op jit(solution)/shard_map/ppermute | solution.py:33
  147.0 19.4 %collective-permute-start.19 = (bf16[1536,768]{1,0:T(8,128)(2,1)}, bf16[1536,768]{1,0:T(8,128)(2,1)}, u32[]{:S(2)}, u32[]{:S(2)}) collective-permute-start(bf16[1536,768]{1,0:T(8,128)(2,1)} %get-tuple-element.196.reduce_ref), channel_id=1, source_target_pairs={{0,4},{4,0},{1,5},{5,1},{2,6},{6,2},{3,7},{7,3},{8,12},{12,8},{9,1... | collective-permute-start | bytes 7077896 | tf_op jit(solution)/shard_map/ppermute | solution.py:33
  174.1 9.4 %collective-permute-start.20 = (bf16[256,768]{1,0:T(8,128)(2,1)S(1)}, bf16[256,768]{1,0:T(8,128)(2,1)S(1)}, u32[]{:S(2)}, u32[]{:S(2)}) collective-permute-start(bf16[256,768]{1,0:T(8,128)(2,1)S(1)} %get-tuple-element.184), channel_id=1, source_target_pairs={{0,16},{1,17},{2,18},{3,19},{4,20},{5,21},{6,22},{7,23},{8,24},{9,... | collective-permute-start | bytes 1179656 | tf_op jit(solution)/shard_map/ppermute | solution.py:37
  175.6 16.4 %collective-permute-start.21 = (bf16[256,768]{1,0:T(8,128)(2,1)S(1)}, bf16[256,768]{1,0:T(8,128)(2,1)S(1)}, u32[]{:S(2)}, u32[]{:S(2)}) collective-permute-start(bf16[256,768]{1,0:T(8,128)(2,1)S(1)} %get-tuple-element.185), channel_id=1, source_target_pairs={{0,16},{1,17},{2,18},{3,19},{4,20},{5,21},{6,22},{7,23},{8,24},{9,... | collective-permute-start | bytes 1179656 | tf_op jit(solution)/shard_map/ppermute | solution.py:37
  254.6 18.6 %collective-permute-start.23 = (bf16[256,768]{1,0:T(8,128)(2,1)S(1)}, bf16[256,768]{1,0:T(8,128)(2,1)S(1)}, u32[]{:S(2)}, u32[]{:S(2)}) collective-permute-start(bf16[256,768]{1,0:T(8,128)(2,1)S(1)} %get-tuple-element.183), channel_id=1, source_target_pairs={{16,0},{20,1},{17,4},{21,5},{24,8},{28,9},{25,12},{29,13},{18,16},... | collective-permute-start | bytes 1179656 | tf_op jit(solution)/shard_map/ppermute | solution.py:64
  255.4 21.5 %collective-permute-start.24 = (bf16[256,768]{1,0:T(8,128)(2,1)S(1)}, bf16[256,768]{1,0:T(8,128)(2,1)S(1)}, u32[]{:S(2)}, u32[]{:S(2)}) collective-permute-start(bf16[256,768]{1,0:T(8,128)(2,1)S(1)} %get-tuple-element.182), channel_id=1, source_target_pairs={{16,3},{20,2},{17,7},{21,6},{24,11},{28,10},{25,15},{29,14},{18,19... | collective-permute-start | bytes 1179656 | tf_op jit(solution)/shard_map/ppermute | solution.py:64
  285.6 12.6 %collective-permute-start.26 = (bf16[256,768]{1,0:T(8,128)(2,1)S(1)}, bf16[256,768]{1,0:T(8,128)(2,1)S(1)}, u32[]{:S(2)}, u32[]{:S(2)}) collective-permute-start(bf16[256,768]{1,0:T(8,128)(2,1)S(1)} %get-tuple-element.180), channel_id=1, source_target_pairs={{16,0},{17,1},{18,2},{19,3},{20,4},{21,5},{22,6},{23,7},{24,8},{25... | collective-permute-start | bytes 1179656 | tf_op jit(solution)/shard_map/ppermute | solution.py:37
  287.0 19.6 %collective-permute-start.27 = (bf16[256,768]{1,0:T(8,128)(2,1)S(1)}, bf16[256,768]{1,0:T(8,128)(2,1)S(1)}, u32[]{:S(2)}, u32[]{:S(2)}) collective-permute-start(bf16[256,768]{1,0:T(8,128)(2,1)S(1)} %get-tuple-element.181), channel_id=1, source_target_pairs={{16,0},{17,1},{18,2},{19,3},{20,4},{21,5},{22,6},{23,7},{24,8},{25... | collective-permute-start | bytes 1179656 | tf_op jit(solution)/shard_map/ppermute | solution.py:37
  357.4 24.9 %collective-permute-start.52 = (bf16[768,768]{1,0:T(8,128)(2,1)}, bf16[768,768]{1,0:T(8,128)(2,1)}, u32[]{:S(2)}, u32[]{:S(2)}) collective-permute-start(bf16[768,768]{1,0:T(8,128)(2,1)} %convolution_convert_fusion.7), channel_id=1, source_target_pairs={{0,4},{4,0},{1,5},{5,1},{2,6},{6,2},{3,7},{7,3},{8,12},{12,8},{9,1... | collective-permute-start | bytes 3538952 | tf_op jit(solution)/shard_map/ppermute | solution.py:33
  357.9 31.0 %collective-permute-start.41 = (bf16[768,768]{1,0:T(8,128)(2,1)}, bf16[768,768]{1,0:T(8,128)(2,1)}, u32[]{:S(2)}, u32[]{:S(2)}) collective-permute-start(bf16[768,768]{1,0:T(8,128)(2,1)} %convolution_convert_fusion.4), channel_id=1, source_target_pairs={{0,4},{4,0},{1,5},{5,1},{2,6},{6,2},{3,7},{7,3},{8,12},{12,8},{9,1... | collective-permute-start | bytes 3538952 | tf_op jit(solution)/shard_map/ppermute | solution.py:33
  358.0 27.1 %collective-permute-start.42 = (bf16[768,768]{1,0:T(8,128)(2,1)}, bf16[768,768]{1,0:T(8,128)(2,1)}, u32[]{:S(2)}, u32[]{:S(2)}) collective-permute-start(bf16[768,768]{1,0:T(8,128)(2,1)} %convolution_convert_fusion.5), channel_id=1, source_target_pairs={{0,4},{4,0},{1,5},{5,1},{2,6},{6,2},{3,7},{7,3},{8,12},{12,8},{9,1... | collective-permute-start | bytes 3538952 | tf_op jit(solution)/shard_map/ppermute | solution.py:33
  379.3 26.8 %collective-permute-start.31 = (bf16[2,4,208,768]{3,2,1,0:T(8,128)(2,1)S(1)}, bf16[2,4,208,768]{3,2,1,0:T(8,128)(2,1)S(1)}, u32[]{:S(2)}, u32[]{:S(2)}) collective-permute-start(bf16[2,4,208,768]{3,2,1,0:T(8,128)(2,1)S(1)} %select_bitcast_fusion), channel_id=1, source_target_pairs={{0,4},{4,0},{1,5},{5,1},{2,6},{6,2},{3,7},{7,3},{8,12},{12,8},{9,1... | collective-permute-start | bytes 7667720 | tf_op jit(solution)/shard_map/ppermute | solution.py:33
  384.0 15.9 %collective-permute-start.54 = (bf16[2,192,768]{2,1,0:T(8,128)(2,1)S(1)}, bf16[2,192,768]{2,1,0:T(8,128)(2,1)S(1)}, u32[]{:S(2)}, u32[]{:S(2)}) collective-permute-start(bf16[2,192,768]{2,1,0:T(8,128)(2,1)S(1)} %fusion.74), channel_id=1, source_target_pairs={{0,2},{2,3},{3,1},{1,0},{4,6},{6,7},{7,5},{5,4},{8,10},{10,11},{11... | collective-permute-start | bytes 1769480 | tf_op jit(solution)/shard_map/ppermute | solution.py:29
  387.7 14.6 %collective-permute-start.45 = (bf16[192,768]{1,0:T(8,128)(2,1)S(1)}, bf16[192,768]{1,0:T(8,128)(2,1)S(1)}, u32[]{:S(2)}, u32[]{:S(2)}) collective-permute-start(bf16[192,768]{1,0:T(8,128)(2,1)S(1)} %get-tuple-element.171), channel_id=1, source_target_pairs={{0,8},{8,0},{1,9},{9,1},{2,10},{10,2},{3,11},{11,3},{4,12},{12,4},... | collective-permute-start | bytes 884744 | tf_op jit(solution)/shard_map/ppermute | solution.py:33
  396.0 9.4 %collective-permute-start.44 = (bf16[192,768]{1,0:T(8,128)(2,1)S(1)}, bf16[192,768]{1,0:T(8,128)(2,1)S(1)}, u32[]{:S(2)}, u32[]{:S(2)}) collective-permute-start(bf16[192,768]{1,0:T(8,128)(2,1)S(1)} %add_convert_fusion.21), channel_id=1, source_target_pairs={{0,2},{2,3},{3,1},{1,0},{4,6},{6,7},{7,5},{5,4},{8,10},{10,11},{11... | collective-permute-start | bytes 884744 | tf_op jit(solution)/shard_map/ppermute | solution.py:29
  397.1 11.8 %collective-permute-start.47 = (bf16[192,768]{1,0:T(8,128)(2,1)S(1)}, bf16[192,768]{1,0:T(8,128)(2,1)S(1)}, u32[]{:S(2)}, u32[]{:S(2)}) collective-permute-start(bf16[192,768]{1,0:T(8,128)(2,1)S(1)} %get-tuple-element.170), channel_id=1, source_target_pairs={{0,8},{8,0},{1,9},{9,1},{2,10},{10,2},{3,11},{11,3},{4,12},{12,4},... | collective-permute-start | bytes 884744 | tf_op jit(solution)/shard_map/ppermute | solution.py:33
  400.0 26.2 %collective-permute-start.55 = (bf16[2,192,768]{2,1,0:T(8,128)(2,1)S(1)}, bf16[2,192,768]{2,1,0:T(8,128)(2,1)S(1)}, u32[]{:S(2)}, u32[]{:S(2)}) collective-permute-start(bf16[2,192,768]{2,1,0:T(8,128)(2,1)S(1)} %fusion.42), channel_id=1, source_target_pairs={{0,2},{2,3},{3,1},{1,0},{4,6},{6,7},{7,5},{5,4},{8,10},{10,11},{11... | collective-permute-start | bytes 1769480 | tf_op jit(solution)/shard_map/ppermute | solution.py:29
  405.5 18.8 %collective-permute-start.46 = (bf16[192,768]{1,0:T(8,128)(2,1)S(1)}, bf16[192,768]{1,0:T(8,128)(2,1)S(1)}, u32[]{:S(2)}, u32[]{:S(2)}) collective-permute-start(bf16[192,768]{1,0:T(8,128)(2,1)S(1)} %add_convert_fusion.19), channel_id=1, source_target_pairs={{0,2},{2,3},{3,1},{1,0},{4,6},{6,7},{7,5},{5,4},{8,10},{10,11},{11... | collective-permute-start | bytes 884744 | tf_op jit(solution)/shard_map/ppermute | solution.py:29
  407.4 17.6 %collective-permute-start.32 = (bf16[208,768]{1,0:T(8,128)(2,1)S(1)}, bf16[208,768]{1,0:T(8,128)(2,1)S(1)}, u32[]{:S(2)}, u32[]{:S(2)}) collective-permute-start(bf16[208,768]{1,0:T(8,128)(2,1)S(1)} %get-tuple-element.158), channel_id=1, source_target_pairs={{0,8},{8,0},{1,9},{9,1},{2,10},{10,2},{3,11},{11,3},{4,12},{12,4},... | collective-permute-start | bytes 958472 | tf_op jit(solution)/shard_map/ppermute | solution.py:33
  407.7 37.4 %collective-permute-start.49 = (bf16[192,768]{1,0:T(8,128)(2,1)S(1)}, bf16[192,768]{1,0:T(8,128)(2,1)S(1)}, u32[]{:S(2)}, u32[]{:S(2)}) collective-permute-start(bf16[192,768]{1,0:T(8,128)(2,1)S(1)} %get-tuple-element.169), channel_id=1, source_target_pairs={{0,8},{8,0},{1,9},{9,1},{2,10},{10,2},{3,11},{11,3},{4,12},{12,4},... | collective-permute-start | bytes 884744 | tf_op jit(solution)/shard_map/ppermute | solution.py:33
  424.5 20.9 %collective-permute-start.48 = (bf16[192,768]{1,0:T(8,128)(2,1)S(1)}, bf16[192,768]{1,0:T(8,128)(2,1)S(1)}, u32[]{:S(2)}, u32[]{:S(2)}) collective-permute-start(bf16[192,768]{1,0:T(8,128)(2,1)S(1)} %add_convert_fusion.17), channel_id=1, source_target_pairs={{0,2},{2,3},{3,1},{1,0},{4,6},{6,7},{7,5},{5,4},{8,10},{10,11},{11... | collective-permute-start | bytes 884744 | tf_op jit(solution)/shard_map/ppermute | solution.py:29
  425.0 14.1 %collective-permute-start.33 = (bf16[208,768]{1,0:T(8,128)(2,1)S(1)}, bf16[208,768]{1,0:T(8,128)(2,1)S(1)}, u32[]{:S(2)}, u32[]{:S(2)}) collective-permute-start(bf16[208,768]{1,0:T(8,128)(2,1)S(1)} %fusion.70), channel_id=1, source_target_pairs={{0,2},{2,3},{3,1},{1,0},{4,6},{6,7},{7,5},{5,4},{8,10},{10,11},{11... | collective-permute-start | bytes 958472 | tf_op jit(solution)/shard_map/ppermute | solution.py:29
  426.4 25.5 %collective-permute-start.56 = (bf16[2,192,768]{2,1,0:T(8,128)(2,1)S(1)}, bf16[2,192,768]{2,1,0:T(8,128)(2,1)S(1)}, u32[]{:S(2)}, u32[]{:S(2)}) collective-permute-start(bf16[2,192,768]{2,1,0:T(8,128)(2,1)S(1)} %fusion.41), channel_id=1, source_target_pairs={{0,2},{2,3},{3,1},{1,0},{4,6},{6,7},{7,5},{5,4},{8,10},{10,11},{11... | collective-permute-start | bytes 1769480 | tf_op jit(solution)/shard_map/ppermute | solution.py:29
  431.8 50.5 %collective-permute-start.29 = (bf16[256,768]{1,0:T(8,128)(2,1)S(1)}, bf16[256,768]{1,0:T(8,128)(2,1)S(1)}, u32[]{:S(2)}, u32[]{:S(2)}) collective-permute-start(bf16[256,768]{1,0:T(8,128)(2,1)S(1)} %get-tuple-element.179), channel_id=1, source_target_pairs={{0,0},{4,1},{1,4},{5,5},{8,8},{12,9},{9,12},{13,13},{2,16},{6,17},... | collective-permute-start | bytes 1179656 | tf_op jit(solution)/shard_map/ppermute | solution.py:64
  439.2 43.1 %collective-permute-start.30 = (bf16[256,768]{1,0:T(8,128)(2,1)S(1)}, bf16[256,768]{1,0:T(8,128)(2,1)S(1)}, u32[]{:S(2)}, u32[]{:S(2)}) collective-permute-start(bf16[256,768]{1,0:T(8,128)(2,1)S(1)} %get-tuple-element.178), channel_id=1, source_target_pairs={{0,3},{4,2},{1,7},{5,6},{8,11},{12,10},{9,15},{13,14},{2,19},{6,18... | collective-permute-start | bytes 1179656 | tf_op jit(solution)/shard_map/ppermute | solution.py:64
  445.4 27.8 %collective-permute-start.35 = (bf16[208,768]{1,0:T(8,128)(2,1)S(1)}, bf16[208,768]{1,0:T(8,128)(2,1)S(1)}, u32[]{:S(2)}, u32[]{:S(2)}) collective-permute-start(bf16[208,768]{1,0:T(8,128)(2,1)S(1)} %add_convert_fusion.12), channel_id=1, source_target_pairs={{0,2},{2,3},{3,1},{1,0},{4,6},{6,7},{7,5},{5,4},{8,10},{10,11},{11... | collective-permute-start | bytes 958472 | tf_op jit(solution)/shard_map/ppermute | solution.py:29
  451.8 31.2 %collective-permute-start.50 = (bf16[192,768]{1,0:T(8,128)(2,1)S(1)}, bf16[192,768]{1,0:T(8,128)(2,1)S(1)}, u32[]{:S(2)}, u32[]{:S(2)}) collective-permute-start(bf16[192,768]{1,0:T(8,128)(2,1)S(1)} %add_convert_fusion.15), channel_id=1, source_target_pairs={{0,8},{8,0},{1,9},{9,1},{2,10},{10,2},{3,11},{11,3},{4,12},{12,4},... | collective-permute-start | bytes 884744 | tf_op jit(solution)/shard_map/ppermute | solution.py:33
  453.3 38.7 %collective-permute-start.57 = (bf16[2,192,768]{2,1,0:T(8,128)(2,1)S(1)}, bf16[2,192,768]{2,1,0:T(8,128)(2,1)S(1)}, u32[]{:S(2)}, u32[]{:S(2)}) collective-permute-start(bf16[2,192,768]{2,1,0:T(8,128)(2,1)S(1)} %fusion.40), channel_id=1, source_target_pairs={{0,8},{8,0},{1,9},{9,1},{2,10},{10,2},{3,11},{11,3},{4,12},{12,4},... | collective-permute-start | bytes 1769480 | tf_op jit(solution)/shard_map/ppermute | solution.py:33
  473.2 10.5 %collective-permute-start.38 = (bf16[208,768]{1,0:T(8,128)(2,1)S(1)}, bf16[208,768]{1,0:T(8,128)(2,1)S(1)}, u32[]{:S(2)}, u32[]{:S(2)}) collective-permute-start(bf16[208,768]{1,0:T(8,128)(2,1)S(1)} %get-tuple-element.155), channel_id=1, source_target_pairs={{0,8},{8,0},{1,9},{9,1},{2,10},{10,2},{3,11},{11,3},{4,12},{12,4},... | collective-permute-start | bytes 958472 | tf_op jit(solution)/shard_map/ppermute | solution.py:33
  482.3 9.5 %collective-permute-start.37 = (bf16[208,768]{1,0:T(8,128)(2,1)S(1)}, bf16[208,768]{1,0:T(8,128)(2,1)S(1)}, u32[]{:S(2)}, u32[]{:S(2)}) collective-permute-start(bf16[208,768]{1,0:T(8,128)(2,1)S(1)} %add_convert_fusion.11), channel_id=1, source_target_pairs={{0,2},{2,3},{3,1},{1,0},{4,6},{6,7},{7,5},{5,4},{8,10},{10,11},{11... | collective-permute-start | bytes 958472 | tf_op jit(solution)/shard_map/ppermute | solution.py:29
  483.1 19.8 %collective-permute-start.51 = (bf16[384,768]{1,0:T(8,128)(2,1)S(1)}, bf16[384,768]{1,0:T(8,128)(2,1)S(1)}, u32[]{:S(2)}, u32[]{:S(2)}) collective-permute-start(bf16[384,768]{1,0:T(8,128)(2,1)S(1)} %pad_maximum_fusion.17), channel_id=1, source_target_pairs={{0,4},{4,0},{1,5},{5,1},{2,6},{6,2},{3,7},{7,3},{8,12},{12,8},{9,1... | collective-permute-start | bytes 1769480 | tf_op jit(solution)/shard_map/ppermute | solution.py:33
  493.1 12.0 %collective-permute-start.58 = (bf16[384,768]{1,0:T(8,128)(2,1)}, bf16[384,768]{1,0:T(8,128)(2,1)}, u32[]{:S(2)}, u32[]{:S(2)}) collective-permute-start(bf16[384,768]{1,0:T(8,128)(2,1)} %pad_maximum_fusion.18), channel_id=1, source_target_pairs={{0,4},{4,0},{1,5},{5,1},{2,6},{6,2},{3,7},{7,3},{8,12},{12,8},{9,1... | collective-permute-start | bytes 1769480 | tf_op jit(solution)/shard_map/ppermute | solution.py:33
  (98 other events, 660.7 us)

commit v2 on v1

v2 whole, which is shorter than its diff:
```python
import functools

import jax
import jax.numpy as jnp
import numpy as np
from jax import lax
from jax.experimental import pallas as pl
from jax.experimental.pallas import tpu as pltpu
from jax.sharding import Mesh
from jax.sharding import PartitionSpec as P

HEAD = 64
DEPTH = 12
BRANCH = DEPTH ** (-0.5)
EPSILON = 1e-05
NEGATIVE = -1e30
LANES = 128
AXES = ("pipe", "y", "core", "tensor")
F32 = jnp.float32
BF16 = jnp.bfloat16


def ring_order(count):
    return list(range(0, count, 2)) + list(range(1, count, 2))[::-1]


def ring(value):
    order = ring_order(lax.axis_size("tensor"))
    return lax.ppermute(value, "tensor", list(zip(order, order[1:] + order[:1])))


def swap(value, axis):
    return lax.ppermute(value, axis, [(0, 1), (1, 0)])


def along_pipe(value, by):
    return lax.ppermute(value, "pipe", [(0, 1)] if by > 0 else [(1, 0)])


def routes(section, large):
    count = lax.axis_size("tensor")

    def index(x, y, c, z):
        return ((x * 2 + y) * 2 + c) * count + z

    pairs = []
    for micro in range(2):
        for y in range(2):
            for c in range(2):
                for core in range(2):
                    block = 3 - core if large else core
                    pairs.append((index(micro, y, c, block), index(section, y, core, 2 * micro + c)))
    return pairs


def fetch(block, section):
    return [lax.ppermute(block, AXES, routes(section, large)) for large in (False, True)]


def give_back(small, large, section):
    pieces = []
    for rows, is_large in ((small, False), (large, True)):
        pairs = [(b, a) for a, b in routes(section, is_large)]
        pieces.append(lax.ppermute(rows, AXES, pairs))
    return jnp.where(lax.axis_index("tensor") < 2, pieces[0], pieces[1])


def nt(left, right):
    return lax.dot_general(left, right, (((1,), (1,)), ((), ())), preferred_element_type=F32)


def tn(left, right):
    return lax.dot_general(left, right, (((0,), (0,)), ((), ())), preferred_element_type=F32)


def tk(left, right):
    turned = right.astype(F32).T.astype(BF16)
    return nn(turned, left).T


def nn(left, right):
    return lax.dot_general(left, right, (((1,), (0,)), ((), ())), preferred_element_type=F32)


def head_mask(rows, head):
    lanes = lax.broadcasted_iota(jnp.int32, (rows, LANES), 1)
    return (lanes >= head * HEAD) & (lanes < (head + 1) * HEAD)


def only(mask, value, factor=1.0):
    return jnp.where(mask, value.astype(F32) * factor, 0.0).astype(BF16)


def attend_kernel(keep_weights, core_ref, q_ref, k_ref, v_ref, ko_ref, vo_ref, o_ref, *p_refs):
    rows = q_ref.shape[0] // 2
    second = core_ref[0] == 1
    keys = lax.broadcasted_iota(jnp.int32, (rows, rows), 0)
    places = lax.broadcasted_iota(jnp.int32, (rows, rows), 1)
    allowed = keys <= places
    factor = HEAD ** (-0.5)
    small = pl.ds(0, rows)
    large = pl.ds(rows, rows)
    k5 = jnp.where(second, ko_ref[small, :].astype(F32), ko_ref[large, :].astype(F32)).astype(BF16)
    v5 = jnp.where(second, vo_ref[small, :].astype(F32), vo_ref[large, :].astype(F32))
    out_small = None
    out_large = None
    for head in range(LANES // HEAD):
        mask = head_mask(rows, head)

        def query(value):
            return only(mask, value, factor)

        qs, ql = query(q_ref[small, :]), query(q_ref[large, :])
        qf = query(jnp.where(second, q_ref[small, :].astype(F32), q_ref[large, :].astype(F32)))
        s1 = jnp.where(allowed, nt(k_ref[small, :], qs), NEGATIVE)
        s2 = nt(k_ref[small, :], ql)
        s3 = jnp.where(allowed, nt(k_ref[large, :], ql), NEGATIVE)
        s4 = nt(ko_ref[small, :], ql)
        s5 = nt(k5, qf)

        def peak(value):
            return jnp.max(value, axis=0, keepdims=True)

        def total(value):
            return jnp.sum(value, axis=0, keepdims=True)

        m5 = peak(s5)
        ms = peak(s1)
        ml = jnp.maximum(jnp.maximum(peak(s2), peak(s3)), peak(s4))
        ms = jnp.where(second, jnp.maximum(ms, m5), ms)
        ml = jnp.where(second, ml, jnp.maximum(ml, m5))
        mf = jnp.where(second, ms, ml)
        e1 = jnp.exp(s1 - ms)
        e2 = jnp.exp(s2 - ml)
        e3 = jnp.exp(s3 - ml)
        e4 = jnp.exp(s4 - ml)
        e5 = jnp.exp(s5 - mf)
        t5 = total(e5)
        rs = total(e1)
        rl = total(e2) + total(e3) + total(e4)
        rs = 1.0 / jnp.where(second, rs + t5, rs)
        rl = 1.0 / jnp.where(second, rl, rl + t5)
        rf = jnp.where(second, rs, rl)
        p1 = (e1 * rs).astype(BF16)
        p2 = (e2 * rl).astype(BF16)
        p3 = (e3 * rl).astype(BF16)
        p4 = (e4 * rl).astype(BF16)
        p5 = (e5 * rf).astype(BF16)
        if keep_weights:
            for place, value in enumerate((p1, p2, p3, p4, p5)):
                p_refs[0][head, place] = value
        vs = only(mask, v_ref[small, :])
        o5 = tk(p5, only(mask, v5))
        os = tk(p1, vs) + jnp.where(second, o5, 0.0)
        ol = (
            tk(p2, vs)
            + tk(p3, only(mask, v_ref[large, :]))
            + tk(p4, only(mask, vo_ref[small, :]))
            + jnp.where(second, 0.0, o5)
        )
        out_small = os if out_small is None else out_small + os
        out_large = ol if out_large is None else out_large + ol
    o_ref[small, :] = out_small.astype(BF16)
    o_ref[large, :] = out_large.astype(BF16)


def attend_back_kernel(
    core_ref, q_ref, k_ref, v_ref, ko_ref, vo_ref, go_ref, o_ref, p_ref, gq_ref, own_ref, other_ref, sums_ref
):
    rows = q_ref.shape[0] // 2
    second = core_ref[0] == 1
    factor = HEAD ** (-0.5)
    small = pl.ds(0, rows)
    large = pl.ds(rows, rows)

    def fifth(ref, first, last):
        return jnp.where(second, ref[first, :].astype(F32), ref[last, :].astype(F32))

    k5 = fifth(ko_ref, small, large)
    v5 = fifth(vo_ref, small, large).astype(BF16)
    q5 = fifth(q_ref, small, large)
    g5 = fifth(go_ref, small, large)
    product = go_ref[...].astype(F32) * o_ref[...].astype(F32)
    high = product.astype(BF16)
    low = (product - high.astype(F32)).astype(BF16)
    totals = {}

    def add(name, value):
        totals[name] = value if name not in totals else totals[name] + value

    for head in range(LANES // HEAD):
        mask = head_mask(rows, head)
        ones = jnp.where(head_mask(16, head), 1.0, 0.0).astype(BF16)
        inner = (nt(ones, high) + nt(ones, low))[0:1]
        ds_, dl_ = inner[:, :rows], inner[:, rows:]
        df_ = jnp.where(second, ds_, dl_)

        def weight(place):
            return p_ref[head, place]

        qs, ql, qf = (only(mask, value, factor) for value in (q_ref[small, :], q_ref[large, :], q5))
        gs, gl, gf = (only(mask, value) for value in (go_ref[small, :], go_ref[large, :], g5))

        def score_grad(place, values, rows_grad, shift):
            return (weight(place).astype(F32) * (nt(values, rows_grad) - shift)).astype(BF16)

        z1 = score_grad(0, v_ref[small, :], gs, ds_)
        z2 = score_grad(1, v_ref[small, :], gl, dl_)
        z3 = score_grad(2, v_ref[large, :], gl, dl_)
        z4 = score_grad(3, vo_ref[small, :], gl, dl_)
        z5 = score_grad(4, v5, gf, df_)
        k_small = only(mask, k_ref[small, :])
        gq5 = tk(z5, only(mask, k5))
        add("qs", tk(z1, k_small) + jnp.where(second, gq5, 0.0))
        add(
            "ql",
            tk(z2, k_small)
            + tk(z3, only(mask, k_ref[large, :]))
            + tk(z4, only(mask, ko_ref[small, :]))
            + jnp.where(second, 0.0, gq5),
        )
        add("ks", nn(z1, qs) + nn(z2, ql))
        add("kl", nn(z3, ql))
        add("k4", nn(z4, ql))
        add("k5", nn(z5, qf))
        add("vs", nn(weight(0), gs) + nn(weight(1), gl))
        add("vl", nn(weight(2), gl))
        add("v4", nn(weight(3), gl))
        add("v5", nn(weight(4), gf))
    gqs, gql = totals["qs"] * factor, totals["ql"] * factor
    gq_ref[small, :] = gqs.astype(BF16)
    gq_ref[large, :] = gql.astype(BF16)
    for place, name in enumerate("kv"):
        own_ref[place, small, :] = totals[name + "s"]
        own_ref[place, large, :] = totals[name + "l"]
        four, five = totals[name + "4"], totals[name + "5"]
        other_ref[place, small, :] = (four + jnp.where(second, five, 0.0)).astype(BF16)
        other_ref[place, large, :] = jnp.where(second, 0.0, five).astype(BF16)
    sum_q = jnp.sum(gqs, axis=0, keepdims=True) + jnp.sum(gql, axis=0, keepdims=True)
    sum_v = jnp.sum(totals["vs"] + totals["vl"] + totals["v4"] + totals["v5"], axis=0, keepdims=True)
    row = lax.broadcasted_iota(jnp.int32, (8, LANES), 0)
    sums_ref[...] = jnp.where(row == 0, sum_q, jnp.where(row == 1, sum_v, 0.0))


def attend(core, q, k, v, k_other, v_other, keep_weights):
    length, width = q.shape
    rows = length // 2
    column = pl.BlockSpec((length, LANES), lambda i: (0, i))
    shapes = [jax.ShapeDtypeStruct((length, width), BF16)]
    outs = [column]
    if keep_weights:
        shapes.append(pltpu.HBM((width // HEAD, 5, rows, rows), BF16))
        outs.append(pl.BlockSpec((2, 5, rows, rows), lambda i: (i, 0, 0, 0)))
    return pl.pallas_call(
        functools.partial(attend_kernel, keep_weights),
        grid=(width // LANES,),
        out_shape=shapes,
        in_specs=[pl.BlockSpec(memory_space=pltpu.SMEM)] + [column] * 5,
        out_specs=outs,
        compiler_params=pltpu.CompilerParams(vmem_limit_bytes=40 * 1024 * 1024),
        cost_estimate=pl.CostEstimate(
            flops=20 * rows * rows * width * 2, bytes_accessed=16 * length * width, transcendentals=0
        ),
        name="attend",
    )(core, q, k, v, k_other, v_other)


def attend_back(core, q, k, v, k_other, v_other, grad_mixed, mixed, weights):
    length, width = q.shape
    rows = length // 2
    column = pl.BlockSpec((length, LANES), lambda i: (0, i))
    double = pl.BlockSpec((2, length, LANES), lambda i: (0, 0, i))
    return pl.pallas_call(
        attend_back_kernel,
        grid=(width // LANES,),
        out_shape=[
            jax.ShapeDtypeStruct((length, width), BF16),
            jax.ShapeDtypeStruct((2, length, width), F32),
            jax.ShapeDtypeStruct((2, length, width), BF16),
            jax.ShapeDtypeStruct((8, width), F32),
        ],
        in_specs=[pl.BlockSpec(memory_space=pltpu.SMEM)]
        + [column] * 7
        + [pl.BlockSpec((2, 5, rows, rows), lambda i: (i, 0, 0, 0))],
        out_specs=[column, double, double, pl.BlockSpec((8, LANES), lambda i: (0, i))],
        compiler_params=pltpu.CompilerParams(vmem_limit_bytes=40 * 1024 * 1024),
        cost_estimate=pl.CostEstimate(
            flops=40 * rows * rows * width * 2, bytes_accessed=40 * length * width, transcendentals=0
        ),
        name="attend_back",
    )(core, q, k, v, k_other, v_other, grad_mixed, mixed, weights)


def gelu_and_slope(values):
    root = float(np.sqrt(2 / np.pi))
    cubic = 0.044715 * root
    square = values * values
    bend = jnp.tanh(values * (root + cubic * square))
    half = 0.5 + 0.5 * bend
    gate = values * half
    slope = half + gate * ((1.0 - bend) * (root + (3 * cubic) * square))
    return (gate, slope)


def tiles_of(units):
    return units // 512 if units % 512 == 0 else 1


def expand_kernel(rows_ref, expand_ref, bias_ref, reduce_ref, start_ref, total_ref):
    units = expand_ref.shape[0]
    piece = 256 if units % 256 == 0 else units
    rows = rows_ref[...]
    total = None
    for offset in range(0, units, piece):
        part = pl.ds(offset, piece)
        gate, _ = gelu_and_slope(nt(rows, expand_ref[part, :]) + bias_ref[:, part])
        term = nn(gate.astype(BF16), reduce_ref[part, :])
        total = term if total is None else total + term

    @pl.when(pl.program_id(0) == 0)
    def _():
        total_ref[...] = start_ref[...] + total

    @pl.when(pl.program_id(0) > 0)
    def _():
        total_ref[...] += total


def feed_half(rows, expand_w, bias, reduce_w, start, row_part=None):
    length, width = rows.shape
    units = expand_w.shape[0]
    steps = tiles_of(units)
    tile = units // steps
    if row_part is not None:
        length = length // 2
    place = row_part or 0
    whole = pl.BlockSpec((length, width), lambda i: (0, 0))
    taken = pl.BlockSpec((length, width), lambda i: (place, 0))
    weight = pl.BlockSpec((tile, width), lambda i: (i, 0))
    return pl.pallas_call(
        expand_kernel,
        grid=(steps,),
        out_shape=jax.ShapeDtypeStruct((length, width), F32),
        in_specs=[taken, weight, pl.BlockSpec((1, tile), lambda i: (0, i)), weight, taken],
        out_specs=whole,
        compiler_params=pltpu.CompilerParams(vmem_limit_bytes=40 * 1024 * 1024),
        cost_estimate=pl.CostEstimate(
            flops=4 * length * width * units, bytes_accessed=4 * width * units, transcendentals=0
        ),
        name="feed_half",
    )(rows, expand_w, bias.reshape(1, units), reduce_w, start)


def both_kernel(
    steps, rows_ref, grad_ref, e0_ref, e1_ref, b0_ref, b1_ref, r0_ref, r1_ref,
    total_ref, grad_total_ref, h0_ref, h1_ref, s0_ref, s1_ref,
):
    place = pl.program_id(0)

    @pl.when(place == 0)
    def _():
        total_ref[...] = jnp.zeros_like(total_ref)
        grad_total_ref[...] = jnp.zeros_like(grad_total_ref)

    def tile(expand_ref, bias_ref, reduce_ref, hidden_ref, slope_ref):
        gate, slope = gelu_and_slope(nt(rows_ref[...], expand_ref[...]) + bias_ref[...])
        hidden = gate.astype(BF16)
        slope = slope.astype(BF16)
        hidden_ref[...] = hidden
        slope_ref[...] = slope
        total_ref[...] += nn(hidden, reduce_ref[...])
        pre = nt(grad_ref[...], reduce_ref[...]) * slope.astype(F32)
        grad_total_ref[...] += nn(pre.astype(BF16), expand_ref[...])

    @pl.when(place < steps)
    def _():
        tile(e0_ref, b0_ref, r0_ref, h0_ref, s0_ref)

    @pl.when(place >= steps)
    def _():
        tile(e1_ref, b1_ref, r1_ref, h1_ref, s1_ref)


def back_kernel(
    steps, grad_ref, e0_ref, e1_ref, r0_ref, r1_ref, s0_ref, s1_ref,
    total_ref, p0_ref, p1_ref, sums0_ref, sums1_ref,
):
    place = pl.program_id(0)

    @pl.when(place == 0)
    def _():
        total_ref[...] = jnp.zeros_like(total_ref)

    def tile(expand_ref, reduce_ref, slope_ref, pre_ref, sums_ref):
        pre = nt(grad_ref[...], reduce_ref[...]) * slope_ref[...].astype(F32)
        sums_ref[...] = jnp.broadcast_to(jnp.sum(pre, axis=0, keepdims=True), sums_ref.shape)
        rounded = pre.astype(BF16)
        pre_ref[...] = rounded
        total_ref[...] += nn(rounded, expand_ref[...])

    @pl.when(place < steps)
    def _():
        tile(e0_ref, r0_ref, s0_ref, p0_ref, sums0_ref)

    @pl.when(place >= steps)
    def _():
        tile(e1_ref, r1_ref, s1_ref, p1_ref, sums1_ref)


def feed_specs(length, width, units):
    steps = tiles_of(units)
    tile = units // steps
    whole = pl.BlockSpec((length, width), lambda i: (0, 0))

    def early(i):
        return jnp.minimum(i, steps - 1)

    def late(i):
        return jnp.maximum(i - steps, 0)

    weight = [pl.BlockSpec((tile, width), lambda i, f=f: (f(i), 0)) for f in (early, late)]
    across = [pl.BlockSpec((length, tile), lambda i, f=f: (0, f(i))) for f in (early, late)]
    row = [pl.BlockSpec((1, tile), lambda i, f=f: (0, f(i))) for f in (early, late)]
    rows = [pl.BlockSpec((8, tile), lambda i, f=f: (0, f(i))) for f in (early, late)]
    return steps, whole, weight, across, row, rows


def feed_both(rows, grad, halves):
    length, width = rows.shape
    units = halves[0][0].shape[0]
    steps, whole, weight, across, row, _ = feed_specs(length, width, units)
    total = jax.ShapeDtypeStruct((length, width), F32)
    kept = jax.ShapeDtypeStruct((length, units), BF16)
    (e0, b0, r0), (e1, b1, r1) = halves
    return pl.pallas_call(
        functools.partial(both_kernel, steps),
        grid=(2 * steps,),
        out_shape=[total, total, kept, kept, kept, kept],
        in_specs=[whole, whole, *weight, *row, *weight],
        out_specs=[whole, whole, *across, *across],
        compiler_params=pltpu.CompilerParams(vmem_limit_bytes=40 * 1024 * 1024),
        cost_estimate=pl.CostEstimate(
            flops=16 * length * width * units, bytes_accessed=8 * width * units, transcendentals=0
        ),
        name="feed_both",
    )(rows, grad, e0, e1, b0.reshape(1, units), b1.reshape(1, units), r0, r1)


def feed_back(grad, halves, slope):
    length, width = grad.shape
    units = halves[0][0].shape[0]
    steps, whole, weight, across, _, rows = feed_specs(length, width, units)
    kept = jax.ShapeDtypeStruct((length, units), BF16)
    sums = jax.ShapeDtypeStruct((8, units), F32)
    (e0, _, r0), (e1, _, r1) = halves
    return pl.pallas_call(
        functools.partial(back_kernel, steps),
        grid=(2 * steps,),
        out_shape=[jax.ShapeDtypeStruct((length, width), F32), kept, kept, sums, sums],
        in_specs=[whole, *weight, *weight, *across],
        out_specs=[whole, *across, *rows],
        compiler_params=pltpu.CompilerParams(vmem_limit_bytes=40 * 1024 * 1024),
        cost_estimate=pl.CostEstimate(
            flops=8 * length * width * units, bytes_accessed=8 * width * units, transcendentals=0
        ),
        name="feed_back",
    )(grad, e0, e1, r0, r1, *slope)


def tie(value, *others):
    return lax.optimization_barrier((value, *others))[0]


def normalize_rows(rows):
    centred = rows - jnp.mean(rows, axis=-1, keepdims=True)
    inverse = lax.rsqrt(jnp.mean(centred * centred, axis=-1, keepdims=True) + EPSILON)
    return (centred * inverse, inverse)


def norm_backward(grad_normed, normed, inverse, gain):
    scaled = grad_normed * gain
    centred = scaled - jnp.mean(scaled, axis=-1, keepdims=True)
    return inverse * (centred - normed * jnp.mean(scaled * normed, axis=-1, keepdims=True))


def attention_forward(core, rows_in, weights, keep, before=(), after=()):
    gain_a, shift_a, proj, bias_q, bias_v, bias_out = weights
    normed_one, inverse_one = normalize_rows(rows_in)
    ready_one = narrow(normed_one * gain_a + shift_a)
    k = narrow(nt(ready_one, proj[1]))
    k_other = swap(k, "core")
    v = narrow(nt(ready_one, proj[2]) + bias_v)
    v_other = swap(v, "core")
    q = narrow(nt(ready_one, proj[0]) + bias_q)
    if before:
        q, *before = lax.optimization_barrier((q, *before))
        after = [*after[:-2], *after[-1](before)]
    mixed, *kept_weights = attend(core, q, k, v, k_other, v_other, keep)
    mixed, *after = lax.optimization_barrier((mixed, *after))
    middle = rows_in + BRANCH * (nn(mixed, proj[3]) + bias_out)
    kept = (normed_one, inverse_one, ready_one, (q, k, v, k_other, v_other), mixed, *kept_weights)
    return middle, kept, after


def feed_start(middle, weights):
    gain_b, shift_b, _, _ = weights
    normed_two, inverse_two = normalize_rows(middle)
    return normed_two, inverse_two, narrow(normed_two * gain_b + shift_b)


def feed_forward_only(middle, weights):
    ready_two = feed_start(middle, weights)[2]
    first, second = weights[2]
    total = feed_half(ready_two, *first, jnp.broadcast_to(weights[3], middle.shape))
    block = middle.shape[0] // 2
    results = []
    for part in range(2):
        rows = slice(part * block, (part + 1) * block)
        piece = feed_half(ready_two, *second, tie(total, *results), part)
        results.append(narrow(middle[rows] + BRANCH * piece))
    return results


def feed_forward_and_back(middle, grad_result, weights):
    normed_two, inverse_two, ready_two = feed_start(middle, weights)
    rounded = narrow(BRANCH * grad_result)
    total, grad_total, *kept = feed_both(ready_two, rounded, weights[2])
    result = narrow(middle + BRANCH * (total + weights[3]))
    grad_middle = grad_result + norm_backward(grad_total, normed_two, inverse_two, weights[0])
    return result, grad_middle, (normed_two, inverse_two, ready_two, kept[:2], kept[2:])


def attention_backward(core, kept, grad_middle, weights, before=(), after=()):
    gain_a, _, proj, _, _, _ = weights
    normed_one, inverse_one, ready_one, projected, mixed, attention = kept
    grad_attended = BRANCH * grad_middle
    rounded_attended = narrow(grad_attended)
    grad_mixed = narrow(nt(tie(rounded_attended, *before), proj[3]))
    grad_q, own, other, sums = attend_back(core, *projected, grad_mixed, mixed, attention)
    other, *after = lax.optimization_barrier((other, *after))
    grad_kv = narrow(own + swap(other, "core").astype(F32))
    grad_normed_one = nn(grad_q, proj[0]) + nn(grad_kv[0], proj[1]) + nn(grad_kv[1], proj[2])
    grad_in = grad_middle + norm_backward(grad_normed_one, normed_one, inverse_one, gain_a)
    shared = [grad_normed_one * normed_one, grad_normed_one, grad_attended]
    return grad_in, rounded_attended, (grad_q, grad_kv[0], grad_kv[1]), sums[:2], shared, after


def narrow(value):
    return value.astype(BF16)


def wide_add(left, right):
    return narrow(left.astype(F32) + right.astype(F32))


def over_groups(value):
    return lax.psum(value, "outer") if lax.axis_size("outer") > 1 else value


def ring_add(parts):
    count = len(parts)
    total = parts[1 % count]
    for step in range(1, count):
        total = wide_add(ring(total), parts[(step + 1) % count])
    return total


def thirds(values):
    pieces = []
    for _ in range(3):
        piece = lax.reduce_precision(values, 8, 7)
        pieces.append(narrow(piece))
        values = values - piece
    return jnp.stack(pieces)


def shards(
    inputs, cotangent, gain_one, shift_one, attend_in, attend_bias, attend_out, out_bias,
    gain_two, shift_two, expand_in, expand_bias, reduce_out, reduce_bias,
):
    count = lax.axis_size("tensor")
    x, y, c, z = (lax.axis_index(axis) for axis in AXES)
    is_first = x == 0
    core = c.reshape(1).astype(jnp.int32)
    width = attend_in.shape[1]
    local = attend_in.shape[3]
    units = expand_in.shape[2]
    part = units // 4
    spare = 16

    def either(index, pair):
        first, second = pair
        return jnp.where(index == 0, first, second), jnp.where(index == 0, second, first)

    def relative(blocks):
        rows = [either(y, blocks[:2]), either(y, blocks[2:])]
        return list(zip(*(either(c, pair) for pair in zip(*rows))))

    def quarters(value, axis):
        return relative(jnp.split(value, 4, axis))

    typed = [*attend_in[0].transpose(1, 2, 0), attend_out[0]]
    (mine, mine_y), _ = relative(typed)
    biases = thirds(jnp.concatenate([attend_bias[0].reshape(2 * local), expand_bias[0]])).reshape(-1)
    biases = jnp.pad(biases, (0, spare * width - biases.size)).reshape(spare, width)
    piece = jnp.concatenate([mine, biases])
    bias_rows = [biases]
    own_parts = [quarters(expand_in[0].T, 0), quarters(reduce_out[0], 0)]
    feed = [jnp.concatenate([value[0][0] for value in own_parts])]
    feed_y = [jnp.concatenate([value[0][1] for value in own_parts])]
    pieces, pieces_y = [ring(piece)], []
    arrived = fetch(inputs[0, 0], 0)
    while len(pieces) < count - 1:
        pieces_y.append(swap(pieces[-1][:local], "y"))
        pieces.append(ring(pieces[-1]))
        pieces[-1], pieces_y[-1], feed[0], *arrived = lax.optimization_barrier(
            (pieces[-1], pieces_y[-1], feed[0], *arrived)
        )
        if len(pieces) == count - 1:
            feed.append(ring(feed[0]))
    pieces_y.append(swap(pieces[-1][:local], "y"))
    feed[1], pieces_y[-1] = lax.optimization_barrier((feed[1], pieces_y[-1]))
    feed_y.append(swap(feed[1], "y"))
    feed.append(ring(feed[1]))
    before = (feed[2], feed_y[1])
    bias_rows += [value[local:] for value in pieces]
    pieces = [mine] + [value[:local] for value in pieces]
    pieces_y = [mine_y] + pieces_y
    pieces = jnp.concatenate(pieces)
    pieces_y = jnp.concatenate(pieces_y)
    proj = relative([pieces, pieces_y, swap(pieces, "core"), swap(pieces_y, "core")])
    proj = [*proj[0], *proj[1]]
    biases = jnp.stack(bias_rows).reshape(count, -1)[:, : 3 * (2 * local + units)].reshape(count, 3, 2 * local + units)
    biases = biases.astype(F32)
    biases = biases[:, 0] + (biases[:, 1] + biases[:, 2])
    bias_q, bias_v = biases[:, :local].reshape(width), biases[:, local : 2 * local].reshape(width)
    expand_b = quarters(biases[:, 2 * local :], 1)
    expand_b = [jnp.concatenate([value.reshape(count * part) for value in pair]) for pair in expand_b]
    attention_weights = (gain_one[0], shift_one[0], proj, bias_q, bias_v, out_bias[0])

    rows_in = jnp.concatenate(arrived)
    middle, _, after = attention_forward(
        core, rows_in.astype(F32), attention_weights, False, before,
        (before, lambda ready: (ring(ready[0]), swap(ready[0], "y"))),
    )
    feed.append(after[0])
    feed_y += [after[1], swap(after[0], "y")]
    own_half = [
        jnp.concatenate([value[kind * part : (kind + 1) * part] for value in feed + feed_y]) for kind in range(2)
    ]
    other_half = [swap(value, "core") for value in own_half]
    feed_weights = (
        gain_two[0],
        shift_two[0],
        [(own_half[0], expand_b[0], own_half[1]), (other_half[0], expand_b[1], other_half[1])],
        reduce_bias[0],
    )
    passed = jnp.concatenate([along_pipe(rows, 1) for rows in feed_forward_only(middle, feed_weights)])
    last = jnp.concatenate(fetch(tie(cotangent[0, 0], passed), 1))
    rows_in = jnp.where(is_first, rows_in, passed)
    middle, kept_attention, _ = attention_forward(core, rows_in.astype(F32), attention_weights, True)
    result, grad_middle, kept_feed = feed_forward_and_back(middle, last.astype(F32), feed_weights)
    block = result.shape[0] // 2
    outputs = give_back(result[:block], result[block:], 1)
    grad_in, _, _, _, _, (outputs,) = attention_backward(
        core, kept_attention, grad_middle, attention_weights, (), (outputs,)
    )
    grad_in = narrow(grad_in)
    returned = jnp.concatenate([along_pipe(grad_in[:block], -1), along_pipe(grad_in[block:], -1)])
    grad_result = jnp.where(is_first, returned, last).astype(F32)
    grad_outcome = BRANCH * grad_result
    rounded_outcome = narrow(grad_outcome)
    normed_two, inverse_two, ready_two, hidden, slope = kept_feed
    span = count * part

    def by_slot(value):
        return [value[slot * part : (slot + 1) * part] for slot in range(count)]

    def steps_of(parts):
        state = [parts[1 % count]]

        def start():
            state.append(ring(state[-1]))
            return state[-1]

        def finish(arrived, step):
            state.append(wide_add(arrived, parts[(step + 1) % count]))
            return state[-1]

        return start, finish

    send = narrow(tn(hidden[1], rounded_outcome))
    arrived = swap(send, "core")
    keep = tn(hidden[0], tie(rounded_outcome, send))
    total, pre_own, pre_other, sums_own, sums_other = feed_back(tie(rounded_outcome, keep), feed_weights[2], slope)
    reduce_sums = wide_add(keep, tie(arrived, total))
    reduce_y = swap(reduce_sums[span:], "y")
    total = tie(total, reduce_sums)
    grad_middle = grad_result + norm_backward(total, normed_two, inverse_two, gain_two[0])
    shared_feed = [total * normed_two, total, grad_outcome]
    send = narrow(tn(tie(pre_other, grad_middle), ready_two))
    arrived = swap(send, "core")
    keep = tn(pre_own, tie(ready_two, send))
    expand_sums = wide_add(keep, tie(arrived, keep))
    expand_parts = [jnp.concatenate(pair) for pair in zip(by_slot(expand_sums[:span]), by_slot(expand_sums[span:]))]
    expand_start, expand_finish = steps_of(expand_parts)
    grad_in, rounded_attended, grad_qkv, sums_qv, shared_attention, after = attention_backward(
        core, kept_attention, grad_middle, attention_weights, expand_parts, (expand_start(), reduce_y)
    )
    expand_step = expand_finish(after[0], 1)
    reduce_parts = by_slot(wide_add(reduce_sums[:span], after[1]))
    reduce_start, reduce_finish = steps_of(reduce_parts)
    grad_qkv = lax.optimization_barrier((*grad_qkv, expand_step, *reduce_parts))[:3]
    grad_in = narrow(grad_in)
    expand_step = expand_start()
    mixed, ready_one = kept_attention[4], kept_attention[2]
    left = jnp.stack([*grad_qkv, mixed])
    index = 2 * c + y

    def typed_grad(shift):
        right = jnp.where((index ^ shift) == 3, rounded_attended, ready_one)
        return tn(lax.dynamic_index_in_dim(left, index ^ shift, 0, False), right)

    send = [narrow(typed_grad(shift)) for shift in (3, 2)]
    arrived = [swap(value, "core") for value in send]
    left = tie(left, *send)
    keep = [typed_grad(shift) for shift in (1, 0)]
    expand_step, keep[1] = lax.optimization_barrier((expand_step, keep[1]))
    expand_step = expand_finish(expand_step, 2)
    shared = shared_attention + shared_feed
    shared = jnp.stack([jnp.sum(value, axis=0) for value in shared])
    sums_qv = sums_qv.reshape(2, count, local)
    sums_qv = jnp.concatenate([sums_qv[0], sums_qv[1], jnp.zeros((count, width - 2 * local), F32)], axis=1)[:, None]
    sums_pre = [value.reshape(count, part) for half in (sums_own[0], sums_other[0]) for value in jnp.split(half, 2)]
    sums_pre = quarters(jnp.concatenate(sums_pre, axis=1), 1)
    sums_pre = jnp.concatenate(sums_pre[0] + sums_pre[1], axis=1)[:, None]
    vectors = jnp.concatenate([jnp.broadcast_to(shared, (count,) + shared.shape), sums_qv, sums_pre], axis=1)
    vectors = jnp.pad(vectors, ((0, 0), (0, spare - 8), (0, 0)))
    vectors = vectors + swap(vectors, "core")

    sums = [wide_add(a, b) for a, b in zip(keep, arrived)]
    to_y, to_keep = by_slot(sums[0]), by_slot(sums[1])
    typed_parts = [None] * count

    def typed_swap(slot):
        return swap(to_y[slot], "y")

    moving_y, moving_e, vectors_y = typed_swap(1), expand_start(), swap(vectors, "y")
    moving_y, vectors_y, to_y[2] = lax.optimization_barrier((moving_y, vectors_y, to_y[2]))
    typed_parts[1] = wide_add(to_keep[1], moving_y)
    vectors = narrow(vectors + vectors_y)
    reduce_parts = [jnp.concatenate([a, b]) for a, b in zip(reduce_parts, vectors)]
    reduce_start, reduce_finish = steps_of(reduce_parts)
    typed_start, typed_finish = steps_of(typed_parts)
    moving_t, moving_y, moving_r = typed_start(), typed_swap(2), reduce_start()
    moving_t, moving_y, moving_e = lax.optimization_barrier((moving_t, moving_y, moving_e))
    typed_parts[2] = wide_add(to_keep[2], moving_y)
    typed_finish(moving_t, 1)
    expand_total = expand_finish(moving_e, 3).reshape(2, part, width)
    moving_t, moving_y, expand_other = typed_start(), typed_swap(3), swap(expand_total, "y")
    moving_t, moving_y, moving_r = lax.optimization_barrier((moving_t, moving_y, moving_r))
    typed_parts[3] = wide_add(to_keep[3], moving_y)
    typed_finish(moving_t, 2)
    reduce_finish(moving_r, 1)
    moving_t, moving_y, moving_r = typed_start(), typed_swap(0), reduce_start()
    moving_t, moving_y, moving_r, expand_other = lax.optimization_barrier((moving_t, moving_y, moving_r, expand_other))
    typed_parts[0] = wide_add(to_keep[0], moving_y)
    typed_total = typed_finish(moving_t, 3)
    reduce_finish(moving_r, 2)
    reduce_total = reduce_finish(reduce_start(), 3)
    grad_in = tie(grad_in, moving_t)
    input_grad = give_back(grad_in[:block], grad_in[block:], 0)
    def gathered(pair):
        pair = jnp.concatenate(pair)
        blocks = quarters(jnp.concatenate([pair, swap(pair, "core")]), 0)
        return jnp.concatenate(blocks[0] + blocks[1])

    grad_expand = [over_groups(wide_add(expand_total[i], expand_other[1 - i])) for i in range(2)]
    grad_expand = gathered(grad_expand).T.astype(F32)
    typed_total = over_groups(typed_total)
    pair = jnp.concatenate([typed_total, swap(typed_total, "y")])
    pair_other = swap(pair, "core")
    whole = relative([pair[:local], pair[local:], pair_other[:local], pair_other[local:]])
    whole = [*whole[0], *whole[1]]
    grad_attend_in = jnp.stack(whole[:3]).transpose(2, 0, 1).astype(F32)
    grad_attend_out = whole[3].astype(F32)
    reduce_total = over_groups(reduce_total)
    vectors = reduce_total[part : part + 8].astype(F32)
    reduce_total = reduce_total[:part]
    grad_reduce = gathered([reduce_total, swap(reduce_total, "y")]).astype(F32)
    return (
        outputs[None, None],
        input_grad[None, None],
        vectors[0][None],
        vectors[1][None],
        grad_attend_in[None],
        vectors[6, : 2 * local].reshape(1, 2, local),
        grad_attend_out[None],
        vectors[2][None],
        vectors[3][None],
        vectors[4][None],
        grad_expand[None],
        vectors[7, :units][None],
        grad_reduce[None],
        vectors[5][None],
    )


def solution(mesh):
    pipe, groups, count = mesh.devices.shape
    split = Mesh(mesh.devices.reshape(pipe, groups // 4, 2, 2, count), ("pipe", "outer", "y", "core", "tensor"))
    dp = ("outer", "y", "core")
    rows = P("pipe", dp, "tensor", None)
    vector = P("pipe", None)
    placed = (
        rows,
        rows,
        vector,
        vector,
        P("pipe", None, None, "tensor"),
        P("pipe", None, "tensor"),
        P("pipe", "tensor", None),
        vector,
        vector,
        vector,
        P("pipe", None, "tensor"),
        P("pipe", "tensor"),
        P("pipe", "tensor", None),
        vector,
    )
    return jax.shard_map(shards, mesh=split, in_specs=placed, out_specs=(rows, rows) + placed[2:], check_vma=False)
```

time: 520 us -> 464 us (0.89)
  waiting for transfers between devices: 208 us -> 173 us
  local copies, waits for them, and re-layouts: 50.6 us -> 33.6 us
  starting transfers between devices: 54.6 us -> 70.6 us
  Pallas kernels: 109 us -> 94.4 us
    ppermute x15, waiting for transfers between devices: 84.8 us -> 49.6 us  [ring(): lax.ppermute(value, 'tensor', list(zip(order, order[1:] + order[:1])))]
    pallas_call x12 -> x9, Pallas kernels: 109 us -> 94.4 us  [the longest x2 29.8 us: attend_back(): pl.pallas_call(attend_back_kernel, grid=(width // LANES,), out_shape=[jax...]
    unnamed x200 -> x226, local copies, waits for them, and re-layouts: 34.1 us -> 20 us
    ppermute x4, waiting for transfers between devices: 12.4 us -> 3.17 us  [give_back(): pieces.append(lax.ppermute(rows, AXES, pairs))]
    ppermute x15, starting transfers between devices: 5.92 us -> 12.7 us  [ring(): lax.ppermute(value, 'tensor', list(zip(order, order[1:] + order[:1])))]
    ppermute x4, waiting for transfers between devices: 36.2 us -> 42.9 us  [fetch(): lax.ppermute(block, AXES, routes(section, large))]
    unnamed x9 -> x7, other arithmetic: 7.18 us -> 1.19 us
    ppermute x4, starting transfers between devices: 8.62 us -> 14.3 us  [fetch(): lax.ppermute(block, AXES, routes(section, large))]
  transfers between devices with their start and end apart: 59 -> 60, of which waited for: 28 -> 28; matrix products, arithmetic and copies ran while one was open for 16% -> 16% of each run, Pallas kernels for 7% -> 13%
where the time goes in v2:
time: 464 us; the launch traced here: 455 us
  waiting for transfers between devices  173 us (37%)
  Pallas kernels  94.4 us (20%)
  starting transfers between devices  70.6 us (15%)
  other arithmetic  45.9 us (10%)
  matrix products  34.6 us (7%)
  local copies, waits for them, and re-layouts  33.6 us (7%)
    ppermute x15, waiting for transfers between devices, ring(): lax.ppermute(value, 'tensor', list(zip(order, order[1:] + order[:1])))  49.6 us
    ppermute x33, waiting for transfers between devices, swap(): return lax.ppermute(value, axis, [(0, 1), (1, 0)])  43.3 us
    ppermute x4, waiting for transfers between devices, fetch(): lax.ppermute(block, AXES, routes(section, large))  42.9 us
    ppermute x4, waiting for transfers between devices, along_pipe(): return lax.ppermute(value, 'pipe', [(0, 1)] if by > 0 else [(1, 0)])  34.2 us
    pallas_call x2, Pallas kernels, attend_back(): pl.pallas_call(attend_back_kernel, grid=(width // LANES,), out_shape=[jax...  29.8 us
    ppermute x33, starting transfers between devices, swap(): return lax.ppermute(value, axis, [(0, 1), (1, 0)])  24.8 us
    pallas_call x2, Pallas kernels, attend(): pl.pallas_call(functools.partial(attend_kernel, keep_weights), grid=(widt...  24.2 us
    unnamed x226, local copies, waits for them, and re-layouts  20 us
  transfers between devices with their start and end apart: 60, of which 28 were waited for; matrix products, arithmetic and copies ran while one was open for 16% of the time, Pallas kernels for 13%

profile of v2, /device:TPU:17, one launch (start us, length us, event | category | flops | bytes accessed | tf_op | source)
XLA Modules:
  0.0 455.3 jit_solution(6275213565055371532)
XLA Ops:
  6.4 4.0 collective-permute-start.4
  16.3 29.5 %collective-permute-done.3 = bf16[256,768]{1,0:T(8,128)(2,1)} collective-permute-done((bf16[256,768]{1,0:T(8,128)(2,1)}, bf16[256,768]{1,0:T(8,128)(2,1)}, u32[]{:S(2)}, u32[]{:S(2)}) %collective-permute-start.3) | collective-permute-done | bytes 393248 | tf_op jit(solution)/shard_map/ppermute | solution.py:57
  49.0 4.3 collective-permute-done.6
  57.2 3.1 collective-permute-done.8
  60.3 10.8 %collective-permute-done.7 = bf16[384,768]{1,0:T(8,128)(2,1)S(1)} collective-permute-done((bf16[384,768]{1,0:T(8,128)(2,1)S(1)}, bf16[384,768]{1,0:T(8,128)(2,1)S(1)}, u32[]{:S(2)}, u32[]{:S(2)}) %collective-permute-start.7) | collective-permute-done | bytes 589856 | tf_op jit(solution)/shard_map/ppermute | solution.py:29
  89.4 8.5 %collective-permute-done.11 = bf16[384,768]{1,0:T(8,128)(2,1)S(1)} collective-permute-done((bf16[384,768]{1,0:T(8,128)(2,1)S(1)}, bf16[384,768]{1,0:T(8,128)(2,1)S(1)}, u32[]{:S(2)}, u32[]{:S(2)}) %collective-permute-start.11) | collective-permute-done | bytes 589856 | tf_op jit(solution)/shard_map/ppermute | solution.py:29
  100.1 11.3 %attend.2 = bf16[512,768]{1,0:T(8,128)(2,1)S(1)} custom-call(s32[1]{0:T(128)} %bitcast.core_ref, bf16[512,768]{1,0:T(8,128)(2,1)S(1)} %add_convert_fusion.13.q_ref, bf16[512,768]{1,0:T(8,128)(2,1)S(1)} %convolution_convert_fusion.7.k_ref, bf16[512,768]{1,0:T(8,128)(2,1)S(1)} %add_convert_fusion.12.v_ref, ...), custom_call_target="tpu_custom_call" | custom-call | flops 2013265920 | bytes 6291456 | tf_op jit(solution)/shard_map/attend/pallas_call | solution.py:254
  116.9 9.3 %collective-permute-done.17 = bf16[384,768]{1,0:T(8,128)(2,1)S(1)} collective-permute-done((bf16[384,768]{1,0:T(8,128)(2,1)S(1)}, bf16[384,768]{1,0:T(8,128)(2,1)S(1)}, u32[]{:S(2)}, u32[]{:S(2)}) %collective-permute-start.17) | collective-permute-done | bytes 589856 | tf_op jit(solution)/shard_map/ppermute | solution.py:33
  127.1 2.6 collective-permute-start.18
  130.0 2.2 broadcast_select_fusion.4
  134.1 5.8 %feed_half.3.start_ref = f32[512,768]{1,0:T(8,128)S(1)} custom-call(bf16[512,768]{1,0:T(8,128)(2,1)S(1)} %add_convert_fusion.11.rows_ref, bf16[1536,768]{1,0:T(8,128)(2,1)} %get-tuple-element.254.expand_ref.e0_ref, f32[1,1536]{1,0:T(1,128)S(1)} %reshape.403.bias_ref.b0_ref, bf16[1536,768]{1,0:T(8,128)(2,1)} %get-tuple-element.253.reduce_ref.r0_ref, ...), custom_call_target="tpu_custom_call" | custom-call | flops 2415919104 | bytes 4718592 | tf_op jit(solution)/shard_map/feed_half/pallas_call | solution.py:340
  140.0 4.7 %feed_half.4 = f32[256,768]{1,0:T(8,128)S(1)} custom-call(bf16[512,768]{1,0:T(8,128)(2,1)S(1)} %add_convert_fusion.11.rows_ref, bf16[1536,768]{1,0:T(8,128)(2,1)S(1)} %collective-permute-done.18.expand_ref.e1_ref, f32[1,1536]{1,0:T(1,128)S(1)} %reshape.400.bias_ref.b1_ref, bf16[1536,768]{1,0:T(8,128)(2,1)} %collective-permute-done.19.reduce_ref.r1_ref, ...), custom_call_target="tpu_custom_call" | custom-call | flops 1207959552 | bytes 4718592 | tf_op jit(solution)/shard_map/feed_half/pallas_call | solution.py:340
  145.5 3.5 collective-permute-start.20
  149.1 4.1 feed_half.5
  154.8 2.5 collective-permute-done.20
  157.3 8.3 %collective-permute-done.21 = bf16[256,768]{1,0:T(8,128)(2,1)S(1)} collective-permute-done((bf16[256,768]{1,0:T(8,128)(2,1)S(1)}, bf16[256,768]{1,0:T(8,128)(2,1)S(1)}, u32[]{:S(2)}, u32[]{:S(2)}) %collective-permute-start.21) | collective-permute-done | bytes 393248 | tf_op jit(solution)/shard_map/ppermute | solution.py:37
  169.7 8.2 %collective-permute-start.25 = (bf16[256,768]{1,0:T(8,128)(2,1)S(1)}, bf16[256,768]{1,0:T(8,128)(2,1)S(1)}, u32[]{:S(2)}, u32[]{:S(2)}) collective-permute-start(bf16[256,768]{1,0:T(8,128)(2,1)S(1)} %bitcast.157), channel_id=1, source_target_pairs={{3,16},{2,20},{7,17},{6,21},{11,24},{10,28},{15,25},{14,29},{19,18... | collective-permute-start | bytes 1179656 | tf_op jit(solution)/shard_map/ppermute | solution.py:57
  177.9 2.6 collective-permute-start.22
  181.6 13.4 %collective-permute-done.25 = bf16[256,768]{1,0:T(8,128)(2,1)S(1)} collective-permute-done((bf16[256,768]{1,0:T(8,128)(2,1)S(1)}, bf16[256,768]{1,0:T(8,128)(2,1)S(1)}, u32[]{:S(2)}, u32[]{:S(2)}) %collective-permute-start.25) | collective-permute-done | bytes 393248 | tf_op jit(solution)/shard_map/ppermute | solution.py:57
  195.2 12.8 %attend.3 = (bf16[512,768]{1,0:T(8,128)(2,1)S(1)}, bf16[12,5,256,256]{3,2,1,0:T(8,128)(2,1)}) custom-call(s32[1]{0:T(128)} %bitcast.core_ref, bf16[512,768]{1,0:T(8,128)(2,1)S(1)} %add_convert_fusion.10.q_ref, bf16[512,768]{1,0:T(8,128)(2,1)S(1)} %convolution_convert_fusion.6.k_ref, bf16[512,768]{1,0:T(8,128)(2,1)S(1)} %add_convert_fusion.9.v_ref, ...), custom_call_target="tpu_custom_call" | custom-call | flops 2013265920 | bytes 6291456 | tf_op jit(solution)/shard_map/attend/pallas_call | solution.py:254
  209.9 16.5 %feed_both.1 = (f32[512,768]{1,0:T(8,128)S(1)}, f32[512,768]{1,0:T(8,128)S(1)}, bf16[512,1536]{1,0:T(8,128)(2,1)S(1)}, bf16[512,1536]{1,0:T(8,128)(2,1)S(1)}, bf...) custom-call(bf16[512,768]{1,0:T(8,128)(2,1)S(1)} %add_convert_fusion.8.rows_ref, ...), custom_call_target="tpu_custom_call" | custom-call | flops 9663676416 | bytes 9437184 | tf_op jit(solution)/shard_map/feed_both/pallas_call | solution.py:435
  232.5 15.0 %attend_back.2 = (bf16[512,768]{1,0:T(8,128)(2,1)S(1)}, f32[2,512,768]{2,1,0:T(8,128)S(1)}, bf16[2,512,768]{2,1,0:T(8,128)(2,1)S(1)}, f32[8,768]{1,0:T(8,128)}) custom-call(s32[1]{0:T(128)} %bitcast.core_ref, bf16[512,768]{1,0:T(8,128)(2,1)S(1)} %add_convert_fusion.10.q_ref, bf16[512,768]{1,0:T(8,128)(2,1)S(1)} %convolution_convert_fusion.6.k_ref, ...), custom_call_target="tpu_custom_call" | custom-call | flops 4026531840 | bytes 15728640 | tf_op jit(solution)/shard_map/attend_back/pallas_call | solution.py:273
  260.4 15.0 %collective-permute-done.30 = bf16[256,768]{1,0:T(8,128)(2,1)S(1)} collective-permute-done((bf16[256,768]{1,0:T(8,128)(2,1)S(1)}, bf16[256,768]{1,0:T(8,128)(2,1)S(1)}, u32[]{:S(2)}, u32[]{:S(2)}) %collective-permute-start.30) | collective-permute-done | bytes 393248 | tf_op jit(solution)/shard_map/ppermute | solution.py:37
  275.4 8.4 %collective-permute-done.29 = bf16[256,768]{1,0:T(8,128)(2,1)S(1)} collective-permute-done((bf16[256,768]{1,0:T(8,128)(2,1)S(1)}, bf16[256,768]{1,0:T(8,128)(2,1)S(1)}, u32[]{:S(2)}, u32[]{:S(2)}) %collective-permute-start.29) | collective-permute-done | bytes 393248 | tf_op jit(solution)/shard_map/ppermute | solution.py:37
  284.1 2.8 convolution_convert_fusion.1
  289.6 9.3 %feed_back.1 = (f32[512,768]{1,0:T(8,128)S(1)}, bf16[512,1536]{1,0:T(8,128)(2,1)S(1)}, bf16[512,1536]{1,0:T(8,128)(2,1)S(1)}, f32[8,1536]{1,0:T(8,128)S(1)}, f32[8,1536]{1,0:T(8,128)S(1)}) custom-call(bf16[512,768]{1,0:T(8,128)(2,1)S(1)} %fusion.1.grad_ref, bf16[1536,768]{1,0:T(8,128)(2,1)} %get-tuple-element.254.expand_ref.e0_ref, ...), custom_call_target="tpu_custom_call" | custom-call | flops 4831838208 | bytes 9437184 | tf_op jit(solution)/shard_map/feed_back/pallas_call | solution.py:456
  303.5 2.8 convolution_convert_fusion
  311.2 2.4 add_convert_fusion
  317.1 14.8 %attend_back.3 = (bf16[512,768]{1,0:T(8,128)(2,1)S(1)}, f32[2,512,768]{2,1,0:T(8,128)S(1)}, bf16[2,512,768]{2,1,0:T(8,128)(2,1)}, f32[8,768]{1,0:T(8,128)S(1)}) custom-call(s32[1]{0:T(128)} %bitcast.core_ref, bf16[512,768]{1,0:T(8,128)(2,1)S(1)} %copy-done.16, bf16[512,768]{1,0:T(8,128)(2,1)S(1)} %copy-done.10, bf16[512,768]{1,0:T(8,128)(2,1)S(1)} %copy-done.8, ...), custom_call_target="tpu_custom_call" | custom-call | flops 4026531840 | bytes 15728640 | tf_op jit(solution)/shard_map/attend_back/pallas_call | solution.py:273
  332.8 2.4 collective-permute-done.34
  337.1 2.4 fusion.96
  347.8 2.0 convolution_convert_fusion.3
  350.8 2.0 convolution_convert_fusion.2
  354.9 2.1 fusion.39
  359.6 2.5 add_convert_fusion.4
  365.4 5.9 %collective-permute-done.39 = bf16[192,768]{1,0:T(8,128)(2,1)S(1)} collective-permute-done((bf16[192,768]{1,0:T(8,128)(2,1)S(1)}, bf16[192,768]{1,0:T(8,128)(2,1)S(1)}, u32[]{:S(2)}, u32[]{:S(2)}) %collective-permute-start.39) | collective-permute-done | bytes 294944 | tf_op jit(solution)/shard_map/ppermute | solution.py:33
  372.6 3.5 collective-permute-start.47
  376.1 2.8 collective-permute-done.42
  378.9 5.1 %collective-permute-done.43 = bf16[192,768]{1,0:T(8,128)(2,1)S(1)} collective-permute-done((bf16[192,768]{1,0:T(8,128)(2,1)S(1)}, bf16[192,768]{1,0:T(8,128)(2,1)S(1)}, u32[]{:S(2)}, u32[]{:S(2)}) %collective-permute-start.43) | collective-permute-done | bytes 294944 | tf_op jit(solution)/shard_map/ppermute | solution.py:33
  385.9 7.4 %collective-permute-done.45 = bf16[192,768]{1,0:T(8,128)(2,1)S(1)} collective-permute-done((bf16[192,768]{1,0:T(8,128)(2,1)S(1)}, bf16[192,768]{1,0:T(8,128)(2,1)S(1)}, u32[]{:S(2)}, u32[]{:S(2)}) %collective-permute-start.45) | collective-permute-done | bytes 294944 | tf_op jit(solution)/shard_map/ppermute | solution.py:29
  394.0 3.2 collective-permute-start.50
  397.8 3.4 collective-permute-done.48
  401.2 2.9 collective-permute-done.51
  404.2 3.9 collective-permute-done.50
  409.0 6.5 %collective-permute-start.52 = (bf16[256,768]{1,0:T(8,128)(2,1)}, bf16[256,768]{1,0:T(8,128)(2,1)}, u32[]{:S(2)}, u32[]{:S(2)}) collective-permute-start(bf16[256,768]{1,0:T(8,128)(2,1)} %get-tuple-element.248), channel_id=1, source_target_pairs={{0,0},{4,1},{1,4},{5,5},{8,8},{12,9},{9,12},{13,13},{2,16},{6,17},... | collective-permute-start | bytes 1179656 | tf_op jit(solution)/shard_map/ppermute | solution.py:64
  419.2 7.4 %collective-permute-done.55 = bf16[192,768]{1,0:T(8,128)(2,1)S(1)} collective-permute-done((bf16[192,768]{1,0:T(8,128)(2,1)S(1)}, bf16[192,768]{1,0:T(8,128)(2,1)S(1)}, u32[]{:S(2)}, u32[]{:S(2)}) %collective-permute-start.55) | collective-permute-done | bytes 294944 | tf_op jit(solution)/shard_map/ppermute | solution.py:33
  427.4 10.1 %collective-permute-done.54 = bf16[208,768]{1,0:T(8,128)(2,1)S(1)} collective-permute-done((bf16[208,768]{1,0:T(8,128)(2,1)S(1)}, bf16[208,768]{1,0:T(8,128)(2,1)S(1)}, u32[]{:S(2)}, u32[]{:S(2)}) %collective-permute-start.54) | collective-permute-done | bytes 319520 | tf_op jit(solution)/shard_map/ppermute | solution.py:29
  440.2 2.8 collective-permute-done.53
  (486 shorter events, 135.1 us)
Async XLA Ops:
  3.8 9.5 %collective-permute-start = (bf16[208,768]{1,0:T(8,128)(2,1)S(1)}, bf16[208,768]{1,0:T(8,128)(2,1)}, u32[]{:S(2)}, u32[]{:S(2)}) collective-permute-start(bf16[208,768]{1,0:T(8,128)(2,1)S(1)} %pad_maximum_fusion.11), channel_id=1, source_target_pairs={{0,2},{2,3},{3,1},{1,0},{4,6},{6,7},{7,5},{5,4},{8,10},{10,11},{11... | collective-permute-start | bytes 958472 | tf_op jit(solution)/shard_map/ppermute | solution.py:29
  5.2 40.6 %collective-permute-start.3 = (bf16[256,768]{1,0:T(8,128)(2,1)}, bf16[256,768]{1,0:T(8,128)(2,1)}, u32[]{:S(2)}, u32[]{:S(2)}) collective-permute-start(bf16[256,768]{1,0:T(8,128)(2,1)} %bitcast.9), channel_id=1, source_target_pairs={{0,0},{1,4},{4,1},{5,5},{8,8},{9,12},{12,9},{13,13},{16,2},{17,6},... | collective-permute-start | bytes 1179656 | tf_op jit(solution)/shard_map/ppermute | solution.py:57
  6.4 39.3 %collective-permute-start.4 = (bf16[256,768]{1,0:T(8,128)(2,1)}, bf16[256,768]{1,0:T(8,128)(2,1)}, u32[]{:S(2)}, u32[]{:S(2)}) collective-permute-start(bf16[256,768]{1,0:T(8,128)(2,1)} %bitcast.9), channel_id=1, source_target_pairs={{3,0},{2,4},{7,1},{6,5},{11,8},{10,12},{15,9},{14,13},{19,2},{18,6... | collective-permute-start | bytes 1179656 | tf_op jit(solution)/shard_map/ppermute | solution.py:57
  14.3 31.5 %collective-permute-start.2 = (bf16[192,768]{1,0:T(8,128)(2,1)S(1)}, bf16[192,768]{1,0:T(8,128)(2,1)S(1)}, u32[]{:S(2)}, u32[]{:S(2)}) collective-permute-start(bf16[192,768]{1,0:T(8,128)(2,1)S(1)} %slice.353), channel_id=1, source_target_pairs={{0,8},{8,0},{1,9},{9,1},{2,10},{10,2},{3,11},{11,3},{4,12},{12,4},... | collective-permute-start | bytes 884744 | tf_op jit(solution)/shard_map/ppermute | solution.py:33
  15.6 30.2 %collective-permute-start.1 = (bf16[208,768]{1,0:T(8,128)(2,1)}, bf16[208,768]{1,0:T(8,128)(2,1)S(1)}, u32[]{:S(2)}, u32[]{:S(2)}) collective-permute-start(bf16[208,768]{1,0:T(8,128)(2,1)} %collective-permute-done), channel_id=1, source_target_pairs={{0,2},{2,3},{3,1},{1,0},{4,6},{6,7},{7,5},{5,4},{8,10},{10,11},{11... | collective-permute-start | bytes 958472 | tf_op jit(solution)/shard_map/ppermute | solution.py:29
  55.7 26.9 %collective-permute-start.9 = (bf16[768,768]{1,0:T(8,128)(2,1)}, bf16[768,768]{1,0:T(8,128)(2,1)S(1)}, u32[]{:S(2)}, u32[]{:S(2)}) collective-permute-start(bf16[768,768]{1,0:T(8,128)(2,1)} %pad_maximum_fusion.1), channel_id=1, source_target_pairs={{0,4},{4,0},{1,5},{5,1},{2,6},{6,2},{3,7},{7,3},{8,12},{12,8},{9,1... | collective-permute-start | bytes 3538952 | tf_op jit(solution)/shard_map/ppermute | solution.py:33
  55.7 15.4 %collective-permute-start.7 = (bf16[384,768]{1,0:T(8,128)(2,1)S(1)}, bf16[384,768]{1,0:T(8,128)(2,1)S(1)}, u32[]{:S(2)}, u32[]{:S(2)}) collective-permute-start(bf16[384,768]{1,0:T(8,128)(2,1)S(1)} %pad_maximum_fusion.3), channel_id=1, source_target_pairs={{0,2},{2,3},{3,1},{1,0},{4,6},{6,7},{7,5},{5,4},{8,10},{10,11},{11... | collective-permute-start | bytes 1769480 | tf_op jit(solution)/shard_map/ppermute | solution.py:29
  73.1 9.6 %collective-permute-start.10 = (bf16[768,768]{1,0:T(8,128)(2,1)}, bf16[768,768]{1,0:T(8,128)(2,1)S(1)}, u32[]{:S(2)}, u32[]{:S(2)}) collective-permute-start(bf16[768,768]{1,0:T(8,128)(2,1)} %pad_maximum_fusion.2), channel_id=1, source_target_pairs={{0,4},{4,0},{1,5},{5,1},{2,6},{6,2},{3,7},{7,3},{8,12},{12,8},{9,1... | collective-permute-start | bytes 3538952 | tf_op jit(solution)/shard_map/ppermute | solution.py:33
  82.1 15.9 %collective-permute-start.11 = (bf16[384,768]{1,0:T(8,128)(2,1)S(1)}, bf16[384,768]{1,0:T(8,128)(2,1)S(1)}, u32[]{:S(2)}, u32[]{:S(2)}) collective-permute-start(bf16[384,768]{1,0:T(8,128)(2,1)S(1)} %copy-done.80), channel_id=1, source_target_pairs={{0,2},{2,3},{3,1},{1,0},{4,6},{6,7},{7,5},{5,4},{8,10},{10,11},{11... | collective-permute-start | bytes 1769480 | tf_op jit(solution)/shard_map/ppermute | solution.py:29
  82.4 15.5 %collective-permute-start.12 = (bf16[384,768]{1,0:T(8,128)(2,1)S(1)}, bf16[384,768]{1,0:T(8,128)(2,1)S(1)}, u32[]{:S(2)}, u32[]{:S(2)}) collective-permute-start(bf16[384,768]{1,0:T(8,128)(2,1)S(1)} %copy-done.80), channel_id=1, source_target_pairs={{0,8},{8,0},{1,9},{9,1},{2,10},{10,2},{3,11},{11,3},{4,12},{12,4},... | collective-permute-start | bytes 1769480 | tf_op jit(solution)/shard_map/ppermute | solution.py:33
  85.4 14.7 %collective-permute-start.13 = (bf16[512,768]{1,0:T(8,128)(2,1)S(1)}, bf16[512,768]{1,0:T(8,128)(2,1)S(1)}, u32[]{:S(2)}, u32[]{:S(2)}) collective-permute-start(bf16[512,768]{1,0:T(8,128)(2,1)S(1)} %convolution_convert_fusion.7.k_ref), channel_id=1, source_target_pairs={{0,4},{4,0},{1,5},{5,1},{2,6},{6,2},{3,7},{7,3},{8,12},{12,8},{9,1... | collective-permute-start | bytes 2359304 | tf_op jit(solution)/shard_map/ppermute | solution.py:33
  87.7 12.4 %collective-permute-start.14 = (bf16[512,768]{1,0:T(8,128)(2,1)S(1)}, bf16[512,768]{1,0:T(8,128)(2,1)S(1)}, u32[]{:S(2)}, u32[]{:S(2)}) collective-permute-start(bf16[512,768]{1,0:T(8,128)(2,1)S(1)} %add_convert_fusion.12.v_ref), channel_id=1, source_target_pairs={{0,4},{4,0},{1,5},{5,1},{2,6},{6,2},{3,7},{7,3},{8,12},{12,8},{9,1... | collective-permute-start | bytes 2359304 | tf_op jit(solution)/shard_map/ppermute | solution.py:33
  97.9 15.1 %collective-permute-start.15 = (bf16[384,768]{1,0:T(8,128)(2,1)S(1)}, bf16[384,768]{1,0:T(8,128)(2,1)S(1)}, u32[]{:S(2)}, u32[]{:S(2)}) collective-permute-start(bf16[384,768]{1,0:T(8,128)(2,1)S(1)} %collective-permute-done.11), channel_id=1, source_target_pairs={{0,2},{2,3},{3,1},{1,0},{4,6},{6,7},{7,5},{5,4},{8,10},{10,11},{11... | collective-permute-start | bytes 1769480 | tf_op jit(solution)/shard_map/ppermute | solution.py:29
  98.1 15.0 %collective-permute-start.16 = (bf16[384,768]{1,0:T(8,128)(2,1)S(1)}, bf16[384,768]{1,0:T(8,128)(2,1)S(1)}, u32[]{:S(2)}, u32[]{:S(2)}) collective-permute-start(bf16[384,768]{1,0:T(8,128)(2,1)S(1)} %collective-permute-done.11), channel_id=1, source_target_pairs={{0,8},{8,0},{1,9},{9,1},{2,10},{10,2},{3,11},{11,3},{4,12},{12,4},... | collective-permute-start | bytes 1769480 | tf_op jit(solution)/shard_map/ppermute | solution.py:33
  113.1 13.1 %collective-permute-start.17 = (bf16[384,768]{1,0:T(8,128)(2,1)S(1)}, bf16[384,768]{1,0:T(8,128)(2,1)S(1)}, u32[]{:S(2)}, u32[]{:S(2)}) collective-permute-start(bf16[384,768]{1,0:T(8,128)(2,1)S(1)} %collective-permute-done.15), channel_id=1, source_target_pairs={{0,8},{8,0},{1,9},{9,1},{2,10},{10,2},{3,11},{11,3},{4,12},{12,4},... | collective-permute-start | bytes 1769480 | tf_op jit(solution)/shard_map/ppermute | solution.py:33
  127.1 12.9 %collective-permute-start.18 = (bf16[1536,768]{1,0:T(8,128)(2,1)}, bf16[1536,768]{1,0:T(8,128)(2,1)S(1)}, u32[]{:S(2)}, u32[]{:S(2)}) collective-permute-start(bf16[1536,768]{1,0:T(8,128)(2,1)} %get-tuple-element.254.expand_ref.e0_ref), channel_id=1, source_target_pairs={{0,4},{4,0},{1,5},{5,1},{2,6},{6,2},{3,7},{7,3},{8,12},{12,8},{9,1... | collective-permute-start | bytes 7077896 | tf_op jit(solution)/shard_map/ppermute | solution.py:33
  129.7 10.3 %collective-permute-start.19 = (bf16[1536,768]{1,0:T(8,128)(2,1)}, bf16[1536,768]{1,0:T(8,128)(2,1)}, u32[]{:S(2)}, u32[]{:S(2)}) collective-permute-start(bf16[1536,768]{1,0:T(8,128)(2,1)} %get-tuple-element.253.reduce_ref.r0_ref), channel_id=1, source_target_pairs={{0,4},{4,0},{1,5},{5,1},{2,6},{6,2},{3,7},{7,3},{8,12},{12,8},{9,1... | collective-permute-start | bytes 7077896 | tf_op jit(solution)/shard_map/ppermute | solution.py:33
  145.5 11.8 %collective-permute-start.20 = (bf16[256,768]{1,0:T(8,128)(2,1)}, bf16[256,768]{1,0:T(8,128)(2,1)S(1)}, u32[]{:S(2)}, u32[]{:S(2)}) collective-permute-start(bf16[256,768]{1,0:T(8,128)(2,1)} %fusion.34), channel_id=1, source_target_pairs={{0,16},{1,17},{2,18},{3,19},{4,20},{5,21},{6,22},{7,23},{8,24},{9,... | collective-permute-start | bytes 1179656 | tf_op jit(solution)/shard_map/ppermute | solution.py:37
  153.3 12.3 %collective-permute-start.21 = (bf16[256,768]{1,0:T(8,128)(2,1)S(1)}, bf16[256,768]{1,0:T(8,128)(2,1)S(1)}, u32[]{:S(2)}, u32[]{:S(2)}) collective-permute-start(bf16[256,768]{1,0:T(8,128)(2,1)S(1)} %fusion.33), channel_id=1, source_target_pairs={{0,16},{1,17},{2,18},{3,19},{4,20},{5,21},{6,22},{7,23},{8,24},{9,... | collective-permute-start | bytes 1179656 | tf_op jit(solution)/shard_map/ppermute | solution.py:37
  167.9 13.6 %collective-permute-start.24 = (bf16[256,768]{1,0:T(8,128)(2,1)S(1)}, bf16[256,768]{1,0:T(8,128)(2,1)S(1)}, u32[]{:S(2)}, u32[]{:S(2)}) collective-permute-start(bf16[256,768]{1,0:T(8,128)(2,1)S(1)} %bitcast.156), channel_id=1, source_target_pairs={{0,16},{1,20},{4,17},{5,21},{8,24},{9,28},{12,25},{13,29},{16,18},... | collective-permute-start | bytes 1179656 | tf_op jit(solution)/shard_map/ppermute | solution.py:57
  169.7 25.2 %collective-permute-start.25 = (bf16[256,768]{1,0:T(8,128)(2,1)S(1)}, bf16[256,768]{1,0:T(8,128)(2,1)S(1)}, u32[]{:S(2)}, u32[]{:S(2)}) collective-permute-start(bf16[256,768]{1,0:T(8,128)(2,1)S(1)} %bitcast.157), channel_id=1, source_target_pairs={{3,16},{2,20},{7,17},{6,21},{11,24},{10,28},{15,25},{14,29},{19,18... | collective-permute-start | bytes 1179656 | tf_op jit(solution)/shard_map/ppermute | solution.py:57
  177.9 17.2 %collective-permute-start.22 = (bf16[512,768]{1,0:T(8,128)(2,1)S(1)}, bf16[512,768]{1,0:T(8,128)(2,1)S(1)}, u32[]{:S(2)}, u32[]{:S(2)}) collective-permute-start(bf16[512,768]{1,0:T(8,128)(2,1)S(1)} %convolution_convert_fusion.6.k_ref), channel_id=1, source_target_pairs={{0,4},{4,0},{1,5},{5,1},{2,6},{6,2},{3,7},{7,3},{8,12},{12,8},{9,1... | collective-permute-start | bytes 2359304 | tf_op jit(solution)/shard_map/ppermute | solution.py:33
  180.5 14.7 %collective-permute-start.23 = (bf16[512,768]{1,0:T(8,128)(2,1)S(1)}, bf16[512,768]{1,0:T(8,128)(2,1)S(1)}, u32[]{:S(2)}, u32[]{:S(2)}) collective-permute-start(bf16[512,768]{1,0:T(8,128)(2,1)S(1)} %add_convert_fusion.9.v_ref), channel_id=1, source_target_pairs={{0,4},{4,0},{1,5},{5,1},{2,6},{6,2},{3,7},{7,3},{8,12},{12,8},{9,1... | collective-permute-start | bytes 2359304 | tf_op jit(solution)/shard_map/ppermute | solution.py:33
  228.9 18.6 %collective-permute-start.26 = (bf16[256,768]{1,0:T(8,128)(2,1)}, bf16[256,768]{1,0:T(8,128)(2,1)}, u32[]{:S(2)}, u32[]{:S(2)}) collective-permute-start(bf16[256,768]{1,0:T(8,128)(2,1)} %get-tuple-element.252), channel_id=1, source_target_pairs={{16,0},{20,1},{17,4},{21,5},{24,8},{28,9},{25,12},{29,13},{18,16},... | collective-permute-start | bytes 1179656 | tf_op jit(solution)/shard_map/ppermute | solution.py:64
  230.3 17.5 %collective-permute-start.27 = (bf16[256,768]{1,0:T(8,128)(2,1)}, bf16[256,768]{1,0:T(8,128)(2,1)}, u32[]{:S(2)}, u32[]{:S(2)}) collective-permute-start(bf16[256,768]{1,0:T(8,128)(2,1)} %get-tuple-element.251), channel_id=1, source_target_pairs={{16,3},{20,2},{17,7},{21,6},{24,11},{28,10},{25,15},{29,14},{18,19... | collective-permute-start | bytes 1179656 | tf_op jit(solution)/shard_map/ppermute | solution.py:64
  257.6 17.8 %collective-permute-start.30 = (bf16[256,768]{1,0:T(8,128)(2,1)S(1)}, bf16[256,768]{1,0:T(8,128)(2,1)S(1)}, u32[]{:S(2)}, u32[]{:S(2)}) collective-permute-start(bf16[256,768]{1,0:T(8,128)(2,1)S(1)} %get-tuple-element.250), channel_id=1, source_target_pairs={{16,0},{17,1},{18,2},{19,3},{20,4},{21,5},{22,6},{23,7},{24,8},{25... | collective-permute-start | bytes 1179656 | tf_op jit(solution)/shard_map/ppermute | solution.py:37
  258.9 24.9 %collective-permute-start.29 = (bf16[256,768]{1,0:T(8,128)(2,1)S(1)}, bf16[256,768]{1,0:T(8,128)(2,1)S(1)}, u32[]{:S(2)}, u32[]{:S(2)}) collective-permute-start(bf16[256,768]{1,0:T(8,128)(2,1)S(1)} %get-tuple-element.249), channel_id=1, source_target_pairs={{16,0},{17,1},{18,2},{19,3},{20,4},{21,5},{22,6},{23,7},{24,8},{25... | collective-permute-start | bytes 1179656 | tf_op jit(solution)/shard_map/ppermute | solution.py:37
  286.9 12.0 %collective-permute-start.31 = (bf16[1536,768]{1,0:T(8,128)(2,1)}, bf16[1536,768]{1,0:T(8,128)(2,1)S(1)}, u32[]{:S(2)}, u32[]{:S(2)}) collective-permute-start(bf16[1536,768]{1,0:T(8,128)(2,1)} %convolution_convert_fusion.1), channel_id=1, source_target_pairs={{0,4},{4,0},{1,5},{5,1},{2,6},{6,2},{3,7},{7,3},{8,12},{12,8},{9,1... | collective-permute-start | bytes 7077896 | tf_op jit(solution)/shard_map/ppermute | solution.py:33
  308.1 27.1 %collective-permute-start.34 = (bf16[768,768]{1,0:T(8,128)(2,1)S(1)}, bf16[768,768]{1,0:T(8,128)(2,1)S(1)}, u32[]{:S(2)}, u32[]{:S(2)}) collective-permute-start(bf16[768,768]{1,0:T(8,128)(2,1)S(1)} %slice.382), channel_id=1, source_target_pairs={{0,8},{8,0},{1,9},{9,1},{2,10},{10,2},{3,11},{11,3},{4,12},{12,4},... | collective-permute-start | bytes 3538952 | tf_op jit(solution)/shard_map/ppermute | solution.py:33
  314.8 20.4 %collective-permute-start.33 = (bf16[384,768]{1,0:T(8,128)(2,1)S(1)}, bf16[384,768]{1,0:T(8,128)(2,1)S(1)}, u32[]{:S(2)}, u32[]{:S(2)}) collective-permute-start(bf16[384,768]{1,0:T(8,128)(2,1)S(1)} %pad_maximum_fusion.5), channel_id=1, source_target_pairs={{0,2},{2,3},{3,1},{1,0},{4,6},{6,7},{7,5},{5,4},{8,10},{10,11},{11... | collective-permute-start | bytes 1769480 | tf_op jit(solution)/shard_map/ppermute | solution.py:29
  340.6 16.5 %collective-permute-start.36 = (bf16[384,768]{1,0:T(8,128)(2,1)}, bf16[384,768]{1,0:T(8,128)(2,1)}, u32[]{:S(2)}, u32[]{:S(2)}) collective-permute-start(bf16[384,768]{1,0:T(8,128)(2,1)} %add_convert_fusion.16), channel_id=1, source_target_pairs={{0,2},{2,3},{3,1},{1,0},{4,6},{6,7},{7,5},{5,4},{8,10},{10,11},{11... | collective-permute-start | bytes 1769480 | tf_op jit(solution)/shard_map/ppermute | solution.py:29
  349.8 9.7 %collective-permute-start.38 = (bf16[768,768]{1,0:T(8,128)(2,1)}, bf16[768,768]{1,0:T(8,128)(2,1)}, u32[]{:S(2)}, u32[]{:S(2)}) collective-permute-start(bf16[768,768]{1,0:T(8,128)(2,1)} %convolution_convert_fusion.3), channel_id=1, source_target_pairs={{0,4},{4,0},{1,5},{5,1},{2,6},{6,2},{3,7},{7,3},{8,12},{12,8},{9,1... | collective-permute-start | bytes 3538952 | tf_op jit(solution)/shard_map/ppermute | solution.py:33
  352.8 10.9 %collective-permute-start.37 = (bf16[768,768]{1,0:T(8,128)(2,1)}, bf16[768,768]{1,0:T(8,128)(2,1)}, u32[]{:S(2)}, u32[]{:S(2)}) collective-permute-start(bf16[768,768]{1,0:T(8,128)(2,1)} %convolution_convert_fusion.2), channel_id=1, source_target_pairs={{0,4},{4,0},{1,5},{5,1},{2,6},{6,2},{3,7},{7,3},{8,12},{12,8},{9,1... | collective-permute-start | bytes 3538952 | tf_op jit(solution)/shard_map/ppermute | solution.py:33
  358.4 17.7 %collective-permute-start.44 = (bf16[384,768]{1,0:T(8,128)(2,1)S(1)}, bf16[384,768]{1,0:T(8,128)(2,1)S(1)}, u32[]{:S(2)}, u32[]{:S(2)}) collective-permute-start(bf16[384,768]{1,0:T(8,128)(2,1)S(1)} %add_convert_fusion.15), channel_id=1, source_target_pairs={{0,2},{2,3},{3,1},{1,0},{4,6},{6,7},{7,5},{5,4},{8,10},{10,11},{11... | collective-permute-start | bytes 1769480 | tf_op jit(solution)/shard_map/ppermute | solution.py:29
  362.2 9.1 %collective-permute-start.39 = (bf16[192,768]{1,0:T(8,128)(2,1)S(1)}, bf16[192,768]{1,0:T(8,128)(2,1)S(1)}, u32[]{:S(2)}, u32[]{:S(2)}) collective-permute-start(bf16[192,768]{1,0:T(8,128)(2,1)S(1)} %get-tuple-element.240), channel_id=1, source_target_pairs={{0,8},{8,0},{1,9},{9,1},{2,10},{10,2},{3,11},{11,3},{4,12},{12,4},... | collective-permute-start | bytes 884744 | tf_op jit(solution)/shard_map/ppermute | solution.py:33
  363.0 22.9 %collective-permute-start.46 = (bf16[192,768]{1,0:T(8,128)(2,1)S(1)}, bf16[192,768]{1,0:T(8,128)(2,1)S(1)}, u32[]{:S(2)}, u32[]{:S(2)}) collective-permute-start(bf16[192,768]{1,0:T(8,128)(2,1)S(1)} %get-tuple-element.238), channel_id=1, source_target_pairs={{0,8},{8,0},{1,9},{9,1},{2,10},{10,2},{3,11},{11,3},{4,12},{12,4},... | collective-permute-start | bytes 884744 | tf_op jit(solution)/shard_map/ppermute | solution.py:33
  371.4 12.5 %collective-permute-start.43 = (bf16[192,768]{1,0:T(8,128)(2,1)S(1)}, bf16[192,768]{1,0:T(8,128)(2,1)S(1)}, u32[]{:S(2)}, u32[]{:S(2)}) collective-permute-start(bf16[192,768]{1,0:T(8,128)(2,1)S(1)} %get-tuple-element.144), channel_id=1, source_target_pairs={{0,8},{8,0},{1,9},{9,1},{2,10},{10,2},{3,11},{11,3},{4,12},{12,4},... | collective-permute-start | bytes 884744 | tf_op jit(solution)/shard_map/ppermute | solution.py:33
  372.6 13.3 %collective-permute-start.47 = (bf16[208,768]{1,0:T(8,128)(2,1)S(1)}, bf16[208,768]{1,0:T(8,128)(2,1)S(1)}, u32[]{:S(2)}, u32[]{:S(2)}) collective-permute-start(bf16[208,768]{1,0:T(8,128)(2,1)S(1)} %pad_maximum_fusion.12), channel_id=1, source_target_pairs={{0,2},{2,3},{3,1},{1,0},{4,6},{6,7},{7,5},{5,4},{8,10},{10,11},{11... | collective-permute-start | bytes 958472 | tf_op jit(solution)/shard_map/ppermute | solution.py:29
  384.1 9.2 %collective-permute-start.45 = (bf16[192,768]{1,0:T(8,128)(2,1)S(1)}, bf16[192,768]{1,0:T(8,128)(2,1)S(1)}, u32[]{:S(2)}, u32[]{:S(2)}) collective-permute-start(bf16[192,768]{1,0:T(8,128)(2,1)S(1)} %add_convert_fusion.24), channel_id=1, source_target_pairs={{0,2},{2,3},{3,1},{1,0},{4,6},{6,7},{7,5},{5,4},{8,10},{10,11},{11... | collective-permute-start | bytes 884744 | tf_op jit(solution)/shard_map/ppermute | solution.py:29
  384.1 13.7 %collective-permute-start.49 = (bf16[192,768]{1,0:T(8,128)(2,1)S(1)}, bf16[192,768]{1,0:T(8,128)(2,1)S(1)}, u32[]{:S(2)}, u32[]{:S(2)}) collective-permute-start(bf16[192,768]{1,0:T(8,128)(2,1)S(1)} %get-tuple-element.237), channel_id=1, source_target_pairs={{0,8},{8,0},{1,9},{9,1},{2,10},{10,2},{3,11},{11,3},{4,12},{12,4},... | collective-permute-start | bytes 884744 | tf_op jit(solution)/shard_map/ppermute | solution.py:33
  385.3 18.9 %collective-permute-start.51 = (bf16[2,192,768]{2,1,0:T(8,128)(2,1)S(1)}, bf16[2,192,768]{2,1,0:T(8,128)(2,1)S(1)}, u32[]{:S(2)}, u32[]{:S(2)}) collective-permute-start(bf16[2,192,768]{2,1,0:T(8,128)(2,1)S(1)} %bitcast.149), channel_id=1, source_target_pairs={{0,8},{8,0},{1,9},{9,1},{2,10},{10,2},{3,11},{11,3},{4,12},{12,4},... | collective-permute-start | bytes 1769480 | tf_op jit(solution)/shard_map/ppermute | solution.py:33
  394.0 14.0 %collective-permute-start.50 = (bf16[208,768]{1,0:T(8,128)(2,1)S(1)}, bf16[208,768]{1,0:T(8,128)(2,1)S(1)}, u32[]{:S(2)}, u32[]{:S(2)}) collective-permute-start(bf16[208,768]{1,0:T(8,128)(2,1)S(1)} %add_convert_fusion.19), channel_id=1, source_target_pairs={{0,2},{2,3},{3,1},{1,0},{4,6},{6,7},{7,5},{5,4},{8,10},{10,11},{11... | collective-permute-start | bytes 958472 | tf_op jit(solution)/shard_map/ppermute | solution.py:29
  409.0 31.2 %collective-permute-start.52 = (bf16[256,768]{1,0:T(8,128)(2,1)}, bf16[256,768]{1,0:T(8,128)(2,1)}, u32[]{:S(2)}, u32[]{:S(2)}) collective-permute-start(bf16[256,768]{1,0:T(8,128)(2,1)} %get-tuple-element.248), channel_id=1, source_target_pairs={{0,0},{4,1},{1,4},{5,5},{8,8},{12,9},{9,12},{13,13},{2,16},{6,17},... | collective-permute-start | bytes 1179656 | tf_op jit(solution)/shard_map/ppermute | solution.py:64
  415.5 27.6 %collective-permute-start.53 = (bf16[256,768]{1,0:T(8,128)(2,1)}, bf16[256,768]{1,0:T(8,128)(2,1)}, u32[]{:S(2)}, u32[]{:S(2)}) collective-permute-start(bf16[256,768]{1,0:T(8,128)(2,1)} %get-tuple-element.247), channel_id=1, source_target_pairs={{0,3},{4,2},{1,7},{5,6},{8,11},{12,10},{9,15},{13,14},{2,19},{6,18... | collective-permute-start | bytes 1179656 | tf_op jit(solution)/shard_map/ppermute | solution.py:64
  417.5 20.1 %collective-permute-start.54 = (bf16[208,768]{1,0:T(8,128)(2,1)S(1)}, bf16[208,768]{1,0:T(8,128)(2,1)S(1)}, u32[]{:S(2)}, u32[]{:S(2)}) collective-permute-start(bf16[208,768]{1,0:T(8,128)(2,1)S(1)} %add_convert_fusion.18), channel_id=1, source_target_pairs={{0,2},{2,3},{3,1},{1,0},{4,6},{6,7},{7,5},{5,4},{8,10},{10,11},{11... | collective-permute-start | bytes 958472 | tf_op jit(solution)/shard_map/ppermute | solution.py:29
  417.7 8.9 %collective-permute-start.55 = (bf16[192,768]{1,0:T(8,128)(2,1)S(1)}, bf16[192,768]{1,0:T(8,128)(2,1)S(1)}, u32[]{:S(2)}, u32[]{:S(2)}) collective-permute-start(bf16[192,768]{1,0:T(8,128)(2,1)S(1)} %add_convert_fusion.20), channel_id=1, source_target_pairs={{0,8},{8,0},{1,9},{9,1},{2,10},{10,2},{3,11},{11,3},{4,12},{12,4},... | collective-permute-start | bytes 884744 | tf_op jit(solution)/shard_map/ppermute | solution.py:33
  419.1 25.7 %collective-permute-start.57 = (bf16[384,768]{1,0:T(8,128)(2,1)S(1)}, bf16[384,768]{1,0:T(8,128)(2,1)S(1)}, u32[]{:S(2)}, u32[]{:S(2)}) collective-permute-start(bf16[384,768]{1,0:T(8,128)(2,1)S(1)} %pad_maximum_fusion.9), channel_id=1, source_target_pairs={{0,4},{4,0},{1,5},{5,1},{2,6},{6,2},{3,7},{7,3},{8,12},{12,8},{9,1... | collective-permute-start | bytes 1769480 | tf_op jit(solution)/shard_map/ppermute | solution.py:33
  427.4 21.6 %collective-permute-start.56 = (bf16[384,768]{1,0:T(8,128)(2,1)}, bf16[384,768]{1,0:T(8,128)(2,1)}, u32[]{:S(2)}, u32[]{:S(2)}) collective-permute-start(bf16[384,768]{1,0:T(8,128)(2,1)} %pad_maximum_fusion.8), channel_id=1, source_target_pairs={{0,4},{4,0},{1,5},{5,1},{2,6},{6,2},{3,7},{7,3},{8,12},{12,8},{9,1... | collective-permute-start | bytes 1769480 | tf_op jit(solution)/shard_map/ppermute | solution.py:33
  (116 other events, 1714.2 us)

commit v3 on v2

--- a/solution.py
+++ b/solution.py
@@ -80,6 +80,10 @@
 
 def nn(left, right):
     return lax.dot_general(left, right, (((1,), (0,)), ((), ())), preferred_element_type=F32)
+
+
+def estimate(flops, size):
+    return pl.CostEstimate(flops=flops, bytes_accessed=size, transcendentals=0)
 
 
 def head_mask(rows, head):
@@ -258,9 +262,7 @@
         in_specs=[pl.BlockSpec(memory_space=pltpu.SMEM)] + [column] * 5,
         out_specs=outs,
         compiler_params=pltpu.CompilerParams(vmem_limit_bytes=40 * 1024 * 1024),
-        cost_estimate=pl.CostEstimate(
-            flops=20 * rows * rows * width * 2, bytes_accessed=16 * length * width, transcendentals=0
-        ),
+        cost_estimate=estimate(20 * rows * rows * width * 2, 16 * length * width),
         name="attend",
     )(core, q, k, v, k_other, v_other)
 
@@ -284,9 +286,7 @@
         + [pl.BlockSpec((2, 5, rows, rows), lambda i: (i, 0, 0, 0))],
         out_specs=[column, double, double, pl.BlockSpec((8, LANES), lambda i: (0, i))],
         compiler_params=pltpu.CompilerParams(vmem_limit_bytes=40 * 1024 * 1024),
-        cost_estimate=pl.CostEstimate(
-            flops=40 * rows * rows * width * 2, bytes_accessed=40 * length * width, transcendentals=0
-        ),
+        cost_estimate=estimate(40 * rows * rows * width * 2, 40 * length * width),
         name="attend_back",
     )(core, q, k, v, k_other, v_other, grad_mixed, mixed, weights)
 
@@ -344,9 +344,7 @@
         in_specs=[taken, weight, pl.BlockSpec((1, tile), lambda i: (0, i)), weight, taken],
         out_specs=whole,
         compiler_params=pltpu.CompilerParams(vmem_limit_bytes=40 * 1024 * 1024),
-        cost_estimate=pl.CostEstimate(
-            flops=4 * length * width * units, bytes_accessed=4 * width * units, transcendentals=0
-        ),
+        cost_estimate=estimate(4 * length * width * units, 4 * width * units),
         name="feed_half",
     )(rows, expand_w, bias.reshape(1, units), reduce_w, start)
 
@@ -439,9 +437,7 @@
         in_specs=[whole, whole, *weight, *row, *weight],
         out_specs=[whole, whole, *across, *across],
         compiler_params=pltpu.CompilerParams(vmem_limit_bytes=40 * 1024 * 1024),
-        cost_estimate=pl.CostEstimate(
-            flops=16 * length * width * units, bytes_accessed=8 * width * units, transcendentals=0
-        ),
+        cost_estimate=estimate(16 * length * width * units, 8 * width * units),
         name="feed_both",
     )(rows, grad, e0, e1, b0.reshape(1, units), b1.reshape(1, units), r0, r1)
 
@@ -460,9 +456,7 @@
         in_specs=[whole, *weight, *weight, *across],
         out_specs=[whole, *across, *rows],
         compiler_params=pltpu.CompilerParams(vmem_limit_bytes=40 * 1024 * 1024),
-        cost_estimate=pl.CostEstimate(
-            flops=8 * length * width * units, bytes_accessed=8 * width * units, transcendentals=0
-        ),
+        cost_estimate=estimate(8 * length * width * units, 8 * width * units),
         name="feed_back",
     )(grad, e0, e1, r0, r1, *slope)
 
@@ -494,7 +488,7 @@
     q = narrow(nt(ready_one, proj[0]) + bias_q)
     if before:
         q, *before = lax.optimization_barrier((q, *before))
-        after = [*after[:-2], *after[-1](before)]
+        after = after(before)
     mixed, *kept_weights = attend(core, q, k, v, k_other, v_other, keep)
     mixed, *after = lax.optimization_barrier((mixed, *after))
     middle = rows_in + BRANCH * (nn(mixed, proj[3]) + bias_out)
@@ -613,16 +607,19 @@
     while len(pieces) < count - 1:
         pieces_y.append(swap(pieces[-1][:local], "y"))
         pieces.append(ring(pieces[-1]))
-        pieces[-1], pieces_y[-1], feed[0], *arrived = lax.optimization_barrier(
-            (pieces[-1], pieces_y[-1], feed[0], *arrived)
-        )
-        if len(pieces) == count - 1:
-            feed.append(ring(feed[0]))
+        if len(pieces) < count - 1:
+            pieces[-1], pieces_y[-1], feed[0], *arrived = lax.optimization_barrier(
+                (pieces[-1], pieces_y[-1], feed[0], *arrived)
+            )
+    feed.append(ring(feed[0]))
+    pieces[-1], pieces_y[-1] = lax.optimization_barrier((pieces[-1], pieces_y[-1]))
     pieces_y.append(swap(pieces[-1][:local], "y"))
     feed[1], pieces_y[-1] = lax.optimization_barrier((feed[1], pieces_y[-1]))
     feed_y.append(swap(feed[1], "y"))
     feed.append(ring(feed[1]))
-    before = (feed[2], feed_y[1])
+    feed[2], feed_y[1] = lax.optimization_barrier((feed[2], feed_y[1]))
+    feed_y.append(swap(feed[2], "y"))
+    before = (ring(feed[2]), feed_y[2])
     bias_rows += [value[local:] for value in pieces]
     pieces = [mine] + [value[:local] for value in pieces]
     pieces_y = [mine_y] + pieces_y
@@ -641,10 +638,10 @@
     rows_in = jnp.concatenate(arrived)
     middle, _, after = attention_forward(
         core, rows_in.astype(F32), attention_weights, False, before,
-        (before, lambda ready: (ring(ready[0]), swap(ready[0], "y"))),
+        lambda ready: (*ready, swap(ready[0], "y")),
     )
     feed.append(after[0])
-    feed_y += [after[1], swap(after[0], "y")]
+    feed_y[2:] = after[1:]
     own_half = [
         jnp.concatenate([value[kind * part : (kind + 1) * part] for value in feed + feed_y]) for kind in range(2)
     ]
@@ -656,9 +653,12 @@
         reduce_bias[0],
     )
     passed = jnp.concatenate([along_pipe(rows, 1) for rows in feed_forward_only(middle, feed_weights)])
-    last = jnp.concatenate(fetch(tie(cotangent[0, 0], passed), 1))
+    last = fetch(tie(cotangent[0, 0], passed), 1)
     rows_in = jnp.where(is_first, rows_in, passed)
-    middle, kept_attention, _ = attention_forward(core, rows_in.astype(F32), attention_weights, True)
+    middle, kept_attention, last = attention_forward(
+        core, rows_in.astype(F32), attention_weights, True, (), last
+    )
+    last = jnp.concatenate(last)
     result, grad_middle, kept_feed = feed_forward_and_back(middle, last.astype(F32), feed_weights)
     block = result.shape[0] // 2
     outputs = give_back(result[:block], result[block:], 1)
@@ -692,10 +692,11 @@
     send = narrow(tn(hidden[1], rounded_outcome))
     arrived = swap(send, "core")
     keep = tn(hidden[0], tie(rounded_outcome, send))
-    total, pre_own, pre_other, sums_own, sums_other = feed_back(tie(rounded_outcome, keep), feed_weights[2], slope)
-    reduce_sums = wide_add(keep, tie(arrived, total))
+    reduce_sums = wide_add(keep, tie(arrived, keep))
     reduce_y = swap(reduce_sums[span:], "y")
-    total = tie(total, reduce_sums)
+    total, pre_own, pre_other, sums_own, sums_other = feed_back(
+        tie(rounded_outcome, reduce_sums), feed_weights[2], slope
+    )
     grad_middle = grad_result + norm_backward(total, normed_two, inverse_two, gain_two[0])
     shared_feed = [total * normed_two, total, grad_outcome]
     send = narrow(tn(tie(pre_other, grad_middle), ready_two))
@@ -712,7 +713,7 @@
     reduce_start, reduce_finish = steps_of(reduce_parts)
     grad_qkv = lax.optimization_barrier((*grad_qkv, expand_step, *reduce_parts))[:3]
     grad_in = narrow(grad_in)
-    expand_step = expand_start()
+    moving_e, moving_r = expand_start(), reduce_start()
     mixed, ready_one = kept_attention[4], kept_attention[2]
     left = jnp.stack([*grad_qkv, mixed])
     index = 2 * c + y
@@ -725,8 +726,9 @@
     arrived = [swap(value, "core") for value in send]
     left = tie(left, *send)
     keep = [typed_grad(shift) for shift in (1, 0)]
-    expand_step, keep[1] = lax.optimization_barrier((expand_step, keep[1]))
-    expand_step = expand_finish(expand_step, 2)
+    moving_e, moving_r, *keep = lax.optimization_barrier((moving_e, moving_r, *keep))
+    expand_finish(moving_e, 2)
+    reduce_finish(moving_r, 1)
     shared = shared_attention + shared_feed
     shared = jnp.stack([jnp.sum(value, axis=0) for value in shared])
     sums_qv = sums_qv.reshape(2, count, local)
@@ -745,49 +747,49 @@
     def typed_swap(slot):
         return swap(to_y[slot], "y")
 
-    moving_y, moving_e, vectors_y = typed_swap(1), expand_start(), swap(vectors, "y")
-    moving_y, vectors_y, to_y[2] = lax.optimization_barrier((moving_y, vectors_y, to_y[2]))
-    typed_parts[1] = wide_add(to_keep[1], moving_y)
+    moving_y, moving_z, vectors_y = typed_swap(1), typed_swap(2), swap(vectors, "y")
+    moving_e, moving_r = expand_start(), reduce_start()
+    moving_y, vectors_y, to_y[3], to_y[0] = lax.optimization_barrier((moving_y, vectors_y, to_y[3], to_y[0]))
     vectors = narrow(vectors + vectors_y)
-    reduce_parts = [jnp.concatenate([a, b]) for a, b in zip(reduce_parts, vectors)]
-    reduce_start, reduce_finish = steps_of(reduce_parts)
+
+    def typed_part(slot, arrived):
+        typed_parts[slot] = jnp.concatenate([wide_add(to_keep[slot], arrived), vectors[slot]])
+
+    typed_part(1, moving_y)
     typed_start, typed_finish = steps_of(typed_parts)
-    moving_t, moving_y, moving_r = typed_start(), typed_swap(2), reduce_start()
-    moving_t, moving_y, moving_e = lax.optimization_barrier((moving_t, moving_y, moving_e))
-    typed_parts[2] = wide_add(to_keep[2], moving_y)
+    moving_t, moving_y = typed_start(), typed_swap(3)
+    moving_t, moving_z, moving_e, moving_r = lax.optimization_barrier((moving_t, moving_z, moving_e, moving_r))
+    typed_part(2, moving_z)
     typed_finish(moving_t, 1)
+    reduce_finish(moving_r, 2)
     expand_total = expand_finish(moving_e, 3).reshape(2, part, width)
-    moving_t, moving_y, expand_other = typed_start(), typed_swap(3), swap(expand_total, "y")
+    moving_t, moving_z, moving_r = typed_start(), typed_swap(0), reduce_start()
     moving_t, moving_y, moving_r = lax.optimization_barrier((moving_t, moving_y, moving_r))
-    typed_parts[3] = wide_add(to_keep[3], moving_y)
+    typed_part(3, moving_y)
     typed_finish(moving_t, 2)
-    reduce_finish(moving_r, 1)
-    moving_t, moving_y, moving_r = typed_start(), typed_swap(0), reduce_start()
-    moving_t, moving_y, moving_r, expand_other = lax.optimization_barrier((moving_t, moving_y, moving_r, expand_other))
-    typed_parts[0] = wide_add(to_keep[0], moving_y)
-    typed_total = typed_finish(moving_t, 3)
-    reduce_finish(moving_r, 2)
-    reduce_total = reduce_finish(reduce_start(), 3)
-    grad_in = tie(grad_in, moving_t)
+    reduce_total = over_groups(reduce_finish(moving_r, 3))
+    moving_t, expand_other = typed_start(), swap(expand_total, "y")
+    moving_t, moving_z, grad_in, expand_other = lax.optimization_barrier((moving_t, moving_z, grad_in, expand_other))
+    typed_part(0, moving_z)
+    typed_total = over_groups(typed_finish(moving_t, 3))
+    typed_other, reduce_other = swap(typed_total[:local], "y"), swap(reduce_total, "y")
     input_grad = give_back(grad_in[:block], grad_in[block:], 0)
+    typed_other, reduce_other = lax.optimization_barrier((typed_other, reduce_other))
     def gathered(pair):
         pair = jnp.concatenate(pair)
         blocks = quarters(jnp.concatenate([pair, swap(pair, "core")]), 0)
         return jnp.concatenate(blocks[0] + blocks[1])
 
+    pair = jnp.concatenate([typed_total[:local], typed_other])
+    pair_other = swap(pair, "core")
     grad_expand = [over_groups(wide_add(expand_total[i], expand_other[1 - i])) for i in range(2)]
     grad_expand = gathered(grad_expand).T.astype(F32)
-    typed_total = over_groups(typed_total)
-    pair = jnp.concatenate([typed_total, swap(typed_total, "y")])
-    pair_other = swap(pair, "core")
+    grad_reduce = gathered([reduce_total, reduce_other]).astype(F32)
     whole = relative([pair[:local], pair[local:], pair_other[:local], pair_other[local:]])
     whole = [*whole[0], *whole[1]]
     grad_attend_in = jnp.stack(whole[:3]).transpose(2, 0, 1).astype(F32)
     grad_attend_out = whole[3].astype(F32)
-    reduce_total = over_groups(reduce_total)
-    vectors = reduce_total[part : part + 8].astype(F32)
-    reduce_total = reduce_total[:part]
-    grad_reduce = gathered([reduce_total, swap(reduce_total, "y")]).astype(F32)
+    vectors = typed_total[local : local + 8].astype(F32)
     return (
         outputs[None, None],
         input_grad[None, None],

time: 464 us -> 434 us (0.935)
  waiting for transfers between devices: 173 us -> 150 us
  starting transfers between devices: 70.6 us -> 63.8 us
    ppermute x4, waiting for transfers between devices: 42.9 us -> 14.3 us  [fetch(): lax.ppermute(block, AXES, routes(section, large))]
    ppermute x15, waiting for transfers between devices: 49.6 us -> 62.7 us  [ring(): lax.ppermute(value, 'tensor', list(zip(order, order[1:] + order[:1])))]
    ppermute x33, waiting for transfers between devices: 43.3 us -> 31.4 us  [swap(): return lax.ppermute(value, axis, [(0, 1), (1, 0)])]
    ppermute x4, waiting for transfers between devices: 3.17 us -> 9.95 us  [give_back(): pieces.append(lax.ppermute(rows, AXES, pairs))]
    unnamed x226 -> x238, local copies, waits for them, and re-layouts: 20 us -> 22.9 us
    convert_element_type x29 -> x33, other arithmetic: 15.7 us -> 15.1 us  [narrow(): return value.astype(BF16)]
  transfers between devices with their start and end apart: 60 -> 60, of which waited for: 28 -> 27; matrix products, arithmetic and copies ran while one was open for 16% -> 19% of each run, Pallas kernels for 13% -> 15%
where the time goes in v3:
time: 434 us; the launch traced here: 429 us
  waiting for transfers between devices  150 us (35%)
  Pallas kernels  95 us (22%)
  starting transfers between devices  63.8 us (15%)
  other arithmetic  47 us (11%)
  local copies, waits for them, and re-layouts  36.8 us (8%)
  matrix products  33.5 us (8%)
    ppermute x15, waiting for transfers between devices, ring(): lax.ppermute(value, 'tensor', list(zip(order, order[1:] + order[:1])))  62.7 us
    ppermute x4, waiting for transfers between devices, along_pipe(): return lax.ppermute(value, 'pipe', [(0, 1)] if by > 0 else [(1, 0)])  31.7 us
    ppermute x33, waiting for transfers between devices, swap(): return lax.ppermute(value, axis, [(0, 1), (1, 0)])  31.4 us
    pallas_call x2, Pallas kernels, attend_back(): pl.pallas_call(attend_back_kernel, grid=(width // LANES,), out_shape=[jax...  29.8 us
    pallas_call x2, Pallas kernels, attend(): pl.pallas_call(functools.partial(attend_kernel, keep_weights), grid=(widt...  24.2 us
    ppermute x33, starting transfers between devices, swap(): return lax.ppermute(value, axis, [(0, 1), (1, 0)])  23.8 us
    unnamed x238, local copies, waits for them, and re-layouts  22.9 us
    pallas_call x1, Pallas kernels, feed_both(): pl.pallas_call(functools.partial(both_kernel, steps), grid=(2 * steps,),...  16.5 us
  transfers between devices with their start and end apart: 60, of which 27 were waited for; matrix products, arithmetic and copies ran while one was open for 19% of the time, Pallas kernels for 15%

profile of v3, /device:TPU:17, one launch (start us, length us, event | category | flops | bytes accessed | tf_op | source)
XLA Modules:
  0.0 429.1 jit_solution(11415740058487307981)
XLA Ops:
  2.1 2.4 collective-permute-start.4
  6.1 2.1 select_bitcast_fusion.8
  9.0 2.0 collective-permute-start
  14.1 4.2 collective-permute-done
  20.5 4.3 collective-permute-start.1
  25.6 11.3 %collective-permute-done.3 = bf16[256,768]{1,0:T(8,128)(2,1)S(1)} collective-permute-done((bf16[256,768]{1,0:T(8,128)(2,1)}, bf16[256,768]{1,0:T(8,128)(2,1)S(1)}, u32[]{:S(2)}, u32[]{:S(2)}) %collective-permute-start.3) | collective-permute-done | bytes 393248 | tf_op jit(solution)/shard_map/ppermute | solution.py:57
  42.4 3.6 collective-permute-done.6
  50.7 9.1 %collective-permute-done.7 = bf16[384,768]{1,0:T(8,128)(2,1)} collective-permute-done((bf16[384,768]{1,0:T(8,128)(2,1)S(1)}, bf16[384,768]{1,0:T(8,128)(2,1)}, u32[]{:S(2)}, u32[]{:S(2)}) %collective-permute-start.7) | collective-permute-done | bytes 589856 | tf_op jit(solution)/shard_map/ppermute | solution.py:29
  68.0 9.5 %collective-permute-done.11 = bf16[384,768]{1,0:T(8,128)(2,1)} collective-permute-done((bf16[384,768]{1,0:T(8,128)(2,1)}, bf16[384,768]{1,0:T(8,128)(2,1)}, u32[]{:S(2)}, u32[]{:S(2)}) %collective-permute-start.11) | collective-permute-done | bytes 589856 | tf_op jit(solution)/shard_map/ppermute | solution.py:29
  79.2 2.7 broadcast_select_fusion.6
  89.1 3.5 collective-permute-done.13
  97.5 11.3 %attend.2 = bf16[512,768]{1,0:T(8,128)(2,1)S(1)} custom-call(s32[1]{0:T(128)} %bitcast.core_ref, bf16[512,768]{1,0:T(8,128)(2,1)S(1)} %add_convert_fusion.13.q_ref, bf16[512,768]{1,0:T(8,128)(2,1)S(1)} %convolution_convert_fusion.7.k_ref, bf16[512,768]{1,0:T(8,128)(2,1)S(1)} %add_convert_fusion.12.v_ref, ...), custom_call_target="tpu_custom_call" | custom-call | flops 2013265920 | bytes 6291456 | tf_op jit(solution)/shard_map/attend/pallas_call | solution.py:258
  116.0 2.1 collective-permute-start.18
  118.5 2.2 broadcast_select_fusion.4
  123.8 5.6 %feed_half.3.start_ref = f32[512,768]{1,0:T(8,128)S(1)} custom-call(bf16[512,768]{1,0:T(8,128)(2,1)S(1)} %add_convert_fusion.11.rows_ref, bf16[1536,768]{1,0:T(8,128)(2,1)} %get-tuple-element.266.expand_ref.e0_ref, f32[1,1536]{1,0:T(1,128)S(1)} %reshape.403.bias_ref.b0_ref, bf16[1536,768]{1,0:T(8,128)(2,1)S(1)} %copy-done.7, ...), custom_call_target="tpu_custom_call" | custom-call | flops 2415919104 | bytes 4718592 | tf_op jit(solution)/shard_map/feed_half/pallas_call | solution.py:340
  129.4 4.7 %feed_half.4 = f32[256,768]{1,0:T(8,128)S(1)} custom-call(bf16[512,768]{1,0:T(8,128)(2,1)S(1)} %add_convert_fusion.11.rows_ref, bf16[1536,768]{1,0:T(8,128)(2,1)S(1)} %collective-permute-done.18.expand_ref.e1_ref, f32[1,1536]{1,0:T(1,128)S(1)} %reshape.400.bias_ref.b1_ref, bf16[1536,768]{1,0:T(8,128)(2,1)} %collective-permute-done.19.reduce_ref.r1_ref, ...), custom_call_target="tpu_custom_call" | custom-call | flops 1207959552 | bytes 4718592 | tf_op jit(solution)/shard_map/feed_half/pallas_call | solution.py:340
  136.2 4.1 feed_half.5
  142.1 2.0 collective-permute-done.20
  144.2 8.4 %collective-permute-done.21 = bf16[256,768]{1,0:T(8,128)(2,1)S(1)} collective-permute-done((bf16[256,768]{1,0:T(8,128)(2,1)S(1)}, bf16[256,768]{1,0:T(8,128)(2,1)S(1)}, u32[]{:S(2)}, u32[]{:S(2)}) %collective-permute-start.21) | collective-permute-done | bytes 393248 | tf_op jit(solution)/shard_map/ppermute | solution.py:37
  158.3 7.5 %collective-permute-start.25 = (bf16[256,768]{1,0:T(8,128)(2,1)}, bf16[256,768]{1,0:T(8,128)(2,1)S(1)}, u32[]{:S(2)}, u32[]{:S(2)}) collective-permute-start(bf16[256,768]{1,0:T(8,128)(2,1)} %bitcast.157), channel_id=1, source_target_pairs={{3,16},{2,20},{7,17},{6,21},{11,24},{10,28},{15,25},{14,29},{19,18... | collective-permute-start | bytes 1179656 | tf_op jit(solution)/shard_map/ppermute | solution.py:57
  165.8 2.4 add_convert_fusion.10.q_ref
  168.3 12.9 %attend.3 = (bf16[512,768]{1,0:T(8,128)(2,1)S(1)}, bf16[12,5,256,256]{3,2,1,0:T(8,128)(2,1)}) custom-call(s32[1]{0:T(128)} %bitcast.core_ref, bf16[512,768]{1,0:T(8,128)(2,1)S(1)} %add_convert_fusion.10.q_ref, bf16[512,768]{1,0:T(8,128)(2,1)S(1)} %convolution_convert_fusion.6.k_ref, bf16[512,768]{1,0:T(8,128)(2,1)S(1)} %add_convert_fusion.9.v_ref, ...), custom_call_target="tpu_custom_call" | custom-call | flops 2013265920 | bytes 6291456 | tf_op jit(solution)/shard_map/attend/pallas_call | solution.py:258
  181.2 2.9 collective-permute-done.25
  185.9 16.5 %feed_both.1 = (f32[512,768]{1,0:T(8,128)S(1)}, f32[512,768]{1,0:T(8,128)S(1)}, bf16[512,1536]{1,0:T(8,128)(2,1)S(1)}, bf16[512,1536]{1,0:T(8,128)(2,1)S(1)}, bf...) custom-call(bf16[512,768]{1,0:T(8,128)(2,1)S(1)} %add_convert_fusion.8.rows_ref, ...), custom_call_target="tpu_custom_call" | custom-call | flops 9663676416 | bytes 9437184 | tf_op jit(solution)/shard_map/feed_both/pallas_call | solution.py:433
  207.3 15.0 %attend_back.2 = (bf16[512,768]{1,0:T(8,128)(2,1)S(1)}, f32[2,512,768]{2,1,0:T(8,128)S(1)}, bf16[2,512,768]{2,1,0:T(8,128)(2,1)S(1)}, f32[8,768]{1,0:T(8,128)}) custom-call(s32[1]{0:T(128)} %bitcast.core_ref, bf16[512,768]{1,0:T(8,128)(2,1)S(1)} %add_convert_fusion.10.q_ref, bf16[512,768]{1,0:T(8,128)(2,1)S(1)} %convolution_convert_fusion.6.k_ref, ...), custom_call_target="tpu_custom_call" | custom-call | flops 4026531840 | bytes 15728640 | tf_op jit(solution)/shard_map/attend_back/pallas_call | solution.py:275
  222.3 2.4 collective-permute-done.27
  225.4 2.0 fusion.90
  235.9 12.9 %collective-permute-done.30 = bf16[256,768]{1,0:T(8,128)(2,1)S(1)} collective-permute-done((bf16[256,768]{1,0:T(8,128)(2,1)S(1)}, bf16[256,768]{1,0:T(8,128)(2,1)S(1)}, u32[]{:S(2)}, u32[]{:S(2)}) %collective-permute-start.30) | collective-permute-done | bytes 393248 | tf_op jit(solution)/shard_map/ppermute | solution.py:37
  248.8 8.4 %collective-permute-done.29 = bf16[256,768]{1,0:T(8,128)(2,1)S(1)} collective-permute-done((bf16[256,768]{1,0:T(8,128)(2,1)S(1)}, bf16[256,768]{1,0:T(8,128)(2,1)S(1)}, u32[]{:S(2)}, u32[]{:S(2)}) %collective-permute-start.29) | collective-permute-done | bytes 393248 | tf_op jit(solution)/shard_map/ppermute | solution.py:37
  261.5 2.6 collective-permute-done.31
  264.9 10.2 %feed_back.1 = (f32[512,768]{1,0:T(8,128)S(1)}, bf16[512,1536]{1,0:T(8,128)(2,1)S(1)}, bf16[512,1536]{1,0:T(8,128)(2,1)S(1)}, f32[8,1536]{1,0:T(8,128)S(1)}, f32[8,1536]{1,0:T(8,128)S(1)}) custom-call(bf16[512,768]{1,0:T(8,128)(2,1)S(1)} %fusion.1.grad_ref, bf16[1536,768]{1,0:T(8,128)(2,1)} %get-tuple-element.266.expand_ref.e0_ref, ...), custom_call_target="tpu_custom_call" | custom-call | flops 4831838208 | bytes 9437184 | tf_op jit(solution)/shard_map/feed_back/pallas_call | solution.py:452
  280.3 2.2 collective-permute-done.32
  286.5 14.8 %attend_back.3 = (bf16[512,768]{1,0:T(8,128)(2,1)S(1)}, f32[2,512,768]{2,1,0:T(8,128)S(1)}, bf16[2,512,768]{2,1,0:T(8,128)(2,1)}, f32[8,768]{1,0:T(8,128)S(1)}) custom-call(s32[1]{0:T(128)} %bitcast.core_ref, bf16[512,768]{1,0:T(8,128)(2,1)S(1)} %add_convert_fusion.10.q_ref, bf16[512,768]{1,0:T(8,128)(2,1)S(1)} %copy-done.9, ...), custom_call_target="tpu_custom_call" | custom-call | flops 4026531840 | bytes 15728640 | tf_op jit(solution)/shard_map/attend_back/pallas_call | solution.py:275
  302.2 3.9 collective-permute-done.34
  307.8 2.4 fusion.93
  318.7 2.1 convolution_convert_fusion.3
  320.8 2.1 convolution_convert_fusion.2
  323.4 2.4 fusion.37
  327.7 6.0 %collective-permute-done.36 = bf16[192,768]{1,0:T(8,128)(2,1)S(1)} collective-permute-done((bf16[192,768]{1,0:T(8,128)(2,1)S(1)}, bf16[192,768]{1,0:T(8,128)(2,1)S(1)}, u32[]{:S(2)}, u32[]{:S(2)}) %collective-permute-start.36) | collective-permute-done | bytes 294944 | tf_op jit(solution)/shard_map/ppermute | solution.py:29
  333.7 2.4 fusion.20
  345.2 6.3 %collective-permute-done.40 = bf16[192,768]{1,0:T(8,128)(2,1)S(1)} collective-permute-done((bf16[192,768]{1,0:T(8,128)(2,1)S(1)}, bf16[192,768]{1,0:T(8,128)(2,1)S(1)}, u32[]{:S(2)}, u32[]{:S(2)}) %collective-permute-start.40) | collective-permute-done | bytes 294944 | tf_op jit(solution)/shard_map/ppermute | solution.py:33
  353.8 13.3 %collective-permute-done.46 = bf16[192,768]{1,0:T(8,128)(2,1)S(1)} collective-permute-done((bf16[192,768]{1,0:T(8,128)(2,1)S(1)}, bf16[192,768]{1,0:T(8,128)(2,1)S(1)}, u32[]{:S(2)}, u32[]{:S(2)}) %collective-permute-start.46) | collective-permute-done | bytes 294944 | tf_op jit(solution)/shard_map/ppermute | solution.py:29
  369.2 12.4 %collective-permute-done.49 = bf16[192,768]{1,0:T(8,128)(2,1)S(1)} collective-permute-done((bf16[192,768]{1,0:T(8,128)(2,1)S(1)}, bf16[192,768]{1,0:T(8,128)(2,1)S(1)}, u32[]{:S(2)}, u32[]{:S(2)}) %collective-permute-start.49) | collective-permute-done | bytes 294944 | tf_op jit(solution)/shard_map/ppermute | solution.py:29
  382.9 3.0 collective-permute-done.52
  386.0 3.1 collective-permute-done.50
  390.2 6.8 %collective-permute-start.53 = (bf16[256,768]{1,0:T(8,128)(2,1)}, bf16[256,768]{1,0:T(8,128)(2,1)S(1)}, u32[]{:S(2)}, u32[]{:S(2)}) collective-permute-start(bf16[256,768]{1,0:T(8,128)(2,1)} %get-tuple-element.260), channel_id=1, source_target_pairs={{0,0},{4,1},{1,4},{5,5},{8,8},{12,9},{9,12},{13,13},{2,16},{6,17},... | collective-permute-start | bytes 1179656 | tf_op jit(solution)/shard_map/ppermute | solution.py:64
  401.0 6.8 %collective-permute-done.55 = bf16[192,768]{1,0:T(8,128)(2,1)S(1)} collective-permute-done((bf16[192,768]{1,0:T(8,128)(2,1)S(1)}, bf16[192,768]{1,0:T(8,128)(2,1)S(1)}, u32[]{:S(2)}, u32[]{:S(2)}) %collective-permute-start.55) | collective-permute-done | bytes 294944 | tf_op jit(solution)/shard_map/ppermute | solution.py:33
  410.4 7.4 %collective-permute-done.54 = bf16[256,768]{1,0:T(8,128)(2,1)} collective-permute-done((bf16[256,768]{1,0:T(8,128)(2,1)}, bf16[256,768]{1,0:T(8,128)(2,1)}, u32[]{:S(2)}, u32[]{:S(2)}) %collective-permute-start.54) | collective-permute-done | bytes 393248 | tf_op jit(solution)/shard_map/ppermute | solution.py:64
  (502 shorter events, 137.8 us)
Async XLA Ops:
  0.7 36.3 %collective-permute-start.3 = (bf16[256,768]{1,0:T(8,128)(2,1)}, bf16[256,768]{1,0:T(8,128)(2,1)S(1)}, u32[]{:S(2)}, u32[]{:S(2)}) collective-permute-start(bf16[256,768]{1,0:T(8,128)(2,1)} %bitcast.154), channel_id=1, source_target_pairs={{0,0},{1,4},{4,1},{5,5},{8,8},{9,12},{12,9},{13,13},{16,2},{17,6},... | collective-permute-start | bytes 1179656 | tf_op jit(solution)/shard_map/ppermute | solution.py:57
  2.1 34.9 %collective-permute-start.4 = (bf16[256,768]{1,0:T(8,128)(2,1)}, bf16[256,768]{1,0:T(8,128)(2,1)}, u32[]{:S(2)}, u32[]{:S(2)}) collective-permute-start(bf16[256,768]{1,0:T(8,128)(2,1)} %bitcast.155), channel_id=1, source_target_pairs={{3,0},{2,4},{7,1},{6,5},{11,8},{10,12},{15,9},{14,13},{19,2},{18,6... | collective-permute-start | bytes 1179656 | tf_op jit(solution)/shard_map/ppermute | solution.py:57
  19.2 17.7 %collective-permute-start.2 = (bf16[192,768]{1,0:T(8,128)(2,1)S(1)}, bf16[192,768]{1,0:T(8,128)(2,1)S(1)}, u32[]{:S(2)}, u32[]{:S(2)}) collective-permute-start(bf16[192,768]{1,0:T(8,128)(2,1)S(1)} %slice.370), channel_id=1, source_target_pairs={{0,8},{8,0},{1,9},{9,1},{2,10},{10,2},{3,11},{11,3},{4,12},{12,4},... | collective-permute-start | bytes 884744 | tf_op jit(solution)/shard_map/ppermute | solution.py:33
  20.5 16.4 %collective-permute-start.1 = (bf16[208,768]{1,0:T(8,128)(2,1)}, bf16[208,768]{1,0:T(8,128)(2,1)S(1)}, u32[]{:S(2)}, u32[]{:S(2)}) collective-permute-start(bf16[208,768]{1,0:T(8,128)(2,1)} %collective-permute-done), channel_id=1, source_target_pairs={{0,2},{2,3},{3,1},{1,0},{4,6},{6,7},{7,5},{5,4},{8,10},{10,11},{11... | collective-permute-start | bytes 958472 | tf_op jit(solution)/shard_map/ppermute | solution.py:29
  40.0 19.8 %collective-permute-start.7 = (bf16[384,768]{1,0:T(8,128)(2,1)S(1)}, bf16[384,768]{1,0:T(8,128)(2,1)}, u32[]{:S(2)}, u32[]{:S(2)}) collective-permute-start(bf16[384,768]{1,0:T(8,128)(2,1)S(1)} %pad_maximum_fusion.3), channel_id=1, source_target_pairs={{0,2},{2,3},{3,1},{1,0},{4,6},{6,7},{7,5},{5,4},{8,10},{10,11},{11... | collective-permute-start | bytes 1769480 | tf_op jit(solution)/shard_map/ppermute | solution.py:29
  47.6 12.1 %collective-permute-start.8 = (bf16[192,768]{1,0:T(8,128)(2,1)S(1)}, bf16[192,768]{1,0:T(8,128)(2,1)S(1)}, u32[]{:S(2)}, u32[]{:S(2)}) collective-permute-start(bf16[192,768]{1,0:T(8,128)(2,1)S(1)} %slice.290), channel_id=1, source_target_pairs={{0,8},{8,0},{1,9},{9,1},{2,10},{10,2},{3,11},{11,3},{4,12},{12,4},... | collective-permute-start | bytes 884744 | tf_op jit(solution)/shard_map/ppermute | solution.py:33
  50.6 28.5 %collective-permute-start.9 = (bf16[768,768]{1,0:T(8,128)(2,1)}, bf16[768,768]{1,0:T(8,128)(2,1)S(1)}, u32[]{:S(2)}, u32[]{:S(2)}) collective-permute-start(bf16[768,768]{1,0:T(8,128)(2,1)} %pad_maximum_fusion.1), channel_id=1, source_target_pairs={{0,4},{4,0},{1,5},{5,1},{2,6},{6,2},{3,7},{7,3},{8,12},{12,8},{9,1... | collective-permute-start | bytes 3538952 | tf_op jit(solution)/shard_map/ppermute | solution.py:33
  60.9 18.3 %collective-permute-start.10 = (bf16[768,768]{1,0:T(8,128)(2,1)}, bf16[768,768]{1,0:T(8,128)(2,1)}, u32[]{:S(2)}, u32[]{:S(2)}) collective-permute-start(bf16[768,768]{1,0:T(8,128)(2,1)} %pad_maximum_fusion.2), channel_id=1, source_target_pairs={{0,4},{4,0},{1,5},{5,1},{2,6},{6,2},{3,7},{7,3},{8,12},{12,8},{9,1... | collective-permute-start | bytes 3538952 | tf_op jit(solution)/shard_map/ppermute | solution.py:33
  61.4 16.1 %collective-permute-start.11 = (bf16[384,768]{1,0:T(8,128)(2,1)}, bf16[384,768]{1,0:T(8,128)(2,1)}, u32[]{:S(2)}, u32[]{:S(2)}) collective-permute-start(bf16[384,768]{1,0:T(8,128)(2,1)} %collective-permute-done.7), channel_id=1, source_target_pairs={{0,2},{2,3},{3,1},{1,0},{4,6},{6,7},{7,5},{5,4},{8,10},{10,11},{11... | collective-permute-start | bytes 1769480 | tf_op jit(solution)/shard_map/ppermute | solution.py:29
  61.5 16.0 %collective-permute-start.12 = (bf16[384,768]{1,0:T(8,128)(2,1)}, bf16[384,768]{1,0:T(8,128)(2,1)}, u32[]{:S(2)}, u32[]{:S(2)}) collective-permute-start(bf16[384,768]{1,0:T(8,128)(2,1)} %collective-permute-done.7), channel_id=1, source_target_pairs={{0,8},{8,0},{1,9},{9,1},{2,10},{10,2},{3,11},{11,3},{4,12},{12,4},... | collective-permute-start | bytes 1769480 | tf_op jit(solution)/shard_map/ppermute | solution.py:33
  77.5 15.1 %collective-permute-start.13 = (bf16[384,768]{1,0:T(8,128)(2,1)}, bf16[384,768]{1,0:T(8,128)(2,1)S(1)}, u32[]{:S(2)}, u32[]{:S(2)}) collective-permute-start(bf16[384,768]{1,0:T(8,128)(2,1)} %collective-permute-done.11), channel_id=1, source_target_pairs={{0,2},{2,3},{3,1},{1,0},{4,6},{6,7},{7,5},{5,4},{8,10},{10,11},{11... | collective-permute-start | bytes 1769480 | tf_op jit(solution)/shard_map/ppermute | solution.py:29
  78.6 14.1 %collective-permute-start.14 = (bf16[384,768]{1,0:T(8,128)(2,1)}, bf16[384,768]{1,0:T(8,128)(2,1)S(1)}, u32[]{:S(2)}, u32[]{:S(2)}) collective-permute-start(bf16[384,768]{1,0:T(8,128)(2,1)} %collective-permute-done.11), channel_id=1, source_target_pairs={{0,8},{8,0},{1,9},{9,1},{2,10},{10,2},{3,11},{11,3},{4,12},{12,4},... | collective-permute-start | bytes 1769480 | tf_op jit(solution)/shard_map/ppermute | solution.py:33
  83.0 14.5 %collective-permute-start.15 = (bf16[512,768]{1,0:T(8,128)(2,1)S(1)}, bf16[512,768]{1,0:T(8,128)(2,1)S(1)}, u32[]{:S(2)}, u32[]{:S(2)}) collective-permute-start(bf16[512,768]{1,0:T(8,128)(2,1)S(1)} %convolution_convert_fusion.7.k_ref), channel_id=1, source_target_pairs={{0,4},{4,0},{1,5},{5,1},{2,6},{6,2},{3,7},{7,3},{8,12},{12,8},{9,1... | collective-permute-start | bytes 2359304 | tf_op jit(solution)/shard_map/ppermute | solution.py:33
  86.7 10.8 %collective-permute-start.16 = (bf16[512,768]{1,0:T(8,128)(2,1)S(1)}, bf16[512,768]{1,0:T(8,128)(2,1)S(1)}, u32[]{:S(2)}, u32[]{:S(2)}) collective-permute-start(bf16[512,768]{1,0:T(8,128)(2,1)S(1)} %add_convert_fusion.12.v_ref), channel_id=1, source_target_pairs={{0,4},{4,0},{1,5},{5,1},{2,6},{6,2},{3,7},{7,3},{8,12},{12,8},{9,1... | collective-permute-start | bytes 2359304 | tf_op jit(solution)/shard_map/ppermute | solution.py:33
  92.7 16.1 %collective-permute-start.17 = (bf16[384,768]{1,0:T(8,128)(2,1)S(1)}, bf16[384,768]{1,0:T(8,128)(2,1)S(1)}, u32[]{:S(2)}, u32[]{:S(2)}) collective-permute-start(bf16[384,768]{1,0:T(8,128)(2,1)S(1)} %collective-permute-done.13), channel_id=1, source_target_pairs={{0,8},{8,0},{1,9},{9,1},{2,10},{10,2},{3,11},{11,3},{4,12},{12,4},... | collective-permute-start | bytes 1769480 | tf_op jit(solution)/shard_map/ppermute | solution.py:33
  116.0 13.4 %collective-permute-start.18 = (bf16[1536,768]{1,0:T(8,128)(2,1)}, bf16[1536,768]{1,0:T(8,128)(2,1)S(1)}, u32[]{:S(2)}, u32[]{:S(2)}) collective-permute-start(bf16[1536,768]{1,0:T(8,128)(2,1)} %get-tuple-element.266.expand_ref.e0_ref), channel_id=1, source_target_pairs={{0,4},{4,0},{1,5},{5,1},{2,6},{6,2},{3,7},{7,3},{8,12},{12,8},{9,1... | collective-permute-start | bytes 7077896 | tf_op jit(solution)/shard_map/ppermute | solution.py:33
  118.1 11.3 %collective-permute-start.19 = (bf16[1536,768]{1,0:T(8,128)(2,1)}, bf16[1536,768]{1,0:T(8,128)(2,1)}, u32[]{:S(2)}, u32[]{:S(2)}) collective-permute-start(bf16[1536,768]{1,0:T(8,128)(2,1)} %copy-done.6), channel_id=1, source_target_pairs={{0,4},{4,0},{1,5},{5,1},{2,6},{6,2},{3,7},{7,3},{8,12},{12,8},{9,1... | collective-permute-start | bytes 7077896 | tf_op jit(solution)/shard_map/ppermute | solution.py:33
  140.5 12.1 %collective-permute-start.21 = (bf16[256,768]{1,0:T(8,128)(2,1)S(1)}, bf16[256,768]{1,0:T(8,128)(2,1)S(1)}, u32[]{:S(2)}, u32[]{:S(2)}) collective-permute-start(bf16[256,768]{1,0:T(8,128)(2,1)S(1)} %fusion.33), channel_id=1, source_target_pairs={{0,16},{1,17},{2,18},{3,19},{4,20},{5,21},{6,22},{7,23},{8,24},{9,... | collective-permute-start | bytes 1179656 | tf_op jit(solution)/shard_map/ppermute | solution.py:37
  156.1 12.2 %collective-permute-start.22 = (bf16[512,768]{1,0:T(8,128)(2,1)S(1)}, bf16[512,768]{1,0:T(8,128)(2,1)S(1)}, u32[]{:S(2)}, u32[]{:S(2)}) collective-permute-start(bf16[512,768]{1,0:T(8,128)(2,1)S(1)} %convolution_convert_fusion.6.k_ref), channel_id=1, source_target_pairs={{0,4},{4,0},{1,5},{5,1},{2,6},{6,2},{3,7},{7,3},{8,12},{12,8},{9,1... | collective-permute-start | bytes 2359304 | tf_op jit(solution)/shard_map/ppermute | solution.py:33
  157.6 10.8 %collective-permute-start.23 = (bf16[512,768]{1,0:T(8,128)(2,1)S(1)}, bf16[512,768]{1,0:T(8,128)(2,1)S(1)}, u32[]{:S(2)}, u32[]{:S(2)}) collective-permute-start(bf16[512,768]{1,0:T(8,128)(2,1)S(1)} %add_convert_fusion.9.v_ref), channel_id=1, source_target_pairs={{0,4},{4,0},{1,5},{5,1},{2,6},{6,2},{3,7},{7,3},{8,12},{12,8},{9,1... | collective-permute-start | bytes 2359304 | tf_op jit(solution)/shard_map/ppermute | solution.py:33
  157.6 23.6 %collective-permute-start.24 = (bf16[256,768]{1,0:T(8,128)(2,1)}, bf16[256,768]{1,0:T(8,128)(2,1)S(1)}, u32[]{:S(2)}, u32[]{:S(2)}) collective-permute-start(bf16[256,768]{1,0:T(8,128)(2,1)} %bitcast.156), channel_id=1, source_target_pairs={{0,16},{1,20},{4,17},{5,21},{8,24},{9,28},{12,25},{13,29},{16,18},... | collective-permute-start | bytes 1179656 | tf_op jit(solution)/shard_map/ppermute | solution.py:57
  158.3 25.8 %collective-permute-start.25 = (bf16[256,768]{1,0:T(8,128)(2,1)}, bf16[256,768]{1,0:T(8,128)(2,1)S(1)}, u32[]{:S(2)}, u32[]{:S(2)}) collective-permute-start(bf16[256,768]{1,0:T(8,128)(2,1)} %bitcast.157), channel_id=1, source_target_pairs={{3,16},{2,20},{7,17},{6,21},{11,24},{10,28},{15,25},{14,29},{19,18... | collective-permute-start | bytes 1179656 | tf_op jit(solution)/shard_map/ppermute | solution.py:57
  203.9 18.4 %collective-permute-start.26 = (bf16[256,768]{1,0:T(8,128)(2,1)S(1)}, bf16[256,768]{1,0:T(8,128)(2,1)S(1)}, u32[]{:S(2)}, u32[]{:S(2)}) collective-permute-start(bf16[256,768]{1,0:T(8,128)(2,1)S(1)} %get-tuple-element.264), channel_id=1, source_target_pairs={{16,0},{20,1},{17,4},{21,5},{24,8},{28,9},{25,12},{29,13},{18,16},... | collective-permute-start | bytes 1179656 | tf_op jit(solution)/shard_map/ppermute | solution.py:64
  204.7 20.0 %collective-permute-start.27 = (bf16[256,768]{1,0:T(8,128)(2,1)S(1)}, bf16[256,768]{1,0:T(8,128)(2,1)S(1)}, u32[]{:S(2)}, u32[]{:S(2)}) collective-permute-start(bf16[256,768]{1,0:T(8,128)(2,1)S(1)} %get-tuple-element.263), channel_id=1, source_target_pairs={{16,3},{20,2},{17,7},{21,6},{24,11},{28,10},{25,15},{29,14},{18,19... | collective-permute-start | bytes 1179656 | tf_op jit(solution)/shard_map/ppermute | solution.py:64
  233.2 15.6 %collective-permute-start.30 = (bf16[256,768]{1,0:T(8,128)(2,1)S(1)}, bf16[256,768]{1,0:T(8,128)(2,1)S(1)}, u32[]{:S(2)}, u32[]{:S(2)}) collective-permute-start(bf16[256,768]{1,0:T(8,128)(2,1)S(1)} %get-tuple-element.262), channel_id=1, source_target_pairs={{16,0},{17,1},{18,2},{19,3},{20,4},{21,5},{22,6},{23,7},{24,8},{25... | collective-permute-start | bytes 1179656 | tf_op jit(solution)/shard_map/ppermute | solution.py:37
  234.5 22.8 %collective-permute-start.29 = (bf16[256,768]{1,0:T(8,128)(2,1)S(1)}, bf16[256,768]{1,0:T(8,128)(2,1)S(1)}, u32[]{:S(2)}, u32[]{:S(2)}) collective-permute-start(bf16[256,768]{1,0:T(8,128)(2,1)S(1)} %get-tuple-element.261), channel_id=1, source_target_pairs={{16,0},{17,1},{18,2},{19,3},{20,4},{21,5},{22,6},{23,7},{24,8},{25... | collective-permute-start | bytes 1179656 | tf_op jit(solution)/shard_map/ppermute | solution.py:37
  278.4 27.6 %collective-permute-start.34 = (bf16[768,768]{1,0:T(8,128)(2,1)S(1)}, bf16[768,768]{1,0:T(8,128)(2,1)}, u32[]{:S(2)}, u32[]{:S(2)}) collective-permute-start(bf16[768,768]{1,0:T(8,128)(2,1)S(1)} %slice.393), channel_id=1, source_target_pairs={{0,8},{8,0},{1,9},{9,1},{2,10},{10,2},{3,11},{11,3},{4,12},{12,4},... | collective-permute-start | bytes 3538952 | tf_op jit(solution)/shard_map/ppermute | solution.py:33
  284.6 21.4 %collective-permute-start.33 = (bf16[384,768]{1,0:T(8,128)(2,1)S(1)}, bf16[384,768]{1,0:T(8,128)(2,1)}, u32[]{:S(2)}, u32[]{:S(2)}) collective-permute-start(bf16[384,768]{1,0:T(8,128)(2,1)S(1)} %pad_maximum_fusion.5), channel_id=1, source_target_pairs={{0,2},{2,3},{3,1},{1,0},{4,6},{6,7},{7,5},{5,4},{8,10},{10,11},{11... | collective-permute-start | bytes 1769480 | tf_op jit(solution)/shard_map/ppermute | solution.py:29
  311.5 22.2 %collective-permute-start.35 = (bf16[384,768]{1,0:T(8,128)(2,1)S(1)}, bf16[384,768]{1,0:T(8,128)(2,1)S(1)}, u32[]{:S(2)}, u32[]{:S(2)}) collective-permute-start(bf16[384,768]{1,0:T(8,128)(2,1)S(1)} %add_convert_fusion.16), channel_id=1, source_target_pairs={{0,2},{2,3},{3,1},{1,0},{4,6},{6,7},{7,5},{5,4},{8,10},{10,11},{11... | collective-permute-start | bytes 1769480 | tf_op jit(solution)/shard_map/ppermute | solution.py:29
  313.2 20.5 %collective-permute-start.36 = (bf16[192,768]{1,0:T(8,128)(2,1)S(1)}, bf16[192,768]{1,0:T(8,128)(2,1)S(1)}, u32[]{:S(2)}, u32[]{:S(2)}) collective-permute-start(bf16[192,768]{1,0:T(8,128)(2,1)S(1)} %slice.395), channel_id=1, source_target_pairs={{0,2},{2,3},{3,1},{1,0},{4,6},{6,7},{7,5},{5,4},{8,10},{10,11},{11... | collective-permute-start | bytes 884744 | tf_op jit(solution)/shard_map/ppermute | solution.py:29
  320.8 18.3 %collective-permute-start.39 = (bf16[768,768]{1,0:T(8,128)(2,1)}, bf16[768,768]{1,0:T(8,128)(2,1)}, u32[]{:S(2)}, u32[]{:S(2)}) collective-permute-start(bf16[768,768]{1,0:T(8,128)(2,1)} %convolution_convert_fusion.3), channel_id=1, source_target_pairs={{0,4},{4,0},{1,5},{5,1},{2,6},{6,2},{3,7},{7,3},{8,12},{12,8},{9,1... | collective-permute-start | bytes 3538952 | tf_op jit(solution)/shard_map/ppermute | solution.py:33
  322.9 19.2 %collective-permute-start.38 = (bf16[768,768]{1,0:T(8,128)(2,1)}, bf16[768,768]{1,0:T(8,128)(2,1)}, u32[]{:S(2)}, u32[]{:S(2)}) collective-permute-start(bf16[768,768]{1,0:T(8,128)(2,1)} %convolution_convert_fusion.2), channel_id=1, source_target_pairs={{0,4},{4,0},{1,5},{5,1},{2,6},{6,2},{3,7},{7,3},{8,12},{12,8},{9,1... | collective-permute-start | bytes 3538952 | tf_op jit(solution)/shard_map/ppermute | solution.py:33
  338.4 28.7 %collective-permute-start.45 = (bf16[384,768]{1,0:T(8,128)(2,1)S(1)}, bf16[384,768]{1,0:T(8,128)(2,1)S(1)}, u32[]{:S(2)}, u32[]{:S(2)}) collective-permute-start(bf16[384,768]{1,0:T(8,128)(2,1)S(1)} %add_convert_fusion.15), channel_id=1, source_target_pairs={{0,2},{2,3},{3,1},{1,0},{4,6},{6,7},{7,5},{5,4},{8,10},{10,11},{11... | collective-permute-start | bytes 1769480 | tf_op jit(solution)/shard_map/ppermute | solution.py:29
  340.8 10.7 %collective-permute-start.40 = (bf16[192,768]{1,0:T(8,128)(2,1)S(1)}, bf16[192,768]{1,0:T(8,128)(2,1)S(1)}, u32[]{:S(2)}, u32[]{:S(2)}) collective-permute-start(bf16[192,768]{1,0:T(8,128)(2,1)S(1)} %get-tuple-element.256), channel_id=1, source_target_pairs={{0,8},{8,0},{1,9},{9,1},{2,10},{10,2},{3,11},{11,3},{4,12},{12,4},... | collective-permute-start | bytes 884744 | tf_op jit(solution)/shard_map/ppermute | solution.py:33
  351.7 15.4 %collective-permute-start.43 = (bf16[208,768]{1,0:T(8,128)(2,1)S(1)}, bf16[208,768]{1,0:T(8,128)(2,1)S(1)}, u32[]{:S(2)}, u32[]{:S(2)}) collective-permute-start(bf16[208,768]{1,0:T(8,128)(2,1)S(1)} %pad_maximum_fusion.12), channel_id=1, source_target_pairs={{0,2},{2,3},{3,1},{1,0},{4,6},{6,7},{7,5},{5,4},{8,10},{10,11},{11... | collective-permute-start | bytes 958472 | tf_op jit(solution)/shard_map/ppermute | solution.py:29
  351.9 15.2 %collective-permute-start.46 = (bf16[192,768]{1,0:T(8,128)(2,1)S(1)}, bf16[192,768]{1,0:T(8,128)(2,1)S(1)}, u32[]{:S(2)}, u32[]{:S(2)}) collective-permute-start(bf16[192,768]{1,0:T(8,128)(2,1)S(1)} %add_convert_fusion.25), channel_id=1, source_target_pairs={{0,2},{2,3},{3,1},{1,0},{4,6},{6,7},{7,5},{5,4},{8,10},{10,11},{11... | collective-permute-start | bytes 884744 | tf_op jit(solution)/shard_map/ppermute | solution.py:29
  352.3 14.8 %collective-permute-start.44 = (bf16[192,768]{1,0:T(8,128)(2,1)S(1)}, bf16[192,768]{1,0:T(8,128)(2,1)S(1)}, u32[]{:S(2)}, u32[]{:S(2)}) collective-permute-start(bf16[192,768]{1,0:T(8,128)(2,1)S(1)} %get-tuple-element.253), channel_id=1, source_target_pairs={{0,8},{8,0},{1,9},{9,1},{2,10},{10,2},{3,11},{11,3},{4,12},{12,4},... | collective-permute-start | bytes 884744 | tf_op jit(solution)/shard_map/ppermute | solution.py:33
  352.5 16.7 %collective-permute-start.48 = (bf16[192,768]{1,0:T(8,128)(2,1)S(1)}, bf16[192,768]{1,0:T(8,128)(2,1)S(1)}, u32[]{:S(2)}, u32[]{:S(2)}) collective-permute-start(bf16[192,768]{1,0:T(8,128)(2,1)S(1)} %get-tuple-element.161), channel_id=1, source_target_pairs={{0,8},{8,0},{1,9},{9,1},{2,10},{10,2},{3,11},{11,3},{4,12},{12,4},... | collective-permute-start | bytes 884744 | tf_op jit(solution)/shard_map/ppermute | solution.py:33
  367.3 14.4 %collective-permute-start.47 = (bf16[208,768]{1,0:T(8,128)(2,1)S(1)}, bf16[208,768]{1,0:T(8,128)(2,1)S(1)}, u32[]{:S(2)}, u32[]{:S(2)}) collective-permute-start(bf16[208,768]{1,0:T(8,128)(2,1)S(1)} %add_convert_fusion.19), channel_id=1, source_target_pairs={{0,2},{2,3},{3,1},{1,0},{4,6},{6,7},{7,5},{5,4},{8,10},{10,11},{11... | collective-permute-start | bytes 958472 | tf_op jit(solution)/shard_map/ppermute | solution.py:29
  367.4 14.3 %collective-permute-start.49 = (bf16[192,768]{1,0:T(8,128)(2,1)S(1)}, bf16[192,768]{1,0:T(8,128)(2,1)S(1)}, u32[]{:S(2)}, u32[]{:S(2)}) collective-permute-start(bf16[192,768]{1,0:T(8,128)(2,1)S(1)} %add_convert_fusion.23), channel_id=1, source_target_pairs={{0,2},{2,3},{3,1},{1,0},{4,6},{6,7},{7,5},{5,4},{8,10},{10,11},{11... | collective-permute-start | bytes 884744 | tf_op jit(solution)/shard_map/ppermute | solution.py:29
  367.5 15.4 %collective-permute-start.51 = (bf16[192,768]{1,0:T(8,128)(2,1)S(1)}, bf16[192,768]{1,0:T(8,128)(2,1)S(1)}, u32[]{:S(2)}, u32[]{:S(2)}) collective-permute-start(bf16[192,768]{1,0:T(8,128)(2,1)S(1)} %get-tuple-element.165), channel_id=1, source_target_pairs={{0,8},{8,0},{1,9},{9,1},{2,10},{10,2},{3,11},{11,3},{4,12},{12,4},... | collective-permute-start | bytes 884744 | tf_op jit(solution)/shard_map/ppermute | solution.py:33
  367.9 18.0 %collective-permute-start.52 = (bf16[2,192,768]{2,1,0:T(8,128)(2,1)S(1)}, bf16[2,192,768]{2,1,0:T(8,128)(2,1)S(1)}, u32[]{:S(2)}, u32[]{:S(2)}) collective-permute-start(bf16[2,192,768]{2,1,0:T(8,128)(2,1)S(1)} %bitcast.147), channel_id=1, source_target_pairs={{0,8},{8,0},{1,9},{9,1},{2,10},{10,2},{3,11},{11,3},{4,12},{12,4},... | collective-permute-start | bytes 1769480 | tf_op jit(solution)/shard_map/ppermute | solution.py:33
  382.6 18.4 %collective-permute-start.56 = (bf16[192,768]{1,0:T(8,128)(2,1)S(1)}, bf16[192,768]{1,0:T(8,128)(2,1)S(1)}, u32[]{:S(2)}, u32[]{:S(2)}) collective-permute-start(bf16[192,768]{1,0:T(8,128)(2,1)S(1)} %add_convert_fusion.20), channel_id=1, source_target_pairs={{0,8},{8,0},{1,9},{9,1},{2,10},{10,2},{3,11},{11,3},{4,12},{12,4},... | collective-permute-start | bytes 884744 | tf_op jit(solution)/shard_map/ppermute | solution.py:33
  390.2 20.2 %collective-permute-start.53 = (bf16[256,768]{1,0:T(8,128)(2,1)}, bf16[256,768]{1,0:T(8,128)(2,1)S(1)}, u32[]{:S(2)}, u32[]{:S(2)}) collective-permute-start(bf16[256,768]{1,0:T(8,128)(2,1)} %get-tuple-element.260), channel_id=1, source_target_pairs={{0,0},{4,1},{1,4},{5,5},{8,8},{12,9},{9,12},{13,13},{2,16},{6,17},... | collective-permute-start | bytes 1179656 | tf_op jit(solution)/shard_map/ppermute | solution.py:64
  397.0 20.7 %collective-permute-start.54 = (bf16[256,768]{1,0:T(8,128)(2,1)}, bf16[256,768]{1,0:T(8,128)(2,1)}, u32[]{:S(2)}, u32[]{:S(2)}) collective-permute-start(bf16[256,768]{1,0:T(8,128)(2,1)} %get-tuple-element.259), channel_id=1, source_target_pairs={{0,3},{4,2},{1,7},{5,6},{8,11},{12,10},{9,15},{13,14},{2,19},{6,18... | collective-permute-start | bytes 1179656 | tf_op jit(solution)/shard_map/ppermute | solution.py:64
  400.1 19.5 %collective-permute-start.58 = (bf16[384,768]{1,0:T(8,128)(2,1)S(1)}, bf16[384,768]{1,0:T(8,128)(2,1)}, u32[]{:S(2)}, u32[]{:S(2)}) collective-permute-start(bf16[384,768]{1,0:T(8,128)(2,1)S(1)} %pad_maximum_fusion.9), channel_id=1, source_target_pairs={{0,4},{4,0},{1,5},{5,1},{2,6},{6,2},{3,7},{7,3},{8,12},{12,8},{9,1... | collective-permute-start | bytes 1769480 | tf_op jit(solution)/shard_map/ppermute | solution.py:33
  408.7 14.1 %collective-permute-start.57 = (bf16[384,768]{1,0:T(8,128)(2,1)}, bf16[384,768]{1,0:T(8,128)(2,1)}, u32[]{:S(2)}, u32[]{:S(2)}) collective-permute-start(bf16[384,768]{1,0:T(8,128)(2,1)} %pad_maximum_fusion.8), channel_id=1, source_target_pairs={{0,4},{4,0},{1,5},{5,1},{2,6},{6,2},{3,7},{7,3},{8,12},{12,8},{9,1... | collective-permute-start | bytes 1769480 | tf_op jit(solution)/shard_map/ppermute | solution.py:33
  410.2 16.0 %collective-permute-start.59 = (bf16[384,768]{1,0:T(8,128)(2,1)}, bf16[384,768]{1,0:T(8,128)(2,1)}, u32[]{:S(2)}, u32[]{:S(2)}) collective-permute-start(bf16[384,768]{1,0:T(8,128)(2,1)} %pad_maximum_fusion.10), channel_id=1, source_target_pairs={{0,4},{4,0},{1,5},{5,1},{2,6},{6,2},{3,7},{7,3},{8,12},{12,8},{9,1... | collective-permute-start | bytes 1769480 | tf_op jit(solution)/shard_map/ppermute | solution.py:33
  (122 other events, 1369.3 us)

commit v4 on v3

--- a/solution.py
+++ b/solution.py
@@ -49,7 +49,7 @@
             for c in range(2):
                 for core in range(2):
                     block = 3 - core if large else core
-                    pairs.append((index(micro, y, c, block), index(section, y, core, 2 * micro + c)))
+                    pairs.append((index(micro, y, c, block), index(section, y, core, 2 * c + micro)))
     return pairs
 
 
@@ -73,11 +73,6 @@
     return lax.dot_general(left, right, (((0,), (0,)), ((), ())), preferred_element_type=F32)
 
 
-def tk(left, right):
-    turned = right.astype(F32).T.astype(BF16)
-    return nn(turned, left).T
-
-
 def nn(left, right):
     return lax.dot_general(left, right, (((1,), (0,)), ((), ())), preferred_element_type=F32)
 
@@ -95,7 +90,11 @@
     return jnp.where(mask, value.astype(F32) * factor, 0.0).astype(BF16)
 
 
-def attend_kernel(keep_weights, core_ref, q_ref, k_ref, v_ref, ko_ref, vo_ref, o_ref, *p_refs):
+def turned(value):
+    return value.astype(F32).T.astype(BF16)
+
+
+def attend_kernel(keep_weights, core_ref, q_ref, k_ref, v_ref, ko_ref, vo_ref, o_ref, *kept_refs):
     rows = q_ref.shape[0] // 2
     second = core_ref[0] == 1
     keys = lax.broadcasted_iota(jnp.int32, (rows, rows), 0)
@@ -104,18 +103,17 @@
     factor = HEAD ** (-0.5)
     small = pl.ds(0, rows)
     large = pl.ds(rows, rows)
-    k5 = jnp.where(second, ko_ref[small, :].astype(F32), ko_ref[large, :].astype(F32)).astype(BF16)
-    v5 = jnp.where(second, vo_ref[small, :].astype(F32), vo_ref[large, :].astype(F32))
-    out_small = None
-    out_large = None
+
+    def fifth(ref):
+        return jnp.where(second, ref[small, :].astype(F32), ref[large, :].astype(F32)).astype(BF16)
+
+    k5, q5 = fifth(ko_ref), fifth(q_ref)
+    vs, vl, v4, v5 = turned(v_ref[small, :]), turned(v_ref[large, :]), turned(vo_ref[small, :]), turned(fifth(vo_ref))
+    small_parts, large_parts, scales = [], [], []
     for head in range(LANES // HEAD):
         mask = head_mask(rows, head)
-
-        def query(value):
-            return only(mask, value, factor)
-
-        qs, ql = query(q_ref[small, :]), query(q_ref[large, :])
-        qf = query(jnp.where(second, q_ref[small, :].astype(F32), q_ref[large, :].astype(F32)))
+        lanes = slice(head * HEAD, (head + 1) * HEAD)
+        qs, ql, qf = (only(mask, value, factor) for value in (q_ref[small, :], q_ref[large, :], q5))
         s1 = jnp.where(allowed, nt(k_ref[small, :], qs), NEGATIVE)
         s2 = nt(k_ref[small, :], ql)
         s3 = jnp.where(allowed, nt(k_ref[large, :], ql), NEGATIVE)
@@ -144,32 +142,25 @@
         rl = total(e2) + total(e3) + total(e4)
         rs = 1.0 / jnp.where(second, rs + t5, rs)
         rl = 1.0 / jnp.where(second, rl, rl + t5)
-        rf = jnp.where(second, rs, rl)
-        p1 = (e1 * rs).astype(BF16)
-        p2 = (e2 * rl).astype(BF16)
-        p3 = (e3 * rl).astype(BF16)
-        p4 = (e4 * rl).astype(BF16)
-        p5 = (e5 * rf).astype(BF16)
+        e1, e2, e3, e4, e5 = (value.astype(BF16) for value in (e1, e2, e3, e4, e5))
         if keep_weights:
-            for place, value in enumerate((p1, p2, p3, p4, p5)):
-                p_refs[0][head, place] = value
-        vs = only(mask, v_ref[small, :])
-        o5 = tk(p5, only(mask, v5))
-        os = tk(p1, vs) + jnp.where(second, o5, 0.0)
-        ol = (
-            tk(p2, vs)
-            + tk(p3, only(mask, v_ref[large, :]))
-            + tk(p4, only(mask, vo_ref[small, :]))
-            + jnp.where(second, 0.0, o5)
+            for place, value in enumerate((e1, e2, e3, e4, e5)):
+                kept_refs[0][head, place] = value
+            scales.append(jnp.concatenate([rs, rl], axis=1))
+        o5 = nn(v5[lanes], e5)
+        small_parts.append((nn(vs[lanes], e1) + jnp.where(second, o5, 0.0)) * rs)
+        large_parts.append(
+            (nn(vs[lanes], e2) + nn(vl[lanes], e3) + nn(v4[lanes], e4) + jnp.where(second, 0.0, o5)) * rl
         )
-        out_small = os if out_small is None else out_small + os
-        out_large = ol if out_large is None else out_large + ol
-    o_ref[small, :] = out_small.astype(BF16)
-    o_ref[large, :] = out_large.astype(BF16)
+    o_ref[small, :] = jnp.concatenate(small_parts).T.astype(BF16)
+    o_ref[large, :] = jnp.concatenate(large_parts).T.astype(BF16)
+    if keep_weights:
+        row = lax.broadcasted_iota(jnp.int32, (8, 2 * rows), 0)
+        kept_refs[1][...] = jnp.where(row == 0, scales[0], scales[1])
 
 
 def attend_back_kernel(
-    core_ref, q_ref, k_ref, v_ref, ko_ref, vo_ref, go_ref, o_ref, p_ref, gq_ref, own_ref, other_ref, sums_ref
+    core_ref, q_ref, k_ref, v_ref, ko_ref, vo_ref, go_ref, o_ref, e_ref, scale_ref, gq_ref, own_ref, other_ref, sums_ref
 ):
     rows = q_ref.shape[0] // 2
     second = core_ref[0] == 1
@@ -177,61 +168,59 @@
     small = pl.ds(0, rows)
     large = pl.ds(rows, rows)
 
-    def fifth(ref, first, last):
-        return jnp.where(second, ref[first, :].astype(F32), ref[last, :].astype(F32))
-
-    k5 = fifth(ko_ref, small, large)
-    v5 = fifth(vo_ref, small, large).astype(BF16)
-    q5 = fifth(q_ref, small, large)
-    g5 = fifth(go_ref, small, large)
-    product = go_ref[...].astype(F32) * o_ref[...].astype(F32)
+    def fifth(first, last):
+        return jnp.where(second, first.astype(F32), last.astype(F32)).astype(BF16)
+
+    row = lax.broadcasted_iota(jnp.int32, (LANES, 2 * rows), 0)
+    scale = jnp.where(row < HEAD, scale_ref[0:1, :], scale_ref[1:2, :]).T
+    grads = (go_ref[...].astype(F32) * scale).astype(BF16)
+    product = grads.astype(F32) * o_ref[...].astype(F32)
     high = product.astype(BF16)
     low = (product - high.astype(F32)).astype(BF16)
+    g_small, g_large = grads[:rows], grads[rows:]
+    g5 = fifth(g_small, g_large)
+    q5 = fifth(q_ref[small, :], q_ref[large, :])
+    v5 = fifth(vo_ref[small, :], vo_ref[large, :])
+    ks, kl, k4, k5 = (
+        turned(k_ref[small, :]), turned(k_ref[large, :]), turned(ko_ref[small, :]),
+        turned(fifth(ko_ref[small, :], ko_ref[large, :])),
+    )
     totals = {}
+    gq_small, gq_large = [], []
 
     def add(name, value):
         totals[name] = value if name not in totals else totals[name] + value
 
     for head in range(LANES // HEAD):
         mask = head_mask(rows, head)
+        lanes = slice(head * HEAD, (head + 1) * HEAD)
         ones = jnp.where(head_mask(16, head), 1.0, 0.0).astype(BF16)
         inner = (nt(ones, high) + nt(ones, low))[0:1]
         ds_, dl_ = inner[:, :rows], inner[:, rows:]
         df_ = jnp.where(second, ds_, dl_)
-
-        def weight(place):
-            return p_ref[head, place]
-
         qs, ql, qf = (only(mask, value, factor) for value in (q_ref[small, :], q_ref[large, :], q5))
-        gs, gl, gf = (only(mask, value) for value in (go_ref[small, :], go_ref[large, :], g5))
+        gs, gl, gf = (only(mask, value) for value in (g_small, g_large, g5))
 
         def score_grad(place, values, rows_grad, shift):
-            return (weight(place).astype(F32) * (nt(values, rows_grad) - shift)).astype(BF16)
+            return (e_ref[head, place].astype(F32) * (nt(values, rows_grad) - shift)).astype(BF16)
 
         z1 = score_grad(0, v_ref[small, :], gs, ds_)
         z2 = score_grad(1, v_ref[small, :], gl, dl_)
         z3 = score_grad(2, v_ref[large, :], gl, dl_)
         z4 = score_grad(3, vo_ref[small, :], gl, dl_)
         z5 = score_grad(4, v5, gf, df_)
-        k_small = only(mask, k_ref[small, :])
-        gq5 = tk(z5, only(mask, k5))
-        add("qs", tk(z1, k_small) + jnp.where(second, gq5, 0.0))
-        add(
-            "ql",
-            tk(z2, k_small)
-            + tk(z3, only(mask, k_ref[large, :]))
-            + tk(z4, only(mask, ko_ref[small, :]))
-            + jnp.where(second, 0.0, gq5),
-        )
+        gq5 = nn(k5[lanes], z5)
+        gq_small.append(nn(ks[lanes], z1) + jnp.where(second, gq5, 0.0))
+        gq_large.append(nn(ks[lanes], z2) + nn(kl[lanes], z3) + nn(k4[lanes], z4) + jnp.where(second, 0.0, gq5))
         add("ks", nn(z1, qs) + nn(z2, ql))
         add("kl", nn(z3, ql))
         add("k4", nn(z4, ql))
         add("k5", nn(z5, qf))
-        add("vs", nn(weight(0), gs) + nn(weight(1), gl))
-        add("vl", nn(weight(2), gl))
-        add("v4", nn(weight(3), gl))
-        add("v5", nn(weight(4), gf))
-    gqs, gql = totals["qs"] * factor, totals["ql"] * factor
+        add("vs", nn(e_ref[head, 0], gs) + nn(e_ref[head, 1], gl))
+        add("vl", nn(e_ref[head, 2], gl))
+        add("v4", nn(e_ref[head, 3], gl))
+        add("v5", nn(e_ref[head, 4], gf))
+    gqs, gql = jnp.concatenate(gq_small).T * factor, jnp.concatenate(gq_large).T * factor
     gq_ref[small, :] = gqs.astype(BF16)
     gq_ref[large, :] = gql.astype(BF16)
     for place, name in enumerate("kv"):
@@ -249,15 +238,18 @@
 def attend(core, q, k, v, k_other, v_other, keep_weights):
     length, width = q.shape
     rows = length // 2
+    pairs = width // LANES
     column = pl.BlockSpec((length, LANES), lambda i: (0, i))
     shapes = [jax.ShapeDtypeStruct((length, width), BF16)]
     outs = [column]
     if keep_weights:
         shapes.append(pltpu.HBM((width // HEAD, 5, rows, rows), BF16))
+        shapes.append(jax.ShapeDtypeStruct((8 * pairs, length), F32))
         outs.append(pl.BlockSpec((2, 5, rows, rows), lambda i: (i, 0, 0, 0)))
+        outs.append(pl.BlockSpec((8, length), lambda i: (i, 0)))
     return pl.pallas_call(
         functools.partial(attend_kernel, keep_weights),
-        grid=(width // LANES,),
+        grid=(pairs,),
         out_shape=shapes,
         in_specs=[pl.BlockSpec(memory_space=pltpu.SMEM)] + [column] * 5,
         out_specs=outs,
@@ -267,7 +259,7 @@
     )(core, q, k, v, k_other, v_other)
 
 
-def attend_back(core, q, k, v, k_other, v_other, grad_mixed, mixed, weights):
+def attend_back(core, q, k, v, k_other, v_other, grad_mixed, mixed, weights, scales):
     length, width = q.shape
     rows = length // 2
     column = pl.BlockSpec((length, LANES), lambda i: (0, i))
@@ -283,12 +275,12 @@
         ],
         in_specs=[pl.BlockSpec(memory_space=pltpu.SMEM)]
         + [column] * 7
-        + [pl.BlockSpec((2, 5, rows, rows), lambda i: (i, 0, 0, 0))],
+        + [pl.BlockSpec((2, 5, rows, rows), lambda i: (i, 0, 0, 0)), pl.BlockSpec((8, length), lambda i: (i, 0))],
         out_specs=[column, double, double, pl.BlockSpec((8, LANES), lambda i: (0, i))],
         compiler_params=pltpu.CompilerParams(vmem_limit_bytes=40 * 1024 * 1024),
         cost_estimate=estimate(40 * rows * rows * width * 2, 40 * length * width),
         name="attend_back",
-    )(core, q, k, v, k_other, v_other, grad_mixed, mixed, weights)
+    )(core, q, k, v, k_other, v_other, grad_mixed, mixed, weights, scales)
 
 
 def gelu_and_slope(values):
@@ -302,46 +294,27 @@
     return (gate, slope)
 
 
-def tiles_of(units):
-    return units // 512 if units % 512 == 0 else 1
-
-
 def expand_kernel(rows_ref, expand_ref, bias_ref, reduce_ref, start_ref, total_ref):
-    units = expand_ref.shape[0]
-    piece = 256 if units % 256 == 0 else units
-    rows = rows_ref[...]
-    total = None
-    for offset in range(0, units, piece):
-        part = pl.ds(offset, piece)
-        gate, _ = gelu_and_slope(nt(rows, expand_ref[part, :]) + bias_ref[:, part])
-        term = nn(gate.astype(BF16), reduce_ref[part, :])
-        total = term if total is None else total + term
-
-    @pl.when(pl.program_id(0) == 0)
-    def _():
-        total_ref[...] = start_ref[...] + total
-
-    @pl.when(pl.program_id(0) > 0)
-    def _():
-        total_ref[...] += total
+    gate, _ = gelu_and_slope(nt(rows_ref[...], expand_ref[...]) + bias_ref[...])
+    total_ref[...] = start_ref[...] + nn(gate.astype(BF16), reduce_ref[...])
 
 
 def feed_half(rows, expand_w, bias, reduce_w, start, row_part=None):
     length, width = rows.shape
     units = expand_w.shape[0]
-    steps = tiles_of(units)
-    tile = units // steps
     if row_part is not None:
         length = length // 2
     place = row_part or 0
     whole = pl.BlockSpec((length, width), lambda i: (0, 0))
     taken = pl.BlockSpec((length, width), lambda i: (place, 0))
-    weight = pl.BlockSpec((tile, width), lambda i: (i, 0))
+    start_place = 0 if start.shape[0] == length else place
+    begun = pl.BlockSpec((length, width), lambda i: (start_place, 0))
+    weight = pl.BlockSpec((units, width), lambda i: (0, 0))
     return pl.pallas_call(
         expand_kernel,
-        grid=(steps,),
+        grid=(1,),
         out_shape=jax.ShapeDtypeStruct((length, width), F32),
-        in_specs=[taken, weight, pl.BlockSpec((1, tile), lambda i: (0, i)), weight, taken],
+        in_specs=[taken, weight, pl.BlockSpec((1, units), lambda i: (0, 0)), weight, begun],
         out_specs=whole,
         compiler_params=pltpu.CompilerParams(vmem_limit_bytes=40 * 1024 * 1024),
         cost_estimate=estimate(4 * length * width * units, 4 * width * units),
@@ -405,8 +378,7 @@
         tile(e1_ref, r1_ref, s1_ref, p1_ref, sums1_ref)
 
 
-def feed_specs(length, width, units):
-    steps = tiles_of(units)
+def feed_specs(length, width, units, steps):
     tile = units // steps
     whole = pl.BlockSpec((length, width), lambda i: (0, 0))
 
@@ -426,7 +398,7 @@
 def feed_both(rows, grad, halves):
     length, width = rows.shape
     units = halves[0][0].shape[0]
-    steps, whole, weight, across, row, _ = feed_specs(length, width, units)
+    steps, whole, weight, across, row, _ = feed_specs(length, width, units, 2)
     total = jax.ShapeDtypeStruct((length, width), F32)
     kept = jax.ShapeDtypeStruct((length, units), BF16)
     (e0, b0, r0), (e1, b1, r1) = halves
@@ -445,7 +417,7 @@
 def feed_back(grad, halves, slope):
     length, width = grad.shape
     units = halves[0][0].shape[0]
-    steps, whole, weight, across, _, rows = feed_specs(length, width, units)
+    steps, whole, weight, across, _, rows = feed_specs(length, width, units, 1)
     kept = jax.ShapeDtypeStruct((length, units), BF16)
     sums = jax.ShapeDtypeStruct((8, units), F32)
     (e0, _, r0), (e1, _, r1) = halves
@@ -487,7 +459,8 @@
     v_other = swap(v, "core")
     q = narrow(nt(ready_one, proj[0]) + bias_q)
     if before:
-        q, *before = lax.optimization_barrier((q, *before))
+        q, proj_out, *before = lax.optimization_barrier((q, proj[3], *before))
+        proj = [*proj[:3], proj_out]
         after = after(before)
     mixed, *kept_weights = attend(core, q, k, v, k_other, v_other, keep)
     mixed, *after = lax.optimization_barrier((mixed, *after))
@@ -505,12 +478,15 @@
 def feed_forward_only(middle, weights):
     ready_two = feed_start(middle, weights)[2]
     first, second = weights[2]
-    total = feed_half(ready_two, *first, jnp.broadcast_to(weights[3], middle.shape))
     block = middle.shape[0] // 2
+    total = jnp.broadcast_to(weights[3], (block, middle.shape[1]))
+    totals = [feed_half(ready_two, *first, total, 0)]
     results = []
     for part in range(2):
         rows = slice(part * block, (part + 1) * block)
-        piece = feed_half(ready_two, *second, tie(total, *results), part)
+        if part:
+            totals.append(feed_half(ready_two, *first, tie(total, *results), part))
+        piece = feed_half(ready_two, *second, totals[part], part)
         results.append(narrow(middle[rows] + BRANCH * piece))
     return results
 
@@ -526,11 +502,11 @@
 
 def attention_backward(core, kept, grad_middle, weights, before=(), after=()):
     gain_a, _, proj, _, _, _ = weights
-    normed_one, inverse_one, ready_one, projected, mixed, attention = kept
+    normed_one, inverse_one, ready_one, projected, mixed, *attention = kept
     grad_attended = BRANCH * grad_middle
     rounded_attended = narrow(grad_attended)
     grad_mixed = narrow(nt(tie(rounded_attended, *before), proj[3]))
-    grad_q, own, other, sums = attend_back(core, *projected, grad_mixed, mixed, attention)
+    grad_q, own, other, sums = attend_back(core, *projected, grad_mixed, mixed, *attention)
     other, *after = lax.optimization_barrier((other, *after))
     grad_kv = narrow(own + swap(other, "core").astype(F32))
     grad_normed_one = nn(grad_q, proj[0]) + nn(grad_kv[0], proj[1]) + nn(grad_kv[1], proj[2])

time: 434 us -> 420 us (0.968)
  the two profiles are of different devices: /device:TPU:17 before, /device:TPU:30 now
where the time goes in v4:
time: 420 us; the launch traced here: 415 us
  waiting for transfers between devices  144 us (34%)
  Pallas kernels  90.3 us (22%)
  starting transfers between devices  61.5 us (15%)
  other arithmetic  48.2 us (11%)
  local copies, waits for them, and re-layouts  34.3 us (8%)
  matrix products  33.6 us (8%)
    ppermute x15, waiting for transfers between devices, ring(): lax.ppermute(value, 'tensor', list(zip(order, order[1:] + order[:1])))  52.5 us
    ppermute x33, waiting for transfers between devices, swap(): return lax.ppermute(value, axis, [(0, 1), (1, 0)])  45.5 us
    pallas_call x2, Pallas kernels, attend_back(): pl.pallas_call(attend_back_kernel, grid=(width // LANES,), out_shape=[jax...  28.4 us
    ppermute x4, waiting for transfers between devices, along_pipe(): return lax.ppermute(value, 'pipe', [(0, 1)] if by > 0 else [(1, 0)])  27.8 us
    pallas_call x2, Pallas kernels, attend(): pl.pallas_call(functools.partial(attend_kernel, keep_weights), grid=(pair...  21.3 us
    unnamed x218, local copies, waits for them, and re-layouts  20.9 us
    ppermute x33, starting transfers between devices, swap(): return lax.ppermute(value, axis, [(0, 1), (1, 0)])  19.9 us
    ppermute x4, waiting for transfers between devices, give_back(): pieces.append(lax.ppermute(rows, AXES, pairs))  18.7 us
  transfers between devices with their start and end apart: 60, of which 27 were waited for; matrix products, arithmetic and copies ran while one was open for 20% of the time, Pallas kernels for 15%

profile of v4, /device:TPU:30, one launch (start us, length us, event | category | flops | bytes accessed | tf_op | source)
XLA Modules:
  0.0 415.1 jit_solution(14144559441828255650)
XLA Ops:
  1.5 4.2 %collective-permute-start.4 = (bf16[256,768]{1,0:T(8,128)(2,1)}, bf16[256,768]{1,0:T(8,128)(2,1)}, u32[]{:S(2)}, u32[]{:S(2)}) collective-permute-start(bf16[256,768]{1,0:T(8,128)(2,1)} %bitcast.155), channel_id=1, source_target_pairs={{3,0},{2,4},{7,2},{6,6},{11,8},{10,12},{15,10},{14,14},{19,1},{18,... | collective-permute-start | bytes 1179656 | tf_op jit(solution)/shard_map/ppermute | solution.py:57
  7.3 2.1 select_bitcast_fusion.8
  12.4 9.3 %collective-permute-done = bf16[208,768]{1,0:T(8,128)(2,1)} collective-permute-done((bf16[208,768]{1,0:T(8,128)(2,1)}, bf16[208,768]{1,0:T(8,128)(2,1)}, u32[]{:S(2)}, u32[]{:S(2)}) %collective-permute-start) | collective-permute-done | bytes 319520 | tf_op jit(solution)/shard_map/ppermute | solution.py:29
  25.4 4.2 %collective-permute-done.2 = bf16[192,768]{1,0:T(8,128)(2,1)S(1)} collective-permute-done((bf16[192,768]{1,0:T(8,128)(2,1)S(1)}, bf16[192,768]{1,0:T(8,128)(2,1)S(1)}, u32[]{:S(2)}, u32[]{:S(2)}) %collective-permute-start.2) | collective-permute-done | bytes 294944 | tf_op jit(solution)/shard_map/ppermute | solution.py:33
  31.1 3.1 collective-permute-start.5
  38.3 5.6 %collective-permute-done.6 = bf16[192,768]{1,0:T(8,128)(2,1)S(1)} collective-permute-done((bf16[192,768]{1,0:T(8,128)(2,1)S(1)}, bf16[192,768]{1,0:T(8,128)(2,1)S(1)}, u32[]{:S(2)}, u32[]{:S(2)}) %collective-permute-start.6) | collective-permute-done | bytes 294944 | tf_op jit(solution)/shard_map/ppermute | solution.py:33
  47.5 6.7 %collective-permute-done.7 = bf16[384,768]{1,0:T(8,128)(2,1)} collective-permute-done((bf16[384,768]{1,0:T(8,128)(2,1)S(1)}, bf16[384,768]{1,0:T(8,128)(2,1)}, u32[]{:S(2)}, u32[]{:S(2)}) %collective-permute-start.7) | collective-permute-done | bytes 589856 | tf_op jit(solution)/shard_map/ppermute | solution.py:29
  56.2 3.2 collective-permute-start.11
  64.9 7.6 %collective-permute-done.11 = bf16[384,768]{1,0:T(8,128)(2,1)} collective-permute-done((bf16[384,768]{1,0:T(8,128)(2,1)}, bf16[384,768]{1,0:T(8,128)(2,1)}, u32[]{:S(2)}, u32[]{:S(2)}) %collective-permute-start.11) | collective-permute-done | bytes 589856 | tf_op jit(solution)/shard_map/ppermute | solution.py:29
  72.6 2.2 collective-permute-done.12
  95.8 9.6 %attend.2 = bf16[512,768]{1,0:T(8,128)(2,1)S(1)} custom-call(s32[1]{0:T(128)} %bitcast.core_ref, bf16[512,768]{1,0:T(8,128)(2,1)S(1)} %add_convert_fusion.13.q_ref, bf16[512,768]{1,0:T(8,128)(2,1)S(1)} %convolution_convert_fusion.7.k_ref, bf16[512,768]{1,0:T(8,128)(2,1)S(1)} %add_convert_fusion.12.v_ref, ...), custom_call_target="tpu_custom_call" | custom-call | flops 2013265920 | bytes 6291456 | tf_op jit(solution)/shard_map/attend/pallas_call | solution.py:250
  112.3 2.4 fusion.88
  115.4 3.3 feed_half.4.start_ref
  119.4 4.0 feed_half.5
  125.4 3.3 feed_half.6.start_ref
  128.7 4.0 feed_half.7
  134.2 2.3 collective-permute-done.20
  136.6 9.4 %collective-permute-done.21 = bf16[256,768]{1,0:T(8,128)(2,1)S(1)} collective-permute-done((bf16[256,768]{1,0:T(8,128)(2,1)S(1)}, bf16[256,768]{1,0:T(8,128)(2,1)S(1)}, u32[]{:S(2)}, u32[]{:S(2)}) %collective-permute-start.21) | collective-permute-done | bytes 393248 | tf_op jit(solution)/shard_map/ppermute | solution.py:37
  151.4 3.8 collective-permute-start.25
  155.3 2.4 add_convert_fusion.10.q_ref
  157.7 11.7 %attend.3 = (bf16[512,768]{1,0:T(8,128)(2,1)S(1)}, bf16[12,5,256,256]{3,2,1,0:T(8,128)(2,1)}, f32[48,512]{1,0:T(8,128)S(1)}) custom-call(s32[1]{0:T(128)} %bitcast.core_ref, bf16[512,768]{1,0:T(8,128)(2,1)S(1)} %add_convert_fusion.10.q_ref, bf16[512,768]{1,0:T(8,128)(2,1)S(1)} %convolution_convert_fusion.6.k_ref, ...), custom_call_target="tpu_custom_call" | custom-call | flops 2013265920 | bytes 6291456 | tf_op jit(solution)/shard_map/attend/pallas_call | solution.py:250
  171.2 15.8 %feed_both.1 = (f32[512,768]{1,0:T(8,128)S(1)}, f32[512,768]{1,0:T(8,128)S(1)}, bf16[512,1536]{1,0:T(8,128)(2,1)S(1)}, bf16[512,1536]{1,0:T(8,128)(2,1)S(1)}, bf...) custom-call(bf16[512,768]{1,0:T(8,128)(2,1)S(1)} %add_convert_fusion.8.rows_ref, ...), custom_call_target="tpu_custom_call" | custom-call | flops 9663676416 | bytes 9437184 | tf_op jit(solution)/shard_map/feed_both/pallas_call | solution.py:405
  189.2 4.3 %collective-permute-start.26 = (bf16[256,768]{1,0:T(8,128)(2,1)}, bf16[256,768]{1,0:T(8,128)(2,1)}, u32[]{:S(2)}, u32[]{:S(2)}) collective-permute-start(bf16[256,768]{1,0:T(8,128)(2,1)} %get-tuple-element.268), channel_id=1, source_target_pairs={{16,0},{20,1},{18,4},{22,5},{24,8},{28,9},{26,12},{30,13},{17,16},... | collective-permute-start | bytes 1179656 | tf_op jit(solution)/shard_map/ppermute | solution.py:64
  193.5 2.1 collective-permute-start.27
  196.5 14.2 %attend_back.2 = (bf16[512,768]{1,0:T(8,128)(2,1)S(1)}, f32[2,512,768]{2,1,0:T(8,128)S(1)}, bf16[2,512,768]{2,1,0:T(8,128)(2,1)S(1)}, f32[8,768]{1,0:T(8,128)}) custom-call(s32[1]{0:T(128)} %bitcast.core_ref, bf16[512,768]{1,0:T(8,128)(2,1)S(1)} %add_convert_fusion.10.q_ref, bf16[512,768]{1,0:T(8,128)(2,1)S(1)} %convolution_convert_fusion.6.k_ref, ...), custom_call_target="tpu_custom_call" | custom-call | flops 4026531840 | bytes 15728640 | tf_op jit(solution)/shard_map/attend_back/pallas_call | solution.py:267
  210.7 4.0 collective-permute-done.27
  217.3 2.6 collective-permute-done.28
  226.9 8.1 %collective-permute-done.30 = bf16[256,768]{1,0:T(8,128)(2,1)S(1)} collective-permute-done((bf16[256,768]{1,0:T(8,128)(2,1)S(1)}, bf16[256,768]{1,0:T(8,128)(2,1)S(1)}, u32[]{:S(2)}, u32[]{:S(2)}) %collective-permute-start.30) | collective-permute-done | bytes 393248 | tf_op jit(solution)/shard_map/ppermute | solution.py:37
  235.0 7.9 %collective-permute-done.29 = bf16[256,768]{1,0:T(8,128)(2,1)S(1)} collective-permute-done((bf16[256,768]{1,0:T(8,128)(2,1)S(1)}, bf16[256,768]{1,0:T(8,128)(2,1)S(1)}, u32[]{:S(2)}, u32[]{:S(2)}) %collective-permute-start.29) | collective-permute-done | bytes 393248 | tf_op jit(solution)/shard_map/ppermute | solution.py:37
  246.3 2.9 collective-permute-done.31
  250.1 10.3 %feed_back.1 = (f32[512,768]{1,0:T(8,128)S(1)}, bf16[512,1536]{1,0:T(8,128)(2,1)S(1)}, bf16[512,1536]{1,0:T(8,128)(2,1)S(1)}, f32[8,1536]{1,0:T(8,128)S(1)}, f32[8,1536]{1,0:T(8,128)S(1)}) custom-call(bf16[512,768]{1,0:T(8,128)(2,1)S(1)} %fusion.1.grad_ref, bf16[1536,768]{1,0:T(8,128)(2,1)} %get-tuple-element.270.expand_ref.e0_ref, ...), custom_call_target="tpu_custom_call" | custom-call | flops 4831838208 | bytes 9437184 | tf_op jit(solution)/shard_map/feed_back/pallas_call | solution.py:424
  265.7 2.2 collective-permute-done.32
  271.6 14.3 %attend_back.3 = (bf16[512,768]{1,0:T(8,128)(2,1)S(1)}, f32[2,512,768]{2,1,0:T(8,128)S(1)}, bf16[2,512,768]{2,1,0:T(8,128)(2,1)}, f32[8,768]{1,0:T(8,128)S(1)}) custom-call(s32[1]{0:T(128)} %bitcast.core_ref, bf16[512,768]{1,0:T(8,128)(2,1)S(1)} %add_convert_fusion.10.q_ref, bf16[512,768]{1,0:T(8,128)(2,1)S(1)} %copy-done.6, bf16[512,768]{1,0:T(8,128)(2,1)S(1)} %copy-done.8, ...), custom_call_target="tpu_custom_call" | custom-call | flops 4026531840 | bytes 15728640 | tf_op jit(solution)/shard_map/attend_back/pallas_call | solution.py:267
  286.7 5.2 %collective-permute-done.34 = bf16[768,768]{1,0:T(8,128)(2,1)} collective-permute-done((bf16[768,768]{1,0:T(8,128)(2,1)S(1)}, bf16[768,768]{1,0:T(8,128)(2,1)}, u32[]{:S(2)}, u32[]{:S(2)}) %collective-permute-start.34) | collective-permute-done | bytes 1179680 | tf_op jit(solution)/shard_map/ppermute | solution.py:33
  292.8 2.4 fusion.93
  303.6 2.1 convolution_convert_fusion.3
  306.2 2.1 convolution_convert_fusion.2
  308.3 2.4 fusion.37
  312.6 5.9 %collective-permute-done.36 = bf16[192,768]{1,0:T(8,128)(2,1)S(1)} collective-permute-done((bf16[192,768]{1,0:T(8,128)(2,1)S(1)}, bf16[192,768]{1,0:T(8,128)(2,1)S(1)}, u32[]{:S(2)}, u32[]{:S(2)}) %collective-permute-start.36) | collective-permute-done | bytes 294944 | tf_op jit(solution)/shard_map/ppermute | solution.py:29
  318.6 2.4 fusion.20
  329.3 2.4 collective-permute-done.42
  331.7 5.4 %collective-permute-done.40 = bf16[192,768]{1,0:T(8,128)(2,1)S(1)} collective-permute-done((bf16[192,768]{1,0:T(8,128)(2,1)S(1)}, bf16[192,768]{1,0:T(8,128)(2,1)S(1)}, u32[]{:S(2)}, u32[]{:S(2)}) %collective-permute-start.40) | collective-permute-done | bytes 294944 | tf_op jit(solution)/shard_map/ppermute | solution.py:33
  341.0 11.4 %collective-permute-done.46 = bf16[192,768]{1,0:T(8,128)(2,1)S(1)} collective-permute-done((bf16[192,768]{1,0:T(8,128)(2,1)S(1)}, bf16[192,768]{1,0:T(8,128)(2,1)S(1)}, u32[]{:S(2)}, u32[]{:S(2)}) %collective-permute-start.46) | collective-permute-done | bytes 294944 | tf_op jit(solution)/shard_map/ppermute | solution.py:29
  356.6 10.1 %collective-permute-done.49 = bf16[192,768]{1,0:T(8,128)(2,1)S(1)} collective-permute-done((bf16[192,768]{1,0:T(8,128)(2,1)S(1)}, bf16[192,768]{1,0:T(8,128)(2,1)S(1)}, u32[]{:S(2)}, u32[]{:S(2)}) %collective-permute-start.49) | collective-permute-done | bytes 294944 | tf_op jit(solution)/shard_map/ppermute | solution.py:29
  366.9 2.8 collective-permute-start.50
  370.9 6.0 %collective-permute-done.52 = bf16[2,192,768]{2,1,0:T(8,128)(2,1)S(1)} collective-permute-done((bf16[2,192,768]{2,1,0:T(8,128)(2,1)S(1)}, bf16[2,192,768]{2,1,0:T(8,128)(2,1)S(1)}, u32[]{:S(2)}, u32[]{:S(2)}) %collective-permute-start.52) | collective-permute-done | bytes 589856 | tf_op jit(solution)/shard_map/ppermute | solution.py:33
  383.3 3.6 collective-permute-done.55
  389.2 14.7 %collective-permute-done.54 = bf16[256,768]{1,0:T(8,128)(2,1)} collective-permute-done((bf16[256,768]{1,0:T(8,128)(2,1)}, bf16[256,768]{1,0:T(8,128)(2,1)}, u32[]{:S(2)}, u32[]{:S(2)}) %collective-permute-start.54) | collective-permute-done | bytes 393248 | tf_op jit(solution)/shard_map/ppermute | solution.py:64
  (483 shorter events, 140.3 us)
Async XLA Ops:
  0.7 24.7 %collective-permute-start.3 = (bf16[256,768]{1,0:T(8,128)(2,1)}, bf16[256,768]{1,0:T(8,128)(2,1)S(1)}, u32[]{:S(2)}, u32[]{:S(2)}) collective-permute-start(bf16[256,768]{1,0:T(8,128)(2,1)} %bitcast.154), channel_id=1, source_target_pairs={{0,0},{1,4},{4,2},{5,6},{8,8},{9,12},{12,10},{13,14},{16,1},{17,5}... | collective-permute-start | bytes 1179656 | tf_op jit(solution)/shard_map/ppermute | solution.py:57
  1.5 23.9 %collective-permute-start.4 = (bf16[256,768]{1,0:T(8,128)(2,1)}, bf16[256,768]{1,0:T(8,128)(2,1)}, u32[]{:S(2)}, u32[]{:S(2)}) collective-permute-start(bf16[256,768]{1,0:T(8,128)(2,1)} %bitcast.155), channel_id=1, source_target_pairs={{3,0},{2,4},{7,2},{6,6},{11,8},{10,12},{15,10},{14,14},{19,1},{18,... | collective-permute-start | bytes 1179656 | tf_op jit(solution)/shard_map/ppermute | solution.py:57
  10.2 11.5 %collective-permute-start = (bf16[208,768]{1,0:T(8,128)(2,1)}, bf16[208,768]{1,0:T(8,128)(2,1)}, u32[]{:S(2)}, u32[]{:S(2)}) collective-permute-start(bf16[208,768]{1,0:T(8,128)(2,1)} %pad_maximum_fusion.11), channel_id=1, source_target_pairs={{0,2},{2,3},{3,1},{1,0},{4,6},{6,7},{7,5},{5,4},{8,10},{10,11},{11... | collective-permute-start | bytes 958472 | tf_op jit(solution)/shard_map/ppermute | solution.py:29
  31.1 12.8 %collective-permute-start.5 = (bf16[208,768]{1,0:T(8,128)(2,1)S(1)}, bf16[208,768]{1,0:T(8,128)(2,1)S(1)}, u32[]{:S(2)}, u32[]{:S(2)}) collective-permute-start(bf16[208,768]{1,0:T(8,128)(2,1)S(1)} %collective-permute-done.1), channel_id=1, source_target_pairs={{0,2},{2,3},{3,1},{1,0},{4,6},{6,7},{7,5},{5,4},{8,10},{10,11},{11... | collective-permute-start | bytes 958472 | tf_op jit(solution)/shard_map/ppermute | solution.py:29
  34.3 9.7 %collective-permute-start.6 = (bf16[192,768]{1,0:T(8,128)(2,1)S(1)}, bf16[192,768]{1,0:T(8,128)(2,1)S(1)}, u32[]{:S(2)}, u32[]{:S(2)}) collective-permute-start(bf16[192,768]{1,0:T(8,128)(2,1)S(1)} %slice.289), channel_id=1, source_target_pairs={{0,8},{8,0},{1,9},{9,1},{2,10},{10,2},{3,11},{11,3},{4,12},{12,4},... | collective-permute-start | bytes 884744 | tf_op jit(solution)/shard_map/ppermute | solution.py:33
  35.9 18.3 %collective-permute-start.7 = (bf16[384,768]{1,0:T(8,128)(2,1)S(1)}, bf16[384,768]{1,0:T(8,128)(2,1)}, u32[]{:S(2)}, u32[]{:S(2)}) collective-permute-start(bf16[384,768]{1,0:T(8,128)(2,1)S(1)} %pad_maximum_fusion.3), channel_id=1, source_target_pairs={{0,2},{2,3},{3,1},{1,0},{4,6},{6,7},{7,5},{5,4},{8,10},{10,11},{11... | collective-permute-start | bytes 1769480 | tf_op jit(solution)/shard_map/ppermute | solution.py:29
  44.0 10.2 %collective-permute-start.8 = (bf16[192,768]{1,0:T(8,128)(2,1)S(1)}, bf16[192,768]{1,0:T(8,128)(2,1)S(1)}, u32[]{:S(2)}, u32[]{:S(2)}) collective-permute-start(bf16[192,768]{1,0:T(8,128)(2,1)S(1)} %slice.290), channel_id=1, source_target_pairs={{0,8},{8,0},{1,9},{9,1},{2,10},{10,2},{3,11},{11,3},{4,12},{12,4},... | collective-permute-start | bytes 884744 | tf_op jit(solution)/shard_map/ppermute | solution.py:33
  47.3 30.5 %collective-permute-start.9 = (bf16[768,768]{1,0:T(8,128)(2,1)}, bf16[768,768]{1,0:T(8,128)(2,1)S(1)}, u32[]{:S(2)}, u32[]{:S(2)}) collective-permute-start(bf16[768,768]{1,0:T(8,128)(2,1)} %pad_maximum_fusion.1), channel_id=1, source_target_pairs={{0,4},{4,0},{1,5},{5,1},{2,6},{6,2},{3,7},{7,3},{8,12},{12,8},{9,1... | collective-permute-start | bytes 3538952 | tf_op jit(solution)/shard_map/ppermute | solution.py:33
  55.3 22.5 %collective-permute-start.10 = (bf16[768,768]{1,0:T(8,128)(2,1)}, bf16[768,768]{1,0:T(8,128)(2,1)}, u32[]{:S(2)}, u32[]{:S(2)}) collective-permute-start(bf16[768,768]{1,0:T(8,128)(2,1)} %pad_maximum_fusion.2), channel_id=1, source_target_pairs={{0,4},{4,0},{1,5},{5,1},{2,6},{6,2},{3,7},{7,3},{8,12},{12,8},{9,1... | collective-permute-start | bytes 3538952 | tf_op jit(solution)/shard_map/ppermute | solution.py:33
  56.2 16.4 %collective-permute-start.11 = (bf16[384,768]{1,0:T(8,128)(2,1)}, bf16[384,768]{1,0:T(8,128)(2,1)}, u32[]{:S(2)}, u32[]{:S(2)}) collective-permute-start(bf16[384,768]{1,0:T(8,128)(2,1)} %collective-permute-done.7), channel_id=1, source_target_pairs={{0,2},{2,3},{3,1},{1,0},{4,6},{6,7},{7,5},{5,4},{8,10},{10,11},{11... | collective-permute-start | bytes 1769480 | tf_op jit(solution)/shard_map/ppermute | solution.py:29
  59.4 15.3 %collective-permute-start.12 = (bf16[384,768]{1,0:T(8,128)(2,1)}, bf16[384,768]{1,0:T(8,128)(2,1)}, u32[]{:S(2)}, u32[]{:S(2)}) collective-permute-start(bf16[384,768]{1,0:T(8,128)(2,1)} %collective-permute-done.7), channel_id=1, source_target_pairs={{0,8},{8,0},{1,9},{9,1},{2,10},{10,2},{3,11},{11,3},{4,12},{12,4},... | collective-permute-start | bytes 1769480 | tf_op jit(solution)/shard_map/ppermute | solution.py:33
  74.8 14.7 %collective-permute-start.13 = (bf16[384,768]{1,0:T(8,128)(2,1)}, bf16[384,768]{1,0:T(8,128)(2,1)S(1)}, u32[]{:S(2)}, u32[]{:S(2)}) collective-permute-start(bf16[384,768]{1,0:T(8,128)(2,1)} %collective-permute-done.11), channel_id=1, source_target_pairs={{0,2},{2,3},{3,1},{1,0},{4,6},{6,7},{7,5},{5,4},{8,10},{10,11},{11... | collective-permute-start | bytes 1769480 | tf_op jit(solution)/shard_map/ppermute | solution.py:29
  76.2 14.4 %collective-permute-start.14 = (bf16[384,768]{1,0:T(8,128)(2,1)}, bf16[384,768]{1,0:T(8,128)(2,1)S(1)}, u32[]{:S(2)}, u32[]{:S(2)}) collective-permute-start(bf16[384,768]{1,0:T(8,128)(2,1)} %collective-permute-done.11), channel_id=1, source_target_pairs={{0,8},{8,0},{1,9},{9,1},{2,10},{10,2},{3,11},{11,3},{4,12},{12,4},... | collective-permute-start | bytes 1769480 | tf_op jit(solution)/shard_map/ppermute | solution.py:33
  81.9 13.9 %collective-permute-start.15 = (bf16[512,768]{1,0:T(8,128)(2,1)S(1)}, bf16[512,768]{1,0:T(8,128)(2,1)S(1)}, u32[]{:S(2)}, u32[]{:S(2)}) collective-permute-start(bf16[512,768]{1,0:T(8,128)(2,1)S(1)} %convolution_convert_fusion.7.k_ref), channel_id=1, source_target_pairs={{0,4},{4,0},{1,5},{5,1},{2,6},{6,2},{3,7},{7,3},{8,12},{12,8},{9,1... | collective-permute-start | bytes 2359304 | tf_op jit(solution)/shard_map/ppermute | solution.py:33
  85.2 10.5 %collective-permute-start.16 = (bf16[512,768]{1,0:T(8,128)(2,1)S(1)}, bf16[512,768]{1,0:T(8,128)(2,1)S(1)}, u32[]{:S(2)}, u32[]{:S(2)}) collective-permute-start(bf16[512,768]{1,0:T(8,128)(2,1)S(1)} %add_convert_fusion.12.v_ref), channel_id=1, source_target_pairs={{0,4},{4,0},{1,5},{5,1},{2,6},{6,2},{3,7},{7,3},{8,12},{12,8},{9,1... | collective-permute-start | bytes 2359304 | tf_op jit(solution)/shard_map/ppermute | solution.py:33
  90.6 14.8 %collective-permute-start.17 = (bf16[384,768]{1,0:T(8,128)(2,1)S(1)}, bf16[384,768]{1,0:T(8,128)(2,1)S(1)}, u32[]{:S(2)}, u32[]{:S(2)}) collective-permute-start(bf16[384,768]{1,0:T(8,128)(2,1)S(1)} %collective-permute-done.13), channel_id=1, source_target_pairs={{0,8},{8,0},{1,9},{9,1},{2,10},{10,2},{3,11},{11,3},{4,12},{12,4},... | collective-permute-start | bytes 1769480 | tf_op jit(solution)/shard_map/ppermute | solution.py:33
  111.2 8.2 %collective-permute-start.18 = (bf16[1536,768]{1,0:T(8,128)(2,1)}, bf16[1536,768]{1,0:T(8,128)(2,1)}, u32[]{:S(2)}, u32[]{:S(2)}) collective-permute-start(bf16[1536,768]{1,0:T(8,128)(2,1)} %get-tuple-element.270.expand_ref.e0_ref), channel_id=1, source_target_pairs={{0,4},{4,0},{1,5},{5,1},{2,6},{6,2},{3,7},{7,3},{8,12},{12,8},{9,1... | collective-permute-start | bytes 7077896 | tf_op jit(solution)/shard_map/ppermute | solution.py:33
  123.5 13.1 %collective-permute-start.20 = (bf16[256,768]{1,0:T(8,128)(2,1)S(1)}, bf16[256,768]{1,0:T(8,128)(2,1)S(1)}, u32[]{:S(2)}, u32[]{:S(2)}) collective-permute-start(bf16[256,768]{1,0:T(8,128)(2,1)S(1)} %fusion.34), channel_id=1, source_target_pairs={{0,16},{1,17},{2,18},{3,19},{4,20},{5,21},{6,22},{7,23},{8,24},{9,... | collective-permute-start | bytes 1179656 | tf_op jit(solution)/shard_map/ppermute | solution.py:37
  132.8 13.2 %collective-permute-start.21 = (bf16[256,768]{1,0:T(8,128)(2,1)S(1)}, bf16[256,768]{1,0:T(8,128)(2,1)S(1)}, u32[]{:S(2)}, u32[]{:S(2)}) collective-permute-start(bf16[256,768]{1,0:T(8,128)(2,1)S(1)} %fusion.33), channel_id=1, source_target_pairs={{0,16},{1,17},{2,18},{3,19},{4,20},{5,21},{6,22},{7,23},{8,24},{9,... | collective-permute-start | bytes 1179656 | tf_op jit(solution)/shard_map/ppermute | solution.py:37
  150.1 19.3 %collective-permute-start.24 = (bf16[256,768]{1,0:T(8,128)(2,1)}, bf16[256,768]{1,0:T(8,128)(2,1)S(1)}, u32[]{:S(2)}, u32[]{:S(2)}) collective-permute-start(bf16[256,768]{1,0:T(8,128)(2,1)} %bitcast.156), channel_id=1, source_target_pairs={{0,16},{1,20},{4,18},{5,22},{8,24},{9,28},{12,26},{13,30},{16,17},... | collective-permute-start | bytes 1179656 | tf_op jit(solution)/shard_map/ppermute | solution.py:57
  151.4 18.0 %collective-permute-start.25 = (bf16[256,768]{1,0:T(8,128)(2,1)}, bf16[256,768]{1,0:T(8,128)(2,1)S(1)}, u32[]{:S(2)}, u32[]{:S(2)}) collective-permute-start(bf16[256,768]{1,0:T(8,128)(2,1)} %bitcast.157), channel_id=1, source_target_pairs={{3,16},{2,20},{7,18},{6,22},{11,24},{10,28},{15,26},{14,30},{19,17... | collective-permute-start | bytes 1179656 | tf_op jit(solution)/shard_map/ppermute | solution.py:57
  189.2 21.5 %collective-permute-start.26 = (bf16[256,768]{1,0:T(8,128)(2,1)}, bf16[256,768]{1,0:T(8,128)(2,1)}, u32[]{:S(2)}, u32[]{:S(2)}) collective-permute-start(bf16[256,768]{1,0:T(8,128)(2,1)} %get-tuple-element.268), channel_id=1, source_target_pairs={{16,0},{20,1},{18,4},{22,5},{24,8},{28,9},{26,12},{30,13},{17,16},... | collective-permute-start | bytes 1179656 | tf_op jit(solution)/shard_map/ppermute | solution.py:64
  193.5 21.2 %collective-permute-start.27 = (bf16[256,768]{1,0:T(8,128)(2,1)S(1)}, bf16[256,768]{1,0:T(8,128)(2,1)}, u32[]{:S(2)}, u32[]{:S(2)}) collective-permute-start(bf16[256,768]{1,0:T(8,128)(2,1)S(1)} %get-tuple-element.267), channel_id=1, source_target_pairs={{16,3},{20,2},{18,7},{22,6},{24,11},{28,10},{26,15},{30,14},{17,19... | collective-permute-start | bytes 1179656 | tf_op jit(solution)/shard_map/ppermute | solution.py:64
  224.3 10.7 %collective-permute-start.30 = (bf16[256,768]{1,0:T(8,128)(2,1)S(1)}, bf16[256,768]{1,0:T(8,128)(2,1)S(1)}, u32[]{:S(2)}, u32[]{:S(2)}) collective-permute-start(bf16[256,768]{1,0:T(8,128)(2,1)S(1)} %get-tuple-element.266), channel_id=1, source_target_pairs={{16,0},{17,1},{18,2},{19,3},{20,4},{21,5},{22,6},{23,7},{24,8},{25... | collective-permute-start | bytes 1179656 | tf_op jit(solution)/shard_map/ppermute | solution.py:37
  225.6 17.3 %collective-permute-start.29 = (bf16[256,768]{1,0:T(8,128)(2,1)S(1)}, bf16[256,768]{1,0:T(8,128)(2,1)S(1)}, u32[]{:S(2)}, u32[]{:S(2)}) collective-permute-start(bf16[256,768]{1,0:T(8,128)(2,1)S(1)} %get-tuple-element.265), channel_id=1, source_target_pairs={{16,0},{17,1},{18,2},{19,3},{20,4},{21,5},{22,6},{23,7},{24,8},{25... | collective-permute-start | bytes 1179656 | tf_op jit(solution)/shard_map/ppermute | solution.py:37
  263.5 28.4 %collective-permute-start.34 = (bf16[768,768]{1,0:T(8,128)(2,1)S(1)}, bf16[768,768]{1,0:T(8,128)(2,1)}, u32[]{:S(2)}, u32[]{:S(2)}) collective-permute-start(bf16[768,768]{1,0:T(8,128)(2,1)S(1)} %slice.393), channel_id=1, source_target_pairs={{0,8},{8,0},{1,9},{9,1},{2,10},{10,2},{3,11},{11,3},{4,12},{12,4},... | collective-permute-start | bytes 3538952 | tf_op jit(solution)/shard_map/ppermute | solution.py:33
  269.7 22.3 %collective-permute-start.33 = (bf16[384,768]{1,0:T(8,128)(2,1)S(1)}, bf16[384,768]{1,0:T(8,128)(2,1)}, u32[]{:S(2)}, u32[]{:S(2)}) collective-permute-start(bf16[384,768]{1,0:T(8,128)(2,1)S(1)} %pad_maximum_fusion.5), channel_id=1, source_target_pairs={{0,2},{2,3},{3,1},{1,0},{4,6},{6,7},{7,5},{5,4},{8,10},{10,11},{11... | collective-permute-start | bytes 1769480 | tf_op jit(solution)/shard_map/ppermute | solution.py:29
  296.4 22.1 %collective-permute-start.35 = (bf16[384,768]{1,0:T(8,128)(2,1)S(1)}, bf16[384,768]{1,0:T(8,128)(2,1)S(1)}, u32[]{:S(2)}, u32[]{:S(2)}) collective-permute-start(bf16[384,768]{1,0:T(8,128)(2,1)S(1)} %add_convert_fusion.16), channel_id=1, source_target_pairs={{0,2},{2,3},{3,1},{1,0},{4,6},{6,7},{7,5},{5,4},{8,10},{10,11},{11... | collective-permute-start | bytes 1769480 | tf_op jit(solution)/shard_map/ppermute | solution.py:29
  298.2 20.4 %collective-permute-start.36 = (bf16[192,768]{1,0:T(8,128)(2,1)S(1)}, bf16[192,768]{1,0:T(8,128)(2,1)S(1)}, u32[]{:S(2)}, u32[]{:S(2)}) collective-permute-start(bf16[192,768]{1,0:T(8,128)(2,1)S(1)} %slice.395), channel_id=1, source_target_pairs={{0,2},{2,3},{3,1},{1,0},{4,6},{6,7},{7,5},{5,4},{8,10},{10,11},{11... | collective-permute-start | bytes 884744 | tf_op jit(solution)/shard_map/ppermute | solution.py:29
  305.7 18.8 %collective-permute-start.39 = (bf16[768,768]{1,0:T(8,128)(2,1)}, bf16[768,768]{1,0:T(8,128)(2,1)}, u32[]{:S(2)}, u32[]{:S(2)}) collective-permute-start(bf16[768,768]{1,0:T(8,128)(2,1)} %convolution_convert_fusion.3), channel_id=1, source_target_pairs={{0,4},{4,0},{1,5},{5,1},{2,6},{6,2},{3,7},{7,3},{8,12},{12,8},{9,1... | collective-permute-start | bytes 3538952 | tf_op jit(solution)/shard_map/ppermute | solution.py:33
  308.3 19.5 %collective-permute-start.38 = (bf16[768,768]{1,0:T(8,128)(2,1)}, bf16[768,768]{1,0:T(8,128)(2,1)}, u32[]{:S(2)}, u32[]{:S(2)}) collective-permute-start(bf16[768,768]{1,0:T(8,128)(2,1)} %convolution_convert_fusion.2), channel_id=1, source_target_pairs={{0,4},{4,0},{1,5},{5,1},{2,6},{6,2},{3,7},{7,3},{8,12},{12,8},{9,1... | collective-permute-start | bytes 3538952 | tf_op jit(solution)/shard_map/ppermute | solution.py:33
  322.6 29.8 %collective-permute-start.45 = (bf16[384,768]{1,0:T(8,128)(2,1)S(1)}, bf16[384,768]{1,0:T(8,128)(2,1)S(1)}, u32[]{:S(2)}, u32[]{:S(2)}) collective-permute-start(bf16[384,768]{1,0:T(8,128)(2,1)S(1)} %add_convert_fusion.15), channel_id=1, source_target_pairs={{0,2},{2,3},{3,1},{1,0},{4,6},{6,7},{7,5},{5,4},{8,10},{10,11},{11... | collective-permute-start | bytes 1769480 | tf_op jit(solution)/shard_map/ppermute | solution.py:29
  326.2 11.0 %collective-permute-start.40 = (bf16[192,768]{1,0:T(8,128)(2,1)S(1)}, bf16[192,768]{1,0:T(8,128)(2,1)S(1)}, u32[]{:S(2)}, u32[]{:S(2)}) collective-permute-start(bf16[192,768]{1,0:T(8,128)(2,1)S(1)} %get-tuple-element.260), channel_id=1, source_target_pairs={{0,8},{8,0},{1,9},{9,1},{2,10},{10,2},{3,11},{11,3},{4,12},{12,4},... | collective-permute-start | bytes 884744 | tf_op jit(solution)/shard_map/ppermute | solution.py:33
  337.4 15.1 %collective-permute-start.43 = (bf16[208,768]{1,0:T(8,128)(2,1)S(1)}, bf16[208,768]{1,0:T(8,128)(2,1)S(1)}, u32[]{:S(2)}, u32[]{:S(2)}) collective-permute-start(bf16[208,768]{1,0:T(8,128)(2,1)S(1)} %pad_maximum_fusion.12), channel_id=1, source_target_pairs={{0,2},{2,3},{3,1},{1,0},{4,6},{6,7},{7,5},{5,4},{8,10},{10,11},{11... | collective-permute-start | bytes 958472 | tf_op jit(solution)/shard_map/ppermute | solution.py:29
  337.8 14.6 %collective-permute-start.46 = (bf16[192,768]{1,0:T(8,128)(2,1)S(1)}, bf16[192,768]{1,0:T(8,128)(2,1)S(1)}, u32[]{:S(2)}, u32[]{:S(2)}) collective-permute-start(bf16[192,768]{1,0:T(8,128)(2,1)S(1)} %add_convert_fusion.25), channel_id=1, source_target_pairs={{0,2},{2,3},{3,1},{1,0},{4,6},{6,7},{7,5},{5,4},{8,10},{10,11},{11... | collective-permute-start | bytes 884744 | tf_op jit(solution)/shard_map/ppermute | solution.py:29
  339.0 13.4 %collective-permute-start.44 = (bf16[192,768]{1,0:T(8,128)(2,1)S(1)}, bf16[192,768]{1,0:T(8,128)(2,1)S(1)}, u32[]{:S(2)}, u32[]{:S(2)}) collective-permute-start(bf16[192,768]{1,0:T(8,128)(2,1)S(1)} %get-tuple-element.257), channel_id=1, source_target_pairs={{0,8},{8,0},{1,9},{9,1},{2,10},{10,2},{3,11},{11,3},{4,12},{12,4},... | collective-permute-start | bytes 884744 | tf_op jit(solution)/shard_map/ppermute | solution.py:33
  339.5 17.1 %collective-permute-start.48 = (bf16[192,768]{1,0:T(8,128)(2,1)S(1)}, bf16[192,768]{1,0:T(8,128)(2,1)S(1)}, u32[]{:S(2)}, u32[]{:S(2)}) collective-permute-start(bf16[192,768]{1,0:T(8,128)(2,1)S(1)} %get-tuple-element.165), channel_id=1, source_target_pairs={{0,8},{8,0},{1,9},{9,1},{2,10},{10,2},{3,11},{11,3},{4,12},{12,4},... | collective-permute-start | bytes 884744 | tf_op jit(solution)/shard_map/ppermute | solution.py:33
  352.6 14.1 %collective-permute-start.47 = (bf16[208,768]{1,0:T(8,128)(2,1)S(1)}, bf16[208,768]{1,0:T(8,128)(2,1)S(1)}, u32[]{:S(2)}, u32[]{:S(2)}) collective-permute-start(bf16[208,768]{1,0:T(8,128)(2,1)S(1)} %add_convert_fusion.19), channel_id=1, source_target_pairs={{0,2},{2,3},{3,1},{1,0},{4,6},{6,7},{7,5},{5,4},{8,10},{10,11},{11... | collective-permute-start | bytes 958472 | tf_op jit(solution)/shard_map/ppermute | solution.py:29
  354.2 12.5 %collective-permute-start.49 = (bf16[192,768]{1,0:T(8,128)(2,1)S(1)}, bf16[192,768]{1,0:T(8,128)(2,1)S(1)}, u32[]{:S(2)}, u32[]{:S(2)}) collective-permute-start(bf16[192,768]{1,0:T(8,128)(2,1)S(1)} %add_convert_fusion.23), channel_id=1, source_target_pairs={{0,2},{2,3},{3,1},{1,0},{4,6},{6,7},{7,5},{5,4},{8,10},{10,11},{11... | collective-permute-start | bytes 884744 | tf_op jit(solution)/shard_map/ppermute | solution.py:29
  354.3 16.6 %collective-permute-start.51 = (bf16[192,768]{1,0:T(8,128)(2,1)S(1)}, bf16[192,768]{1,0:T(8,128)(2,1)S(1)}, u32[]{:S(2)}, u32[]{:S(2)}) collective-permute-start(bf16[192,768]{1,0:T(8,128)(2,1)S(1)} %get-tuple-element.169), channel_id=1, source_target_pairs={{0,8},{8,0},{1,9},{9,1},{2,10},{10,2},{3,11},{11,3},{4,12},{12,4},... | collective-permute-start | bytes 884744 | tf_op jit(solution)/shard_map/ppermute | solution.py:33
  355.0 21.9 %collective-permute-start.52 = (bf16[2,192,768]{2,1,0:T(8,128)(2,1)S(1)}, bf16[2,192,768]{2,1,0:T(8,128)(2,1)S(1)}, u32[]{:S(2)}, u32[]{:S(2)}) collective-permute-start(bf16[2,192,768]{2,1,0:T(8,128)(2,1)S(1)} %bitcast.147), channel_id=1, source_target_pairs={{0,8},{8,0},{1,9},{9,1},{2,10},{10,2},{3,11},{11,3},{4,12},{12,4},... | collective-permute-start | bytes 1769480 | tf_op jit(solution)/shard_map/ppermute | solution.py:33
  366.9 10.1 %collective-permute-start.50 = (bf16[208,768]{1,0:T(8,128)(2,1)S(1)}, bf16[208,768]{1,0:T(8,128)(2,1)S(1)}, u32[]{:S(2)}, u32[]{:S(2)}) collective-permute-start(bf16[208,768]{1,0:T(8,128)(2,1)S(1)} %add_convert_fusion.18), channel_id=1, source_target_pairs={{0,2},{2,3},{3,1},{1,0},{4,6},{6,7},{7,5},{5,4},{8,10},{10,11},{11... | collective-permute-start | bytes 958472 | tf_op jit(solution)/shard_map/ppermute | solution.py:29
  370.4 12.9 %collective-permute-start.56 = (bf16[192,768]{1,0:T(8,128)(2,1)S(1)}, bf16[192,768]{1,0:T(8,128)(2,1)S(1)}, u32[]{:S(2)}, u32[]{:S(2)}) collective-permute-start(bf16[192,768]{1,0:T(8,128)(2,1)S(1)} %add_convert_fusion.20), channel_id=1, source_target_pairs={{0,8},{8,0},{1,9},{9,1},{2,10},{10,2},{3,11},{11,3},{4,12},{12,4},... | collective-permute-start | bytes 884744 | tf_op jit(solution)/shard_map/ppermute | solution.py:33
  378.1 11.1 %collective-permute-start.53 = (bf16[256,768]{1,0:T(8,128)(2,1)}, bf16[256,768]{1,0:T(8,128)(2,1)S(1)}, u32[]{:S(2)}, u32[]{:S(2)}) collective-permute-start(bf16[256,768]{1,0:T(8,128)(2,1)} %get-tuple-element.264), channel_id=1, source_target_pairs={{0,0},{4,1},{2,4},{6,5},{8,8},{12,9},{10,12},{14,13},{1,16},{5,17}... | collective-permute-start | bytes 1179656 | tf_op jit(solution)/shard_map/ppermute | solution.py:64
  378.8 25.0 %collective-permute-start.54 = (bf16[256,768]{1,0:T(8,128)(2,1)}, bf16[256,768]{1,0:T(8,128)(2,1)}, u32[]{:S(2)}, u32[]{:S(2)}) collective-permute-start(bf16[256,768]{1,0:T(8,128)(2,1)} %get-tuple-element.263), channel_id=1, source_target_pairs={{0,3},{4,2},{2,7},{6,6},{8,11},{12,10},{10,15},{14,14},{1,19},{5,1... | collective-permute-start | bytes 1179656 | tf_op jit(solution)/shard_map/ppermute | solution.py:64
  381.4 24.2 %collective-permute-start.58 = (bf16[384,768]{1,0:T(8,128)(2,1)S(1)}, bf16[384,768]{1,0:T(8,128)(2,1)}, u32[]{:S(2)}, u32[]{:S(2)}) collective-permute-start(bf16[384,768]{1,0:T(8,128)(2,1)S(1)} %pad_maximum_fusion.9), channel_id=1, source_target_pairs={{0,4},{4,0},{1,5},{5,1},{2,6},{6,2},{3,7},{7,3},{8,12},{12,8},{9,1... | collective-permute-start | bytes 1769480 | tf_op jit(solution)/shard_map/ppermute | solution.py:33
  387.8 21.1 %collective-permute-start.57 = (bf16[384,768]{1,0:T(8,128)(2,1)}, bf16[384,768]{1,0:T(8,128)(2,1)}, u32[]{:S(2)}, u32[]{:S(2)}) collective-permute-start(bf16[384,768]{1,0:T(8,128)(2,1)} %pad_maximum_fusion.8), channel_id=1, source_target_pairs={{0,4},{4,0},{1,5},{5,1},{2,6},{6,2},{3,7},{7,3},{8,12},{12,8},{9,1... | collective-permute-start | bytes 1769480 | tf_op jit(solution)/shard_map/ppermute | solution.py:33
  388.6 23.6 %collective-permute-start.59 = (bf16[384,768]{1,0:T(8,128)(2,1)}, bf16[384,768]{1,0:T(8,128)(2,1)}, u32[]{:S(2)}, u32[]{:S(2)}) collective-permute-start(bf16[384,768]{1,0:T(8,128)(2,1)} %pad_maximum_fusion.10), channel_id=1, source_target_pairs={{0,4},{4,0},{1,5},{5,1},{2,6},{6,2},{3,7},{7,3},{8,12},{12,8},{9,1... | collective-permute-start | bytes 1769480 | tf_op jit(solution)/shard_map/ppermute | solution.py:33
  (112 other events, 1174.8 us)
